TPU v7x, 128 devices: a whole 4x4x4 slice. The times are simulated.
128 devices in a mesh: row: 16 (over y, z_hi, core), col: 8 (over z_lo, x).
Axes of the slice: x: 4, y: 4, z: 4 (z_hi: 2, z_lo: 2; z = z_hi * 2 + z_lo), core: 2. Of those that a mesh axis runs over, the one named last changes fastest.
Arguments:
- features_in: bfloat16 [65536, 256], P(('row', 'col')), may hold values from -6 to 6
- weight: bfloat16 [256, 256], replicated, may hold values from -0.375 to 0.375
- bias_vector: float32 [256], replicated, may hold values from -3 to 3
- cotangent: bfloat16 [65536, 256], P(('row', 'col')), may hold values from -6 to 6
- adjacency: bfloat16 [16, 8, 512, 128, 128], P('row', 'col'), may hold values from -0.0625 to 0.0625
- block_rows: int32 [16, 8, 512], P('row', 'col'), may hold values from 0 to 31, as said below
- block_cols: int32 [16, 8, 512], P('row', 'col'), may hold values from 0 to 63, as said below
- counts: int32 [16, 8], P('row', 'col'), may hold values from 64 to 512, as said below
Outputs:
- output: bfloat16 [65536, 256], P(('row', 'col'))
- grad_x: bfloat16 [65536, 256], P(('row', 'col'))
- grad_w: float32 [256, 256], replicated
Inputs may be any that keep to these rules, and one draw needn't show every extreme that they name: Within one tile the pairs (block_rows, block_cols) of all 512 slots are distinct. `block_cols`: pairs with block_rows as stated there. `counts`: slots at or past a tile's count are not part of A. Some tile has exactly 512 live slots.
All inputs are finite; a program needn't handle non-finite values.
Results may differ from a plain program's by a relative error of at most 0.025.
Values may be sent and summed in bfloat16 or wider, within the bound.
No kernel may reach another device: no remote copies, remote signals or barrier semaphores. Data moves between devices by JAX's collectives and lax.ppermute only.
A program may use at most 192 MiB of HBM per device.

v0:
```python
import math

import jax
import jax.numpy as jnp
from jax import lax
from jax.sharding import PartitionSpec as P

group_cap = 64


def silu_slope(value):
    sigmoid_v = jax.nn.sigmoid(value)
    return sigmoid_v * (1.0 + value * (1.0 - sigmoid_v))


def per_device(
    features_in, weight, bias_vector, cotangent, adjacency, block_rows, block_cols, counts
):
    node_dev, feature_width = features_in.shape
    slot_total = adjacency.shape[2]
    block_size = adjacency.shape[3]
    rows_count = lax.axis_size("row")
    cols_count = lax.axis_size("col")
    row_block_ids = node_dev * cols_count // block_size
    col_blocks = node_dev * rows_count // block_size
    group_member_count = min(group_cap, slot_total)
    tile_blocks = adjacency[0, 0]
    rows_here = block_rows[0, 0]
    cols_here = block_cols[0, 0]
    live_count = counts[0, 0]
    group_total = (live_count + group_member_count - 1) // group_member_count

    def slot_group(group_index):
        first_slot = group_index * group_member_count
        blocks_here = lax.dynamic_slice_in_dim(tile_blocks, first_slot, group_member_count, 0)
        rows_group = lax.dynamic_slice_in_dim(rows_here, first_slot, group_member_count, 0)
        cols_group = lax.dynamic_slice_in_dim(cols_here, first_slot, group_member_count, 0)
        is_live = first_slot + jnp.arange(group_member_count, dtype=jnp.int32) < live_count
        return (blocks_here, rows_group, cols_group, is_live)

    hidden_in = jnp.dot(features_in, weight, preferred_element_type=jnp.float32).astype(
        jnp.bfloat16
    )
    column_set = lax.all_gather(hidden_in, "row", axis=0, tiled=True)
    column_set = column_set.reshape(col_blocks, block_size, feature_width)

    def forward_step(group_index, totals):
        blocks_here, rows_group, cols_group, is_live = slot_group(group_index)
        gathered = jnp.take(column_set, cols_group, axis=0)
        block_products = jnp.einsum(
            "sab,sbf->saf", blocks_here, gathered, preferred_element_type=jnp.float32
        )
        block_products = block_products * is_live.astype(jnp.float32)[:, None, None]
        return totals.at[rows_group].add(block_products)

    partial_rows = lax.fori_loop(
        0,
        group_total,
        forward_step,
        jnp.zeros((row_block_ids, block_size, feature_width), jnp.float32),
    )
    partial_rows = partial_rows.reshape(row_block_ids * block_size, feature_width)
    col_index = lax.axis_index("col")
    row_index = lax.axis_index("row")
    row_sums = lax.psum(partial_rows.astype(jnp.bfloat16), "col").astype(jnp.float32)
    shifted_all = row_sums + bias_vector
    local_node_rows = lax.dynamic_slice_in_dim(shifted_all, col_index * node_dev, node_dev, 0)
    output = jax.nn.silu(local_node_rows).astype(jnp.bfloat16)
    cotangent_gathered_full = lax.all_gather(cotangent, "col", axis=0, tiled=True)
    slope_all = (cotangent_gathered_full.astype(jnp.float32) * silu_slope(shifted_all)).astype(
        jnp.bfloat16
    )
    grad_blocks = slope_all.reshape(row_block_ids, block_size, feature_width)

    def backward_step(group_index, totals):
        blocks_here, rows_group, cols_group, is_live = slot_group(group_index)
        gathered = jnp.take(grad_blocks, rows_group, axis=0)
        block_products = jnp.einsum(
            "sab,saf->sbf", blocks_here, gathered, preferred_element_type=jnp.float32
        )
        block_products = block_products * is_live.astype(jnp.float32)[:, None, None]
        return totals.at[cols_group].add(block_products)

    partial_cols = lax.fori_loop(
        0,
        group_total,
        backward_step,
        jnp.zeros((col_blocks, block_size, feature_width), jnp.float32),
    )
    partial_cols = partial_cols.reshape(col_blocks * block_size, feature_width)
    col_sums = lax.psum(partial_cols.astype(jnp.bfloat16), "row").astype(jnp.float32)
    own_grad = lax.dynamic_slice_in_dim(col_sums, row_index * node_dev, node_dev, 0)
    grad_hidden = own_grad.astype(jnp.bfloat16)
    grad_x = lax.dot_general(
        grad_hidden, weight, (((1,), (1,)), ((), ())), preferred_element_type=jnp.float32
    ).astype(jnp.bfloat16)
    weight_term = lax.dot_general(
        features_in, grad_hidden, (((0,), (0,)), ((), ())), preferred_element_type=jnp.float32
    )
    scale_factor = 1.0 / math.sqrt(node_dev * rows_count * cols_count)
    grad_w = lax.psum(weight_term, ("row", "col")) * scale_factor
    return (output, grad_x, grad_w)


def solution(mesh):
    in_specs = (
        P(("row", "col"), None),
        P(),
        P(),
        P(("row", "col"), None),
        P("row", "col", None, None, None),
        P("row", "col", None),
        P("row", "col", None),
        P("row", "col"),
    )
    out_specs = (P(("row", "col"), None), P(("row", "col"), None), P())
    return jax.shard_map(
        per_device, mesh=mesh, in_specs=in_specs, out_specs=out_specs, check_vma=False
    )
```

profile of v0, /device:TPU:2, one launch (start us, length us, event | category | flops | bytes accessed | tf_op | source)
XLA Modules:
  0.0 982.7 jit_solution(7380397596443363488)
XLA Ops:
  8.1 1.8 convolution_convert_fusion.1
  11.5 58.0 %all-gather.3.cloned.1.call-done = bf16[8192,256]{1,0:T(8,128)(2,1)} async-done(((bf16[512,256]{1,0:T(8,128)(2,1)}), bf16[8192,256]{1,0:T(8,128)(2,1)}) %all-gather.3.cloned.1.call-update) | async-done | bytes 4194320 | tf_op jit(solution)/shard_map/all_gather | solution.py:44
  69.5 2.4 broadcast_in_dim.39
  71.9 258.5 %while.20 = (s32[]{:T(128)}, f32[32,128,256]{2,1,0:T(8,128)}, s32[]{:T(128)}, s32[512]{0:T(512)S(1)}, bf16[512,128,128]{2,1,0:T(8,128)(2,1)}, /*index=5*/s32[512...) while((s32[]{:T(128)}, f32[32,128,256]{2,1,0:T(8,128)}, ...), condition=%wide.region_2.3_spmd, body=%wide.region_0.2_spmd.sunk | while | flops 543164160 | bytes 48241208 | solution.py:56
  72.7 4.9 gather_fusion
  77.7 7.5 broadcast_multiply_fusion.5
  85.1 19.4 %scatter_fusion = f32[32,128,256]{2,1,0:T(8,128)} fusion(f32[32,128,256]{2,1,0:T(8,128)} %get-tuple-element.267, s32[64]{0:T(128)S(1)} %compare_select_fusion.8, f32[64,128,256]{2,1,0:T(8,128)} %broadcast_multiply_fusion.5), kind=kCustom, calls=%fused_computation.2.clone.1 | custom fusion | flops 2097152 | bytes 25166080 | tf_op jit(solution)/shard_map/while/body/scatter-add | solution.py:54
  105.4 5.0 gather_fusion
  110.3 7.4 broadcast_multiply_fusion.5
  117.7 19.3 %scatter_fusion = f32[32,128,256]{2,1,0:T(8,128)} fusion(f32[32,128,256]{2,1,0:T(8,128)} %get-tuple-element.267, s32[64]{0:T(128)S(1)} %compare_select_fusion.8, f32[64,128,256]{2,1,0:T(8,128)} %broadcast_multiply_fusion.5), kind=kCustom, calls=%fused_computation.2.clone.1 | custom fusion | flops 2097152 | bytes 25166080 | tf_op jit(solution)/shard_map/while/body/scatter-add | solution.py:54
  137.8 4.9 gather_fusion
  142.7 7.4 broadcast_multiply_fusion.5
  150.1 19.0 %scatter_fusion = f32[32,128,256]{2,1,0:T(8,128)} fusion(f32[32,128,256]{2,1,0:T(8,128)} %get-tuple-element.267, s32[64]{0:T(128)S(1)} %compare_select_fusion.8, f32[64,128,256]{2,1,0:T(8,128)} %broadcast_multiply_fusion.5), kind=kCustom, calls=%fused_computation.2.clone.1 | custom fusion | flops 2097152 | bytes 25166080 | tf_op jit(solution)/shard_map/while/body/scatter-add | solution.py:54
  169.9 4.9 gather_fusion
  174.9 7.4 broadcast_multiply_fusion.5
  182.2 19.0 %scatter_fusion = f32[32,128,256]{2,1,0:T(8,128)} fusion(f32[32,128,256]{2,1,0:T(8,128)} %get-tuple-element.267, s32[64]{0:T(128)S(1)} %compare_select_fusion.8, f32[64,128,256]{2,1,0:T(8,128)} %broadcast_multiply_fusion.5), kind=kCustom, calls=%fused_computation.2.clone.1 | custom fusion | flops 2097152 | bytes 25166080 | tf_op jit(solution)/shard_map/while/body/scatter-add | solution.py:54
  202.1 4.9 gather_fusion
  207.0 7.4 broadcast_multiply_fusion.5
  214.4 19.3 %scatter_fusion = f32[32,128,256]{2,1,0:T(8,128)} fusion(f32[32,128,256]{2,1,0:T(8,128)} %get-tuple-element.267, s32[64]{0:T(128)S(1)} %compare_select_fusion.8, f32[64,128,256]{2,1,0:T(8,128)} %broadcast_multiply_fusion.5), kind=kCustom, calls=%fused_computation.2.clone.1 | custom fusion | flops 2097152 | bytes 25166080 | tf_op jit(solution)/shard_map/while/body/scatter-add | solution.py:54
  234.5 4.9 gather_fusion
  239.4 7.4 broadcast_multiply_fusion.5
  246.8 19.0 %scatter_fusion = f32[32,128,256]{2,1,0:T(8,128)} fusion(f32[32,128,256]{2,1,0:T(8,128)} %get-tuple-element.267, s32[64]{0:T(128)S(1)} %compare_select_fusion.8, f32[64,128,256]{2,1,0:T(8,128)} %broadcast_multiply_fusion.5), kind=kCustom, calls=%fused_computation.2.clone.1 | custom fusion | flops 2097152 | bytes 25166080 | tf_op jit(solution)/shard_map/while/body/scatter-add | solution.py:54
  266.6 4.9 gather_fusion
  271.5 7.4 broadcast_multiply_fusion.5
  278.9 19.5 %scatter_fusion = f32[32,128,256]{2,1,0:T(8,128)} fusion(f32[32,128,256]{2,1,0:T(8,128)} %get-tuple-element.267, s32[64]{0:T(128)S(1)} %compare_select_fusion.8, f32[64,128,256]{2,1,0:T(8,128)} %broadcast_multiply_fusion.5), kind=kCustom, calls=%fused_computation.2.clone.1 | custom fusion | flops 2097152 | bytes 25166080 | tf_op jit(solution)/shard_map/while/body/scatter-add | solution.py:54
  299.1 4.9 gather_fusion
  304.1 7.4 broadcast_multiply_fusion.5
  311.4 19.0 %scatter_fusion = f32[32,128,256]{2,1,0:T(8,128)} fusion(f32[32,128,256]{2,1,0:T(8,128)} %get-tuple-element.267, s32[64]{0:T(128)S(1)} %compare_select_fusion.8, f32[64,128,256]{2,1,0:T(8,128)} %broadcast_multiply_fusion.5), kind=kCustom, calls=%fused_computation.2.clone.1 | custom fusion | flops 2097152 | bytes 25166080 | tf_op jit(solution)/shard_map/while/body/scatter-add | solution.py:54
  330.4 3.8 convert_element_type.51
  334.3 21.9 %copy.11 = bf16[1,1,512,128,128]{3,4,2,1,0:T(8,128)(2,1)} copy(bf16[1,1,512,128,128]{4,3,2,1,0:T(8,128)(2,1)} %bitcast.19) | data formatting | bytes 33554432 | tf_op args[4]
  356.3 58.9 %all-reduce.4.cloned.1.call-done = bf16[4096,256]{1,0:T(8,128)(2,1)} async-done(((bf16[4096,256]{1,0:T(8,128)(2,1)}), bf16[4096,256]{1,0:T(8,128)(2,1)}) %all-reduce.4.cloned.1.call-update) | async-done | bytes 2097168 | tf_op jit(solution)/shard_map/psum | solution.py:65
  415.1 6.0 multiply_convert_fusion
  421.1 4.3 broadcast_in_dim.40
  425.4 244.1 %while.21 = (s32[]{:T(128)}, f32[64,128,256]{2,1,0:T(8,128)}, s32[]{:T(128)}, s32[512]{0:T(512)S(1)}, bf16[512,128,128]{1,2,0:T(8,128)(2,1)}, /*index=5*/s32[512...) while((s32[]{:T(128)}, f32[64,128,256]{2,1,0:T(8,128)}, ...), condition=%wide.region_6.7_spmd, body=%wide.region_4.6_spmd.sunk | while | flops 543164160 | bytes 48241208 | solution.py:84
  426.2 2.8 gather_fusion.1
  428.9 7.4 broadcast_multiply_fusion.6
  436.3 19.7 %scatter_fusion.1 = f32[64,128,256]{2,1,0:T(8,128)} fusion(f32[64,128,256]{2,1,0:T(8,128)} %get-tuple-element.303, s32[64]{0:T(128)S(1)} %compare_select_fusion.9, f32[64,128,256]{2,1,0:T(8,128)} %broadcast_multiply_fusion.6), kind=kCustom, calls=%fused_computation.3.clone.1 | custom fusion | flops 2097152 | bytes 25166080 | tf_op jit(solution)/shard_map/while/body/scatter-add | solution.py:82
  456.8 2.8 gather_fusion.1
  459.5 7.4 broadcast_multiply_fusion.6
  466.9 19.5 %scatter_fusion.1 = f32[64,128,256]{2,1,0:T(8,128)} fusion(f32[64,128,256]{2,1,0:T(8,128)} %get-tuple-element.303, s32[64]{0:T(128)S(1)} %compare_select_fusion.9, f32[64,128,256]{2,1,0:T(8,128)} %broadcast_multiply_fusion.6), kind=kCustom, calls=%fused_computation.3.clone.1 | custom fusion | flops 2097152 | bytes 25166080 | tf_op jit(solution)/shard_map/while/body/scatter-add | solution.py:82
  487.3 2.8 gather_fusion.1
  490.0 7.4 broadcast_multiply_fusion.6
  497.4 19.6 %scatter_fusion.1 = f32[64,128,256]{2,1,0:T(8,128)} fusion(f32[64,128,256]{2,1,0:T(8,128)} %get-tuple-element.303, s32[64]{0:T(128)S(1)} %compare_select_fusion.9, f32[64,128,256]{2,1,0:T(8,128)} %broadcast_multiply_fusion.6), kind=kCustom, calls=%fused_computation.3.clone.1 | custom fusion | flops 2097152 | bytes 25166080 | tf_op jit(solution)/shard_map/while/body/scatter-add | solution.py:82
  517.8 2.8 gather_fusion.1
  520.5 7.4 broadcast_multiply_fusion.6
  527.9 19.8 %scatter_fusion.1 = f32[64,128,256]{2,1,0:T(8,128)} fusion(f32[64,128,256]{2,1,0:T(8,128)} %get-tuple-element.303, s32[64]{0:T(128)S(1)} %compare_select_fusion.9, f32[64,128,256]{2,1,0:T(8,128)} %broadcast_multiply_fusion.6), kind=kCustom, calls=%fused_computation.3.clone.1 | custom fusion | flops 2097152 | bytes 25166080 | tf_op jit(solution)/shard_map/while/body/scatter-add | solution.py:82
  548.5 2.8 gather_fusion.1
  551.3 7.4 broadcast_multiply_fusion.6
  558.7 19.4 %scatter_fusion.1 = f32[64,128,256]{2,1,0:T(8,128)} fusion(f32[64,128,256]{2,1,0:T(8,128)} %get-tuple-element.303, s32[64]{0:T(128)S(1)} %compare_select_fusion.9, f32[64,128,256]{2,1,0:T(8,128)} %broadcast_multiply_fusion.6), kind=kCustom, calls=%fused_computation.3.clone.1 | custom fusion | flops 2097152 | bytes 25166080 | tf_op jit(solution)/shard_map/while/body/scatter-add | solution.py:82
  578.9 2.8 gather_fusion.1
  581.6 7.4 broadcast_multiply_fusion.6
  589.0 19.6 %scatter_fusion.1 = f32[64,128,256]{2,1,0:T(8,128)} fusion(f32[64,128,256]{2,1,0:T(8,128)} %get-tuple-element.303, s32[64]{0:T(128)S(1)} %compare_select_fusion.9, f32[64,128,256]{2,1,0:T(8,128)} %broadcast_multiply_fusion.6), kind=kCustom, calls=%fused_computation.3.clone.1 | custom fusion | flops 2097152 | bytes 25166080 | tf_op jit(solution)/shard_map/while/body/scatter-add | solution.py:82
  609.4 2.8 gather_fusion.1
  612.1 7.4 broadcast_multiply_fusion.6
  619.5 19.5 %scatter_fusion.1 = f32[64,128,256]{2,1,0:T(8,128)} fusion(f32[64,128,256]{2,1,0:T(8,128)} %get-tuple-element.303, s32[64]{0:T(128)S(1)} %compare_select_fusion.9, f32[64,128,256]{2,1,0:T(8,128)} %broadcast_multiply_fusion.6), kind=kCustom, calls=%fused_computation.3.clone.1 | custom fusion | flops 2097152 | bytes 25166080 | tf_op jit(solution)/shard_map/while/body/scatter-add | solution.py:82
  639.9 2.8 gather_fusion.1
  642.6 7.4 broadcast_multiply_fusion.6
  650.0 19.4 %scatter_fusion.1 = f32[64,128,256]{2,1,0:T(8,128)} fusion(f32[64,128,256]{2,1,0:T(8,128)} %get-tuple-element.303, s32[64]{0:T(128)S(1)} %compare_select_fusion.9, f32[64,128,256]{2,1,0:T(8,128)} %broadcast_multiply_fusion.6), kind=kCustom, calls=%fused_computation.3.clone.1 | custom fusion | flops 2097152 | bytes 25166080 | tf_op jit(solution)/shard_map/while/body/scatter-add | solution.py:82
  669.4 6.0 convert_element_type.57
  675.5 1.9 multiply_convert_fusion.1
  677.4 150.2 %all-reduce.6.cloned.1.call-done = bf16[8192,256]{1,0:T(8,128)(2,1)} async-done(((bf16[8192,256]{1,0:T(8,128)(2,1)}), bf16[8192,256]{1,0:T(8,128)(2,1)}) %all-reduce.6.cloned.1.call-update) | async-done | bytes 4194320 | tf_op jit(solution)/shard_map/psum | solution.py:91
  827.6 1.9 convolution_bitcast_fusion
  829.5 1.9 convolution_convert_fusion
  831.5 142.9 %all-reduce.8.cloned.1.call-done = f32[256,256]{0,1:T(8,128)} async-done(((f32[256,256]{0,1:T(8,128)}), f32[256,256]{0,1:T(8,128)}) %all-reduce.8.cloned.1.call-update) | async-done | bytes 262160 | tf_op jit(solution)/shard_map/psum | solution.py:101
  (71 shorter events, 16.6 us)
Async XLA Ops:
  7.2 1.0 copy-start
  7.2 64.8 %copy-start.3 = (s32[1,1,512]{2,1,0:T(1,128)S(1)}, s32[1,1,512]{2,1,0:T(1,128)}, u32[]{:S(2)}) copy-start(s32[1,1,512]{2,1,0:T(1,128)} %param.18) | copy-start | bytes 6148
  7.2 64.7 %copy-start.2 = (s32[1,1,512]{2,1,0:T(1,128)S(1)}, s32[1,1,512]{2,1,0:T(1,128)}, u32[]{:S(2)}) copy-start(s32[1,1,512]{2,1,0:T(1,128)} %param.17) | copy-start | bytes 6148
  7.2 62.3 %all-gather.3.cloned.1.call-start = ((), (), s32[]{:S(2)}) async-start(), calls=%async_computation | async-start | bytes 4456448 | tf_op jit(solution)/shard_map/all_gather | solution.py:44
  10.0 346.3 %all-gather.5.cloned.1.call-start = ((), (), s32[]{:S(2)}) async-start(), calls=%async_computation.2 | async-start | bytes 2359296 | tf_op jit(solution)/shard_map/all_gather | solution.py:69
  10.7 404.4 %all-reduce.4.cloned.1.call-start = ((), (), s32[]{:S(2)}) async-start(), calls=%async_computation.1 | async-start | bytes 4194304 | tf_op jit(solution)/shard_map/psum | solution.py:65
  334.3 493.3 %all-reduce.6.cloned.1.call-start = ((), (), s32[]{:S(2)}) async-start(), calls=%async_computation.3 | async-start | bytes 8388608 | tf_op jit(solution)/shard_map/psum | solution.py:91
  334.3 80.8 %copy-start.4 = (f32[256]{0:T(256)S(1)}, f32[256]{0:T(256)}, u32[]{:S(2)}) copy-start(f32[256]{0:T(256)} %param.14) | copy-start | bytes 3076
  675.4 154.1 %copy-start.1 = (bf16[256,256]{1,0:T(8,128)(2,1)S(1)}, bf16[256,256]{1,0:T(8,128)(2,1)}, u32[]{:S(2)}) copy-start(bf16[256,256]{1,0:T(8,128)(2,1)} %param.13) | copy-start | bytes 393220
  675.4 299.0 %all-reduce.8.cloned.1.call-start = ((), (), s32[]{:S(2)}) async-start(), calls=%async_computation.4 | async-start | bytes 524288 | tf_op jit(solution)/shard_map/psum | solution.py:101
Sparse Core Ops, SparseCore 0:
  11.0 58.4 all-gather.2
  71.1 37.7 all-gather.4
  334.4 80.6 all-reduce.3
  675.6 151.9 all-reduce.5
  832.8 141.5 all-reduce.7
where the time goes:
time: 985 us; the launch traced here: 983 us
  waiting for transfers between devices  411 us (42%)
  other arithmetic  342 us (35%)
  matrix products  124 us (13%)
  local copies, waits for them, and re-layouts  91.9 us (9%)
  between operations  14.5 us (1%)
    scatter-add x8, other arithmetic, backward_step(): return totals.at[cols_group].add(block_products)  157 us
    scatter-add x8, other arithmetic, forward_step(): return totals.at[rows_group].add(block_products)  153 us
    psum x1, waiting for transfers between devices, per_device(): lax.psum(partial_cols.astype(jnp.bfloat16), 'row').astype(jnp.float32)  150 us
    psum x1, waiting for transfers between devices, per_device(): grad_w = lax.psum(weight_term, ('row', 'col')) * scale_factor  143 us
    dot_general x8, matrix products, forward_step(): jnp.einsum('sab,sbf->saf', blocks_here, gathered, preferred_element_type=...  59.1 us
    dot_general x8, matrix products, backward_step(): jnp.einsum('sab,saf->sbf', blocks_here, gathered, preferred_element_type=...  59 us
    psum x1, waiting for transfers between devices, per_device(): lax.psum(partial_rows.astype(jnp.bfloat16), 'col').astype(jnp.float32)  58.9 us
    all_gather x1, waiting for transfers between devices, per_device(): column_set = lax.all_gather(hidden_in, 'row', axis=0, tiled=True)  58 us
  transfers between devices with their start and end apart: 5, of which 4 were waited for; matrix products, arithmetic and copies ran while one was open for 30% of the time, Pallas kernels for 0%

commit v1 on v0

v1 whole, which is shorter than its diff:
```python
import functools
import math

import jax
import jax.numpy as jnp
from jax import lax
from jax.experimental import pallas as pl
from jax.experimental.pallas import tpu as pltpu
from jax.sharding import PartitionSpec as P

bf16 = jnp.bfloat16
f32 = jnp.float32

group = 4
chunk = 32
buffers = 4
z_cols, x_cols = 2, 4


def xor_pairs(size, mask):
    return [(index, index ^ mask) for index in range(size)]


def row_swap(value, mask):
    return lax.ppermute(value, "row", xor_pairs(16, mask))


def col_swap(value, mask):
    return lax.ppermute(value, "col", xor_pairs(8, mask))


def slot_plan(target, source, live, target_total, source_total, position_total):
    slot_total = target.shape[0]
    slots = jnp.arange(slot_total, dtype=jnp.int32)
    target = jnp.where(live, target, target_total)
    targets = jnp.arange(target_total, dtype=jnp.int32)
    member = target[None, :] == targets[:, None]
    sizes = jnp.sum(member.astype(jnp.int32), axis=1)
    padded = ((sizes + group - 1) >> 2) << 2
    ends = jnp.sum(jnp.where(targets[None, :] <= targets[:, None], padded[None, :], 0), axis=1)
    starts = ends - padded
    same_before = (target[None, :] == target[:, None]) & (slots[None, :] < slots[:, None])
    ranks = jnp.sum(same_before.astype(jnp.int32), axis=1)
    position = jnp.sum(jnp.where(member, starts[:, None], 0), axis=0) + ranks
    position = jnp.where(live, position, -1)
    positions = jnp.arange(position_total, dtype=jnp.int32)
    hit = position[None, :] == positions[:, None]
    entry = slots * 128 + source - source_total
    entries = jnp.sum(jnp.where(hit, entry[None, :], 0), axis=1) + source_total
    first = jnp.arange(position_total // group, dtype=jnp.int32) * group
    group_targets = jnp.sum((ends[None, :] <= first[:, None]).astype(jnp.int32), axis=1)
    chunks = (ends[-1:] + chunk - 1) // chunk
    return jnp.concatenate([entries, group_targets, chunks])


def spmm_kernel(piece_total, position_total, source_total, target_total, transposed, *refs):
    plan, blocks = refs[:2]
    pieces = refs[2 : 2 + piece_total]
    outs = refs[2 + piece_total : -5]
    held, source, total, chunk_sems, piece_sems = refs[-5:]
    chunk_total = plan[position_total + position_total // group]

    def fetch(index):
        place = lax.rem(index, buffers)

        def some(step, carry):
            for member in range(8):
                at = step * 8 + member
                slot = plan[index * chunk + at] >> 7
                pltpu.make_async_copy(
                    blocks.at[slot], held.at[place, at], chunk_sems.at[place]
                ).start()
            return carry

        lax.fori_loop(0, chunk // 8, some, 0)

    piece_copies = [
        pltpu.make_async_copy(piece, source.at[pl.ds(4 * index, 4)], piece_sems.at[index])
        for index, piece in enumerate(pieces)
    ]
    for index in range(buffers - 1):

        @pl.when(index < chunk_total)
        def _():
            fetch(index)

        if index == 0:
            for copy in piece_copies:
                copy.start()

    total[...] = jnp.zeros_like(total)
    source[source_total] = jnp.zeros(source.shape[1:], source.dtype)
    for copy in piece_copies:
        copy.wait()

    def chunk_step(index, carry):
        @pl.when(index + buffers - 1 < chunk_total)
        def _():
            fetch(index + buffers - 1)

        place = lax.rem(index, buffers)
        pltpu.make_async_copy(
            blocks.at[pl.ds(0, chunk)], held.at[place], chunk_sems.at[place]
        ).wait()
        for member in range(chunk // group):
            first = member * group
            target = plan[position_total + index * (chunk // group) + member]
            right = jnp.concatenate(
                [source[plan[index * chunk + first + q] & 127] for q in range(group)], axis=0
            )
            left = [held[place, first + q] for q in range(group)]
            if transposed:
                product = lax.dot_general(
                    jnp.concatenate(left, axis=0),
                    right,
                    (((0,), (0,)), ((), ())),
                    preferred_element_type=f32,
                )
            else:
                product = jnp.dot(
                    jnp.concatenate(left, axis=1), right, preferred_element_type=f32
                )
            total[target] += product
        return carry

    lax.fori_loop(0, chunk_total, chunk_step, 0)
    done = 0
    for out in outs:
        count = math.prod(out.shape[:-2])
        out[...] = total[done : done + count].astype(out.dtype).reshape(out.shape)
        done += count


def spmm(plan, blocks, pieces, target_total, position_total, out_shapes, transposed):
    piece_total = len(pieces)
    source_total = 4 * piece_total
    width = pieces[0].shape[-1]
    any_space = pl.BlockSpec(memory_space=pl.ANY)
    return pl.pallas_call(
        functools.partial(
            spmm_kernel, piece_total, position_total, source_total, target_total, transposed
        ),
        out_shape=[jax.ShapeDtypeStruct(shape, bf16) for shape in out_shapes],
        in_specs=[pl.BlockSpec(memory_space=pltpu.SMEM)] + [any_space] * (1 + piece_total),
        out_specs=[pl.BlockSpec(memory_space=pltpu.VMEM)] * len(out_shapes),
        scratch_shapes=[
            pltpu.VMEM((buffers, chunk, 128, 128), bf16),
            pltpu.VMEM((source_total + 1, 128, width), bf16),
            pltpu.VMEM((target_total + 1, 128, width), f32),
            pltpu.SemaphoreType.DMA((buffers,)),
            pltpu.SemaphoreType.DMA((piece_total,)),
        ],
        compiler_params=pltpu.CompilerParams(vmem_limit_bytes=48 << 20),
        cost_estimate=pl.CostEstimate(
            flops=2 * 512 * 128 * 128 * width, bytes_accessed=24 << 20, transcendentals=0
        ),
    )(plan, blocks, *pieces)


def node_kernel(p0, p1, p2, p3, p4, weight, bias, cotangent, output, sent, weight_grad):
    sums = p0[...].astype(f32)
    for part in (p1, p2, p3, p4):
        sums += part[...].astype(f32)
    aggregated = sums.reshape(output.shape).astype(bf16)
    shifted = jnp.dot(aggregated, weight[...], preferred_element_type=f32) + bias[...]
    sigmoid = jax.nn.sigmoid(shifted)
    output[...] = (shifted * sigmoid).astype(bf16)
    slope = sigmoid * (1.0 + shifted * (1.0 - sigmoid))
    slope_term = (cotangent[...].astype(f32) * slope).astype(bf16)
    sent[...] = lax.dot_general(
        slope_term, weight[...], (((1,), (1,)), ((), ())), preferred_element_type=f32
    ).astype(bf16).reshape(sent.shape)
    weight_grad[...] = lax.dot_general(
        aggregated, slope_term, (((0,), (0,)), ((), ())), preferred_element_type=f32
    )


def add_up(*parts):
    sums = parts[0].astype(f32)
    for part in parts[1:]:
        sums = sums + part.astype(f32)
    return sums


def per_device(
    features_in, weight, bias_vector, cotangent, adjacency, block_rows, block_cols, counts
):
    node_dev, width = features_in.shape
    piece = (4, 128, width)
    blocks = adjacency[0, 0]
    rows_here = block_rows[0, 0]
    cols_here = block_cols[0, 0]
    slot_total = rows_here.shape[0]
    live = jnp.arange(slot_total, dtype=jnp.int32) < counts[0, 0]
    row_index = lax.axis_index("row")
    col_index = lax.axis_index("col")

    row_place = (((col_index ^ (rows_here >> 2)) << 2) | (rows_here & 3)).astype(jnp.int32)
    partner = row_index ^ (cols_here >> 2)
    col_place = ((((partner & 1) << 3) | (partner >> 1)) << 2) | (cols_here & 3)
    forward_plan = slot_plan(row_place, col_place, live, 32, 64, slot_total + 96)
    backward_plan = slot_plan(col_place, row_place, live, 64, 32, slot_total + 192)

    own = features_in.reshape(piece)
    beside = row_swap(own, 2)
    near = [own, beside]
    for y in (1, 3, 2):
        near += [row_swap(own, 4 * y), row_swap(beside, 4 * y)]
    near = near[:2] + near[2:4] + near[6:8] + near[4:6]
    gathered = near + [row_swap(part, 1) for part in near]

    parts = spmm(forward_plan, blocks, gathered, 32, slot_total + 96, [piece] * 8, False)
    across = [col_swap(parts[4 + x], x) for x in (1, 3, 2)]
    here = [col_swap(parts[x], x) for x in (1, 3, 2)]
    across_sum = add_up(parts[4], *across).astype(bf16)
    from_across = col_swap(across_sum, 4)

    output, sent, weight_grad = pl.pallas_call(
        node_kernel,
        out_shape=[
            jax.ShapeDtypeStruct((node_dev, width), bf16),
            jax.ShapeDtypeStruct(piece, bf16),
            jax.ShapeDtypeStruct((width, width), f32),
        ],
        compiler_params=pltpu.CompilerParams(vmem_limit_bytes=32 << 20),
    )(parts[0], *here, from_across, weight, bias_vector[None, :], cotangent)

    beside = col_swap(sent, 4)
    x_order = (1, 3, 2)
    from_here = {x: col_swap(sent, x) for x in x_order}
    from_there = {x: col_swap(beside, x) for x in x_order}
    spread = [sent] + [from_here[x] for x in (1, 2, 3)]
    spread += [beside] + [from_there[x] for x in (1, 2, 3)]

    device_total = 128
    scatter = lax.all_to_all(
        weight_grad.reshape(device_total, -1), ("row", "col"), 0, 0, tiled=True
    )
    scattered = jnp.sum(scatter, axis=0, keepdims=True) * (
        1.0 / math.sqrt(node_dev * device_total)
    )
    grad_w = lax.all_to_all(
        jnp.broadcast_to(scattered, scatter.shape), ("row", "col"), 0, 0, tiled=True
    ).reshape(width, width)

    halves = spmm(
        backward_plan, blocks, spread, 64, slot_total + 192, [(8,) + piece] * 2, True
    )
    mine, theirs = halves
    swapped = row_swap(theirs, 1)
    summed = [add_up(mine[index], swapped[index]).astype(bf16) for index in range(8)]
    across = [row_swap(summed[2 * y + 1], 4 * y) for y in (1, 3, 2)]
    here = [row_swap(summed[2 * y], 4 * y) for y in (1, 3, 2)]
    across_sum = add_up(summed[1], *across).astype(bf16)
    from_across = row_swap(across_sum, 2)
    grad_x = add_up(summed[0], *here, from_across).astype(bf16).reshape(node_dev, width)
    return (output, grad_x, grad_w)


def solution(mesh):
    in_specs = (
        P(("row", "col"), None),
        P(),
        P(),
        P(("row", "col"), None),
        P("row", "col", None, None, None),
        P("row", "col", None),
        P("row", "col", None),
        P("row", "col"),
    )
    out_specs = (P(("row", "col"), None), P(("row", "col"), None), P())
    return jax.shard_map(
        per_device, mesh=mesh, in_specs=in_specs, out_specs=out_specs, check_vma=False
    )
```

time: 985 us -> 178 us (0.18)
  waiting for transfers between devices: 411 us -> 50.1 us
  other arithmetic: 342 us -> 10.1 us
  matrix products: 124 us -> 0 us
  local copies, waits for them, and re-layouts: 91.9 us -> 3.77 us
  starting transfers between devices: 0.2 us -> 45.3 us
  blocking collectives: 0 us -> 38.9 us
  Pallas kernels: 0 us -> 24.5 us
  between operations: 14.5 us -> 2.85 us
    psum x3 -> x0, waiting for transfers between devices: 352 us -> none  [the longest x1 150 us: per_device(): lax.psum(partial_cols.astype(jnp.bfloat16), 'row').astype(jnp.float32)]
    scatter-add x16 -> x0, other arithmetic: 310 us -> none  [the longest x8 157 us: backward_step(): return totals.at[cols_group].add(block_products)]
    dot_general x19 -> x0, matrix products: 124 us -> none  [the longest x8 59.1 us: forward_step(): jnp.einsum('sab,sbf->saf', blocks_here, gathered, preferred_element_type=...]
    gather x16 -> x0, local copies, waits for them, and re-layouts: 61.6 us -> none  [the longest x8 39.5 us: forward_step(): gathered = jnp.take(column_set, cols_group, axis=0)]
    all_gather x2 -> x0, waiting for transfers between devices: 58 us -> none  [the longest x1 58 us: per_device(): column_set = lax.all_gather(hidden_in, 'row', axis=0, tiled=True)]
    ppermute x0 -> x37, waiting for transfers between devices: none -> 50.1 us  [the longest x14 33.3 us: col_swap(): return lax.ppermute(value, 'col', xor_pairs(8, mask))]
    ppermute x0 -> x37, starting transfers between devices: none -> 45.3 us  [the longest x23 26.4 us: row_swap(): return lax.ppermute(value, 'row', xor_pairs(16, mask))]
    all_to_all x0 -> x2, blocking collectives: none -> 38.9 us  [the longest x1 22.9 us: per_device(): lax.all_to_all(weight_grad.reshape(device_total, -1), ('row', 'col'), 0,...]
  transfers between devices with their start and end apart: 5 -> 37, of which waited for: 4 -> 16; matrix products, arithmetic and copies ran while one was open for 30% -> 5% of each run, Pallas kernels for 0% -> 0%
where the time goes in v1:
time: 178 us; the launch traced here: 176 us
  waiting for transfers between devices  50.1 us (28%)
  starting transfers between devices  45.3 us (25%)
  blocking collectives  38.9 us (22%)
  Pallas kernels  24.5 us (14%)
  other arithmetic  10.1 us (6%)
  local copies, waits for them, and re-layouts  3.77 us (2%)
  between operations  2.85 us (2%)
    ppermute x14, waiting for transfers between devices, col_swap(): return lax.ppermute(value, 'col', xor_pairs(8, mask))  33.3 us
    ppermute x23, starting transfers between devices, row_swap(): return lax.ppermute(value, 'row', xor_pairs(16, mask))  26.4 us
    pallas_call x2, Pallas kernels, spmm(): pl.pallas_call(functools.partial(spmm_kernel, piece_total, position_total...  23.5 us
    all_to_all x1, blocking collectives, per_device(): lax.all_to_all(weight_grad.reshape(device_total, -1), ('row', 'col'), 0,...  22.9 us
    ppermute x14, starting transfers between devices, col_swap(): return lax.ppermute(value, 'col', xor_pairs(8, mask))  19 us
    ppermute x23, waiting for transfers between devices, row_swap(): return lax.ppermute(value, 'row', xor_pairs(16, mask))  16.7 us
    all_to_all x1, blocking collectives, per_device(): lax.all_to_all(jnp.broadcast_to(scattered, scatter.shape), ('row', 'col')...  16 us
  transfers between devices with their start and end apart: 37, of which 16 were waited for; matrix products, arithmetic and copies ran while one was open for 5% of the time, Pallas kernels for 0%

profile of v1, /device:TPU:2, one launch (start us, length us, event | category | flops | bytes accessed | tf_op | source)
XLA Modules:
  0.0 175.6 jit_solution(9089216177876204991)
XLA Ops:
  0.7 3.1 %collective-permute-start.5 = (bf16[4,128,256]{2,1,0:T(8,128)(2,1)}, bf16[4,128,256]{2,1,0:T(8,128)(2,1)S(1)}, u32[]{:S(2)}, u32[]{:S(2)}) collective-permute-start(bf16[4,128,256]{2,1,0:T(8,128)(2,1)} %bitcast.33), channel_id=1, source_target_pairs={{0,96},{8,104},{16,112},{24,120},{32,64},{40,72},{48,80},{56,88},{... | collective-permute-start | bytes 786440 | tf_op jit(solution)/shard_map/ppermute | solution.py:25
  3.8 0.6 collective-permute-start.3
  4.4 0.5 collective-permute-start.1
  4.9 3.9 %collective-permute-start = (bf16[4,128,256]{2,1,0:T(8,128)(2,1)}, bf16[4,128,256]{2,1,0:T(8,128)(2,1)S(1)}, u32[]{:S(2)}, u32[]{:S(2)}) collective-permute-start(bf16[4,128,256]{2,1,0:T(8,128)(2,1)} %bitcast.36), channel_id=1, source_target_pairs={{0,16},{8,24},{16,0},{24,8},{32,48},{40,56},{48,32},{56,40},{64,80... | collective-permute-start | bytes 786440 | tf_op jit(solution)/shard_map/ppermute | solution.py:25
  9.4 0.7 shift-left_or_fusion
  10.3 0.3 convert_reduce_fusion
  10.7 0.7 and_or_fusion
  11.6 0.3 convert_reduce_fusion.1
  12.1 3.1 %collective-permute-done.refs_3_ = bf16[4,128,256]{2,1,0:T(8,128)(2,1)S(1)} collective-permute-done((bf16[4,128,256]{2,1,0:T(8,128)(2,1)}, bf16[4,128,256]{2,1,0:T(8,128)(2,1)S(1)}, u32[]{:S(2)}, u32[]{:S(2)}) %collective-permute-start) | collective-permute-done | bytes 262176 | tf_op jit(solution)/shard_map/ppermute | solution.py:25
  15.1 3.0 %collective-permute-start.6 = (bf16[4,128,256]{2,1,0:T(8,128)(2,1)S(1)}, bf16[4,128,256]{2,1,0:T(8,128)(2,1)S(1)}, u32[]{:S(2)}, u32[]{:S(2)}) collective-permute-start(bf16[4,128,256]{2,1,0:T(8,128)(2,1)S(1)} %collective-permute-done.refs_3_), channel_id=1, source_target_pairs={{0,96},{8,104},{16,112},{24,120},{32,64},{40,72},{48,80},{56,88},{... | collective-permute-start | bytes 786440 | tf_op jit(solution)/shard_map/ppermute | solution.py:25
  18.1 0.6 collective-permute-start.4
  18.7 0.5 collective-permute-start.2
  19.2 0.5 collective-permute-start.11
  19.7 0.2 select_reduce_fusion.1
  20.0 0.8 collective-permute-done.13.refs_16_
  20.9 0.2 collective-permute-done.11.refs_14_
  21.3 7.9 %collective-permute-done.6.refs_9_ = bf16[4,128,256]{2,1,0:T(8,128)(2,1)S(1)} collective-permute-done((bf16[4,128,256]{2,1,0:T(8,128)(2,1)S(1)}, bf16[4,128,256]{2,1,0:T(8,128)(2,1)S(1)}, u32[]{:S(2)}, u32[]{:S(2)}) %collective-permute-start.6) | collective-permute-done | bytes 262176 | tf_op jit(solution)/shard_map/ppermute | solution.py:25
  29.2 0.5 collective-permute-start.12
  29.9 0.6 slice.54
  31.3 0.2 collective-permute-done.10.refs_13_
  31.5 0.5 copy-done.5
  32.0 0.9 copy-done
  33.0 9.2 %shard_map.103 = (bf16[4,128,256]{2,1,0:T(8,128)(2,1)S(1)}, bf16[4,128,256]{2,1,0:T(8,128)(2,1)S(1)}, bf16[4,128,256]{2,1,0:T(8,128)(2,1)S(1)}, bf16[4,128,256]{...) custom-call(s32[761]{0:T(1024)S(1)} %pad_add_fusion.refs_0_, ...), custom_call_target="tpu_custom_call" | custom-call | flops 4294967296 | bytes 25165824 | tf_op jit(solution)/shard_map/pallas_call | solution.py:139
  42.2 1.6 collective-permute-start.19
  43.8 2.5 %collective-permute-start.20 = (bf16[4,128,256]{2,1,0:T(8,128)(2,1)S(1)}, bf16[4,128,256]{2,1,0:T(8,128)(2,1)S(1)}, u32[]{:S(2)}, u32[]{:S(2)}) collective-permute-start(bf16[4,128,256]{2,1,0:T(8,128)(2,1)S(1)} %get-tuple-element.23), channel_id=1, source_target_pairs={{0,2},{1,3},{2,0},{3,1},{4,6},{5,7},{6,4},{7,5},{8,10},{9,11},{10,... | collective-permute-start | bytes 786440 | tf_op jit(solution)/shard_map/ppermute | solution.py:29
  46.4 1.5 collective-permute-start.16
  47.9 3.4 %collective-permute-done.18 = bf16[4,128,256]{2,1,0:T(8,128)(2,1)S(1)} collective-permute-done((bf16[4,128,256]{2,1,0:T(8,128)(2,1)S(1)}, bf16[4,128,256]{2,1,0:T(8,128)(2,1)S(1)}, u32[]{:S(2)}, u32[]{:S(2)}) %collective-permute-start.18) | collective-permute-done | bytes 262176 | tf_op jit(solution)/shard_map/ppermute | solution.py:29
  51.4 0.9 collective-permute-start.17
  52.3 3.8 %collective-permute-done.19 = bf16[4,128,256]{2,1,0:T(8,128)(2,1)S(1)} collective-permute-done((bf16[4,128,256]{2,1,0:T(8,128)(2,1)S(1)}, bf16[4,128,256]{2,1,0:T(8,128)(2,1)S(1)}, u32[]{:S(2)}, u32[]{:S(2)}) %collective-permute-start.19) | collective-permute-done | bytes 262176 | tf_op jit(solution)/shard_map/ppermute | solution.py:29
  56.1 2.0 %collective-permute-done.20 = bf16[4,128,256]{2,1,0:T(8,128)(2,1)S(1)} collective-permute-done((bf16[4,128,256]{2,1,0:T(8,128)(2,1)S(1)}, bf16[4,128,256]{2,1,0:T(8,128)(2,1)S(1)}, u32[]{:S(2)}, u32[]{:S(2)}) %collective-permute-start.20) | collective-permute-done | bytes 262176 | tf_op jit(solution)/shard_map/ppermute | solution.py:29
  58.1 0.1 add_convert_fusion.8
  58.3 4.3 %collective-permute-done.15.p1 = bf16[4,128,256]{2,1,0:T(8,128)(2,1)S(1)} collective-permute-done((bf16[4,128,256]{2,1,0:T(8,128)(2,1)S(1)}, bf16[4,128,256]{2,1,0:T(8,128)(2,1)S(1)}, u32[]{:S(2)}, u32[]{:S(2)}) %collective-permute-start.15) | collective-permute-done | bytes 262176 | tf_op jit(solution)/shard_map/ppermute | solution.py:29
  62.7 5.4 %collective-permute-done.16.p2 = bf16[4,128,256]{2,1,0:T(8,128)(2,1)S(1)} collective-permute-done((bf16[4,128,256]{2,1,0:T(8,128)(2,1)S(1)}, bf16[4,128,256]{2,1,0:T(8,128)(2,1)S(1)}, u32[]{:S(2)}, u32[]{:S(2)}) %collective-permute-start.16) | collective-permute-done | bytes 262176 | tf_op jit(solution)/shard_map/ppermute | solution.py:29
  68.1 1.1 shard_map.104
  69.2 0.3 collective-permute-start.25
  69.5 1.2 collective-permute-start.24
  70.7 0.2 select_reduce_fusion
  71.0 2.9 %collective-permute-start.23 = (bf16[4,128,256]{2,1,0:T(8,128)(2,1)S(1)}, bf16[4,128,256]{2,1,0:T(8,128)(2,1)S(1)}, u32[]{:S(2)}, u32[]{:S(2)}) collective-permute-start(bf16[4,128,256]{2,1,0:T(8,128)(2,1)S(1)} %get-tuple-element.25.refs_2_), channel_id=1, source_target_pairs={{0,2},{1,3},{2,0},{3,1},{4,6},{5,7},{6,4},{7,5},{8,10},{9,11},{10,... | collective-permute-start | bytes 786440 | tf_op jit(solution)/shard_map/ppermute | solution.py:29
  73.8 0.7 collective-permute-start.22
  74.5 2.8 %collective-permute-done.25.refs_6_ = bf16[4,128,256]{2,1,0:T(8,128)(2,1)S(1)} collective-permute-done((bf16[4,128,256]{2,1,0:T(8,128)(2,1)S(1)}, bf16[4,128,256]{2,1,0:T(8,128)(2,1)S(1)}, u32[]{:S(2)}, u32[]{:S(2)}) %collective-permute-start.25) | collective-permute-done | bytes 262176 | tf_op jit(solution)/shard_map/ppermute | solution.py:29
  77.3 1.5 collective-permute-start.28
  78.8 2.5 %collective-permute-start.27 = (bf16[4,128,256]{2,1,0:T(8,128)(2,1)S(1)}, bf16[4,128,256]{2,1,0:T(8,128)(2,1)S(1)}, u32[]{:S(2)}, u32[]{:S(2)}) collective-permute-start(bf16[4,128,256]{2,1,0:T(8,128)(2,1)S(1)} %collective-permute-done.25.refs_6_), channel_id=1, source_target_pairs={{0,2},{1,3},{2,0},{3,1},{4,6},{5,7},{6,4},{7,5},{8,10},{9,11},{10,... | collective-permute-start | bytes 786440 | tf_op jit(solution)/shard_map/ppermute | solution.py:29
  81.3 3.0 %collective-permute-done.24.refs_5_ = bf16[4,128,256]{2,1,0:T(8,128)(2,1)S(1)} collective-permute-done((bf16[4,128,256]{2,1,0:T(8,128)(2,1)S(1)}, bf16[4,128,256]{2,1,0:T(8,128)(2,1)S(1)}, u32[]{:S(2)}, u32[]{:S(2)}) %collective-permute-start.24) | collective-permute-done | bytes 262176 | tf_op jit(solution)/shard_map/ppermute | solution.py:29
  84.3 3.1 %collective-permute-start.26 = (bf16[4,128,256]{2,1,0:T(8,128)(2,1)S(1)}, bf16[4,128,256]{2,1,0:T(8,128)(2,1)S(1)}, u32[]{:S(2)}, u32[]{:S(2)}) collective-permute-start(bf16[4,128,256]{2,1,0:T(8,128)(2,1)S(1)} %collective-permute-done.25.refs_6_), channel_id=1, source_target_pairs={{0,1},{1,0},{2,3},{3,2},{4,5},{5,4},{6,7},{7,6},{8,9},{9,8},{10,11... | collective-permute-start | bytes 786440 | tf_op jit(solution)/shard_map/ppermute | solution.py:29
  87.5 0.6 slice.55
  88.9 5.5 %collective-permute-done.28.refs_9_ = bf16[4,128,256]{2,1,0:T(8,128)(2,1)S(1)} collective-permute-done((bf16[4,128,256]{2,1,0:T(8,128)(2,1)S(1)}, bf16[4,128,256]{2,1,0:T(8,128)(2,1)S(1)}, u32[]{:S(2)}, u32[]{:S(2)}) %collective-permute-start.28) | collective-permute-done | bytes 262176 | tf_op jit(solution)/shard_map/ppermute | solution.py:29
  94.5 2.9 %collective-permute-done.26.refs_7_ = bf16[4,128,256]{2,1,0:T(8,128)(2,1)S(1)} collective-permute-done((bf16[4,128,256]{2,1,0:T(8,128)(2,1)S(1)}, bf16[4,128,256]{2,1,0:T(8,128)(2,1)S(1)}, u32[]{:S(2)}, u32[]{:S(2)}) %collective-permute-start.26) | collective-permute-done | bytes 262176 | tf_op jit(solution)/shard_map/ppermute | solution.py:29
  97.4 14.3 %shard_map.105 = (bf16[8,4,128,256]{3,2,1,0:T(8,128)(2,1)S(1)}, bf16[8,4,128,256]{3,2,1,0:T(8,128)(2,1)}) custom-call(s32[881]{0:T(1024)S(1)} %pad_add_fusion.1.refs_0_, bf16[512,128,128]{2,1,0:T(8,128)(2,1)} %bitcast.40, bf16[4,128,256]{2,1,0:T(8,128)(2,1)S(1)} %get-tuple-element.25.refs_2_, bf16[4,128,256]{2,1,0:T(8,128)(2,1)S(1)} %collective-permute-done.22.refs_3_, ...), custom_call_target="tpu_custom_call" | custom-call | flops 4294967296 | bytes 25165824 | tf_op jit(solution)/shard_map/pallas_call | solution.py:139
  111.8 4.4 %collective-permute-done.29 = bf16[8,4,128,256]{3,2,1,0:T(8,128)(2,1)S(1)} collective-permute-done((bf16[8,4,128,256]{3,2,1,0:T(8,128)(2,1)}, bf16[8,4,128,256]{3,2,1,0:T(8,128)(2,1)S(1)}, u32[]{:S(2)}, u32[]{:S(2)}) %collective-permute-start.29) | collective-permute-done | bytes 2097184 | tf_op jit(solution)/shard_map/ppermute | solution.py:25
  116.1 1.6 fusion.10
  117.7 7.1 %collective-permute-start.35 = (bf16[4,128,256]{2,1,0:T(8,128)(2,1)}, bf16[4,128,256]{2,1,0:T(8,128)(2,1)}, u32[]{:S(2)}, u32[]{:S(2)}) collective-permute-start(bf16[4,128,256]{2,1,0:T(8,128)(2,1)} %get-tuple-element.30), channel_id=1, source_target_pairs={{0,64},{8,72},{16,80},{24,88},{32,96},{40,104},{48,112},{56,120},{... | collective-permute-start | bytes 786440 | tf_op jit(solution)/shard_map/ppermute | solution.py:25
  124.8 0.3 all_to_all.13
  125.1 22.9 %all_to_all.16 = f32[128,1,512]{2,1,0:T(1,128)S(1)} all-to-all(f32[128,1,512]{2,1,0:T(1,128)S(1)} %all_to_all.13), channel_id=1, replica_groups=mesh['row'=16,'col'=8] {'row','col'}, dimensions={0} | all-to-all | bytes 524288 | tf_op jit(solution)/shard_map/all_to_all | solution.py:236
  148.0 0.2 reduce_sum.129
  148.2 0.7 collective-permute-start.30
  148.9 1.9 %collective-permute-start.32 = (bf16[4,128,256]{2,1,0:T(8,128)(2,1)S(1)}, bf16[4,128,256]{2,1,0:T(8,128)(2,1)}, u32[]{:S(2)}, u32[]{:S(2)}) collective-permute-start(bf16[4,128,256]{2,1,0:T(8,128)(2,1)S(1)} %get-tuple-element.33), channel_id=1, source_target_pairs={{0,64},{8,72},{16,80},{24,88},{32,96},{40,104},{48,112},{56,120},{... | collective-permute-start | bytes 786440 | tf_op jit(solution)/shard_map/ppermute | solution.py:25
  150.8 2.1 %collective-permute-start.31 = (bf16[4,128,256]{2,1,0:T(8,128)(2,1)S(1)}, bf16[4,128,256]{2,1,0:T(8,128)(2,1)}, u32[]{:S(2)}, u32[]{:S(2)}) collective-permute-start(bf16[4,128,256]{2,1,0:T(8,128)(2,1)S(1)} %get-tuple-element.34), channel_id=1, source_target_pairs={{0,96},{8,104},{16,112},{24,120},{32,64},{40,72},{48,80},{56,88},{... | collective-permute-start | bytes 786440 | tf_op jit(solution)/shard_map/ppermute | solution.py:25
  153.0 2.1 %fusion.4 = bf16[4,128,256]{2,1,0:T(8,128)(2,1)} fusion(bf16[4,128,256]{2,1,0:T(8,128)(2,1)} %collective-permute-done.35, bf16[4,128,256]{2,1,0:T(8,128)(2,1)} %collective-permute-done.34, bf16[4,128,256]{2,1,0:T(8,128)(2,1)} %collective-permute-done.33, bf16[8,4,128,256]{3,2,1,0:T(8,128)(2,1)} %copy-done.4, bf16[8,4,128,256]{3,2,1,0:T(8,128)(2,1)S(1)} %get-tuple-element.26), kind=kLoop, calls=%fused_computation.12 | loop fusion | flops 1572864 | bytes 1572864 | tf_op jit(solution)/shard_map/convert_element_type | solution.py:254
  155.0 0.9 collective-permute-start.36
  155.9 0.1 broadcast_in_dim.135
  156.1 16.0 %all_to_all.17 = f32[128,1,512]{2,1,0:T(1,128)S(1)} all-to-all(f32[128,1,512]{2,1,0:T(1,128)S(1)} %broadcast_in_dim.135), channel_id=1, replica_groups=mesh['row'=16,'col'=8] {'row','col'}, dimensions={0} | all-to-all | bytes 524288 | tf_op jit(solution)/shard_map/all_to_all | solution.py:242
  172.1 0.6 reduce.1
  172.7 0.7 reshape.241
  173.5 2.2 %fusion.8 = bf16[4,128,256]{2,1,0:T(8,128)(2,1)} fusion(bf16[4,128,256]{2,1,0:T(8,128)(2,1)} %collective-permute-done.36, bf16[4,128,256]{2,1,0:T(8,128)(2,1)} %collective-permute-done.32, bf16[4,128,256]{2,1,0:T(8,128)(2,1)} %collective-permute-done.31, bf16[4,128,256]{2,1,0:T(8,128)(2,1)} %collective-permute-done.30, ...), kind=kLoop, calls=%fused_computation.17 | loop fusion | flops 1835008 | bytes 1835008 | tf_op jit(solution)/shard_map/convert_element_type | solution.py:256
  (66 shorter events, 2.0 us)
Async XLA Ops:
  0.6 17.5 %collective-permute-start.7 = (bf16[4,128,256]{2,1,0:T(8,128)(2,1)}, bf16[4,128,256]{2,1,0:T(8,128)(2,1)S(1)}, u32[]{:S(2)}, u32[]{:S(2)}) collective-permute-start(bf16[4,128,256]{2,1,0:T(8,128)(2,1)} %bitcast.32), channel_id=1, source_target_pairs={{0,8},{8,0},{16,24},{24,16},{32,40},{40,32},{48,56},{56,48},{64,72... | collective-permute-start | bytes 786440 | tf_op jit(solution)/shard_map/ppermute | solution.py:25
  0.7 18.0 %collective-permute-start.5 = (bf16[4,128,256]{2,1,0:T(8,128)(2,1)}, bf16[4,128,256]{2,1,0:T(8,128)(2,1)S(1)}, u32[]{:S(2)}, u32[]{:S(2)}) collective-permute-start(bf16[4,128,256]{2,1,0:T(8,128)(2,1)} %bitcast.33), channel_id=1, source_target_pairs={{0,96},{8,104},{16,112},{24,120},{32,64},{40,72},{48,80},{56,88},{... | collective-permute-start | bytes 786440 | tf_op jit(solution)/shard_map/ppermute | solution.py:25
  3.8 15.4 %collective-permute-start.3 = (bf16[4,128,256]{2,1,0:T(8,128)(2,1)}, bf16[4,128,256]{2,1,0:T(8,128)(2,1)S(1)}, u32[]{:S(2)}, u32[]{:S(2)}) collective-permute-start(bf16[4,128,256]{2,1,0:T(8,128)(2,1)} %bitcast.34), channel_id=1, source_target_pairs={{0,64},{8,72},{16,80},{24,88},{32,96},{40,104},{48,112},{56,120},{... | collective-permute-start | bytes 786440 | tf_op jit(solution)/shard_map/ppermute | solution.py:25
  4.4 14.8 %collective-permute-start.1 = (bf16[4,128,256]{2,1,0:T(8,128)(2,1)}, bf16[4,128,256]{2,1,0:T(8,128)(2,1)S(1)}, u32[]{:S(2)}, u32[]{:S(2)}) collective-permute-start(bf16[4,128,256]{2,1,0:T(8,128)(2,1)} %bitcast.35), channel_id=1, source_target_pairs={{0,32},{8,40},{16,48},{24,56},{32,0},{40,8},{48,16},{56,24},{64,96... | collective-permute-start | bytes 786440 | tf_op jit(solution)/shard_map/ppermute | solution.py:25
  4.9 10.2 %collective-permute-start = (bf16[4,128,256]{2,1,0:T(8,128)(2,1)}, bf16[4,128,256]{2,1,0:T(8,128)(2,1)S(1)}, u32[]{:S(2)}, u32[]{:S(2)}) collective-permute-start(bf16[4,128,256]{2,1,0:T(8,128)(2,1)} %bitcast.36), channel_id=1, source_target_pairs={{0,16},{8,24},{16,0},{24,8},{32,48},{40,56},{48,32},{56,40},{64,80... | collective-permute-start | bytes 786440 | tf_op jit(solution)/shard_map/ppermute | solution.py:25
  15.1 14.1 %collective-permute-start.6 = (bf16[4,128,256]{2,1,0:T(8,128)(2,1)S(1)}, bf16[4,128,256]{2,1,0:T(8,128)(2,1)S(1)}, u32[]{:S(2)}, u32[]{:S(2)}) collective-permute-start(bf16[4,128,256]{2,1,0:T(8,128)(2,1)S(1)} %collective-permute-done.refs_3_), channel_id=1, source_target_pairs={{0,96},{8,104},{16,112},{24,120},{32,64},{40,72},{48,80},{56,88},{... | collective-permute-start | bytes 786440 | tf_op jit(solution)/shard_map/ppermute | solution.py:25
  18.1 11.1 %collective-permute-start.4 = (bf16[4,128,256]{2,1,0:T(8,128)(2,1)S(1)}, bf16[4,128,256]{2,1,0:T(8,128)(2,1)S(1)}, u32[]{:S(2)}, u32[]{:S(2)}) collective-permute-start(bf16[4,128,256]{2,1,0:T(8,128)(2,1)S(1)} %collective-permute-done.refs_3_), channel_id=1, source_target_pairs={{0,64},{8,72},{16,80},{24,88},{32,96},{40,104},{48,112},{56,120},{... | collective-permute-start | bytes 786440 | tf_op jit(solution)/shard_map/ppermute | solution.py:25
  18.7 11.1 %collective-permute-start.2 = (bf16[4,128,256]{2,1,0:T(8,128)(2,1)S(1)}, bf16[4,128,256]{2,1,0:T(8,128)(2,1)S(1)}, u32[]{:S(2)}, u32[]{:S(2)}) collective-permute-start(bf16[4,128,256]{2,1,0:T(8,128)(2,1)S(1)} %collective-permute-done.refs_3_), channel_id=1, source_target_pairs={{0,32},{8,40},{16,48},{24,56},{32,0},{40,8},{48,16},{56,24},{64,96... | collective-permute-start | bytes 786440 | tf_op jit(solution)/shard_map/ppermute | solution.py:25
  19.2 1.5 collective-permute-start.13
  19.2 1.9 %collective-permute-start.11 = (bf16[4,128,256]{2,1,0:T(8,128)(2,1)S(1)}, bf16[4,128,256]{2,1,0:T(8,128)(2,1)S(1)}, u32[]{:S(2)}, u32[]{:S(2)}) collective-permute-start(bf16[4,128,256]{2,1,0:T(8,128)(2,1)S(1)} %collective-permute-done.3.refs_6_), channel_id=1, source_target_pairs={{0,8},{8,0},{16,24},{24,16},{32,40},{40,32},{48,56},{56,48},{64,72... | collective-permute-start | bytes 786440 | tf_op jit(solution)/shard_map/ppermute | solution.py:25
  20.8 10.5 %collective-permute-start.8 = (bf16[4,128,256]{2,1,0:T(8,128)(2,1)S(1)}, bf16[4,128,256]{2,1,0:T(8,128)(2,1)S(1)}, u32[]{:S(2)}, u32[]{:S(2)}) collective-permute-start(bf16[4,128,256]{2,1,0:T(8,128)(2,1)S(1)} %collective-permute-done.refs_3_), channel_id=1, source_target_pairs={{0,8},{8,0},{16,24},{24,16},{32,40},{40,32},{48,56},{56,48},{64,72... | collective-permute-start | bytes 786440 | tf_op jit(solution)/shard_map/ppermute | solution.py:25
  21.1 10.1 %collective-permute-start.9 = (bf16[4,128,256]{2,1,0:T(8,128)(2,1)S(1)}, bf16[4,128,256]{2,1,0:T(8,128)(2,1)S(1)}, u32[]{:S(2)}, u32[]{:S(2)}) collective-permute-start(bf16[4,128,256]{2,1,0:T(8,128)(2,1)S(1)} %collective-permute-done.1.refs_4_), channel_id=1, source_target_pairs={{0,8},{8,0},{16,24},{24,16},{32,40},{40,32},{48,56},{56,48},{64,72... | collective-permute-start | bytes 786440 | tf_op jit(solution)/shard_map/ppermute | solution.py:25
  29.2 2.1 %collective-permute-start.14 = (bf16[4,128,256]{2,1,0:T(8,128)(2,1)S(1)}, bf16[4,128,256]{2,1,0:T(8,128)(2,1)S(1)}, u32[]{:S(2)}, u32[]{:S(2)}) collective-permute-start(bf16[4,128,256]{2,1,0:T(8,128)(2,1)S(1)} %collective-permute-done.6.refs_9_), channel_id=1, source_target_pairs={{0,8},{8,0},{16,24},{24,16},{32,40},{40,32},{48,56},{56,48},{64,72... | collective-permute-start | bytes 786440 | tf_op jit(solution)/shard_map/ppermute | solution.py:25
  29.2 2.1 %collective-permute-start.12 = (bf16[4,128,256]{2,1,0:T(8,128)(2,1)S(1)}, bf16[4,128,256]{2,1,0:T(8,128)(2,1)S(1)}, u32[]{:S(2)}, u32[]{:S(2)}) collective-permute-start(bf16[4,128,256]{2,1,0:T(8,128)(2,1)S(1)} %collective-permute-done.4.refs_7_), channel_id=1, source_target_pairs={{0,8},{8,0},{16,24},{24,16},{32,40},{40,32},{48,56},{56,48},{64,72... | collective-permute-start | bytes 786440 | tf_op jit(solution)/shard_map/ppermute | solution.py:25
  29.8 1.7 collective-permute-start.10
  31.3 0.7 copy-start.5
  32.0 0.9 copy-start
  32.9 35.2 %copy-start.1 = (bf16[512,256]{1,0:T(8,128)(2,1)S(1)}, bf16[512,256]{1,0:T(8,128)(2,1)}, u32[]{:S(2)}) copy-start(bf16[512,256]{1,0:T(8,128)(2,1)} %cotangent.1) | copy-start | bytes 786436
  32.9 35.2 %copy-start.2 = (bf16[256,256]{1,0:T(8,128)(2,1)S(1)}, bf16[256,256]{1,0:T(8,128)(2,1)}, u32[]{:S(2)}) copy-start(bf16[256,256]{1,0:T(8,128)(2,1)} %weight.1) | copy-start | bytes 393220
  32.9 35.2 %copy-start.3 = (f32[256]{0:T(256)S(1)}, f32[256]{0:T(256)}, u32[]{:S(2)}) copy-start(f32[256]{0:T(256)} %param.10) | copy-start | bytes 3076
  42.1 9.2 %collective-permute-start.18 = (bf16[4,128,256]{2,1,0:T(8,128)(2,1)S(1)}, bf16[4,128,256]{2,1,0:T(8,128)(2,1)S(1)}, u32[]{:S(2)}, u32[]{:S(2)}) collective-permute-start(bf16[4,128,256]{2,1,0:T(8,128)(2,1)S(1)} %get-tuple-element.21), channel_id=1, source_target_pairs={{0,1},{1,0},{2,3},{3,2},{4,5},{5,4},{6,7},{7,6},{8,9},{9,8},{10,11... | collective-permute-start | bytes 786440 | tf_op jit(solution)/shard_map/ppermute | solution.py:29
  42.2 13.9 %collective-permute-start.19 = (bf16[4,128,256]{2,1,0:T(8,128)(2,1)S(1)}, bf16[4,128,256]{2,1,0:T(8,128)(2,1)S(1)}, u32[]{:S(2)}, u32[]{:S(2)}) collective-permute-start(bf16[4,128,256]{2,1,0:T(8,128)(2,1)S(1)} %get-tuple-element.22), channel_id=1, source_target_pairs={{0,3},{1,2},{2,1},{3,0},{4,7},{5,6},{6,5},{7,4},{8,11},{9,10},{10,... | collective-permute-start | bytes 786440 | tf_op jit(solution)/shard_map/ppermute | solution.py:29
  43.8 14.3 %collective-permute-start.20 = (bf16[4,128,256]{2,1,0:T(8,128)(2,1)S(1)}, bf16[4,128,256]{2,1,0:T(8,128)(2,1)S(1)}, u32[]{:S(2)}, u32[]{:S(2)}) collective-permute-start(bf16[4,128,256]{2,1,0:T(8,128)(2,1)S(1)} %get-tuple-element.23), channel_id=1, source_target_pairs={{0,2},{1,3},{2,0},{3,1},{4,6},{5,7},{6,4},{7,5},{8,10},{9,11},{10,... | collective-permute-start | bytes 786440 | tf_op jit(solution)/shard_map/ppermute | solution.py:29
  46.3 16.3 %collective-permute-start.15 = (bf16[4,128,256]{2,1,0:T(8,128)(2,1)S(1)}, bf16[4,128,256]{2,1,0:T(8,128)(2,1)S(1)}, u32[]{:S(2)}, u32[]{:S(2)}) collective-permute-start(bf16[4,128,256]{2,1,0:T(8,128)(2,1)S(1)} %get-tuple-element.17), channel_id=1, source_target_pairs={{0,1},{1,0},{2,3},{3,2},{4,5},{5,4},{6,7},{7,6},{8,9},{9,8},{10,11... | collective-permute-start | bytes 786440 | tf_op jit(solution)/shard_map/ppermute | solution.py:29
  46.4 21.7 %collective-permute-start.16 = (bf16[4,128,256]{2,1,0:T(8,128)(2,1)S(1)}, bf16[4,128,256]{2,1,0:T(8,128)(2,1)S(1)}, u32[]{:S(2)}, u32[]{:S(2)}) collective-permute-start(bf16[4,128,256]{2,1,0:T(8,128)(2,1)S(1)} %get-tuple-element.18), channel_id=1, source_target_pairs={{0,3},{1,2},{2,1},{3,0},{4,7},{5,6},{6,5},{7,4},{8,11},{9,10},{10,... | collective-permute-start | bytes 786440 | tf_op jit(solution)/shard_map/ppermute | solution.py:29
  51.4 16.7 %collective-permute-start.17 = (bf16[4,128,256]{2,1,0:T(8,128)(2,1)S(1)}, bf16[4,128,256]{2,1,0:T(8,128)(2,1)S(1)}, u32[]{:S(2)}, u32[]{:S(2)}) collective-permute-start(bf16[4,128,256]{2,1,0:T(8,128)(2,1)S(1)} %get-tuple-element.19), channel_id=1, source_target_pairs={{0,2},{1,3},{2,0},{3,1},{4,6},{5,7},{6,4},{7,5},{8,10},{9,11},{10,... | collective-permute-start | bytes 786440 | tf_op jit(solution)/shard_map/ppermute | solution.py:29
  58.2 9.9 %collective-permute-start.21 = (bf16[4,128,256]{2,1,0:T(8,128)(2,1)S(1)}, bf16[4,128,256]{2,1,0:T(8,128)(2,1)S(1)}, u32[]{:S(2)}, u32[]{:S(2)}) collective-permute-start(bf16[4,128,256]{2,1,0:T(8,128)(2,1)S(1)} %add_convert_fusion.8), channel_id=1, source_target_pairs={{0,4},{1,5},{2,6},{3,7},{4,0},{5,1},{6,2},{7,3},{8,12},{9,13},{10,... | collective-permute-start | bytes 786440 | tf_op jit(solution)/shard_map/ppermute | solution.py:29
  69.2 8.1 %collective-permute-start.25 = (bf16[4,128,256]{2,1,0:T(8,128)(2,1)S(1)}, bf16[4,128,256]{2,1,0:T(8,128)(2,1)S(1)}, u32[]{:S(2)}, u32[]{:S(2)}) collective-permute-start(bf16[4,128,256]{2,1,0:T(8,128)(2,1)S(1)} %get-tuple-element.25.refs_2_), channel_id=1, source_target_pairs={{0,4},{1,5},{2,6},{3,7},{4,0},{5,1},{6,2},{7,3},{8,12},{9,13},{10,... | collective-permute-start | bytes 786440 | tf_op jit(solution)/shard_map/ppermute | solution.py:29
  69.5 14.8 %collective-permute-start.24 = (bf16[4,128,256]{2,1,0:T(8,128)(2,1)S(1)}, bf16[4,128,256]{2,1,0:T(8,128)(2,1)S(1)}, u32[]{:S(2)}, u32[]{:S(2)}) collective-permute-start(bf16[4,128,256]{2,1,0:T(8,128)(2,1)S(1)} %get-tuple-element.25.refs_2_), channel_id=1, source_target_pairs={{0,3},{1,2},{2,1},{3,0},{4,7},{5,6},{6,5},{7,4},{8,11},{9,10},{10,... | collective-permute-start | bytes 786440 | tf_op jit(solution)/shard_map/ppermute | solution.py:29
  71.0 17.9 %collective-permute-start.23 = (bf16[4,128,256]{2,1,0:T(8,128)(2,1)S(1)}, bf16[4,128,256]{2,1,0:T(8,128)(2,1)S(1)}, u32[]{:S(2)}, u32[]{:S(2)}) collective-permute-start(bf16[4,128,256]{2,1,0:T(8,128)(2,1)S(1)} %get-tuple-element.25.refs_2_), channel_id=1, source_target_pairs={{0,2},{1,3},{2,0},{3,1},{4,6},{5,7},{6,4},{7,5},{8,10},{9,11},{10,... | collective-permute-start | bytes 786440 | tf_op jit(solution)/shard_map/ppermute | solution.py:29
  73.8 15.1 %collective-permute-start.22 = (bf16[4,128,256]{2,1,0:T(8,128)(2,1)S(1)}, bf16[4,128,256]{2,1,0:T(8,128)(2,1)S(1)}, u32[]{:S(2)}, u32[]{:S(2)}) collective-permute-start(bf16[4,128,256]{2,1,0:T(8,128)(2,1)S(1)} %get-tuple-element.25.refs_2_), channel_id=1, source_target_pairs={{0,1},{1,0},{2,3},{3,2},{4,5},{5,4},{6,7},{7,6},{8,9},{9,8},{10,11... | collective-permute-start | bytes 786440 | tf_op jit(solution)/shard_map/ppermute | solution.py:29
  77.3 17.2 %collective-permute-start.28 = (bf16[4,128,256]{2,1,0:T(8,128)(2,1)S(1)}, bf16[4,128,256]{2,1,0:T(8,128)(2,1)S(1)}, u32[]{:S(2)}, u32[]{:S(2)}) collective-permute-start(bf16[4,128,256]{2,1,0:T(8,128)(2,1)S(1)} %collective-permute-done.25.refs_6_), channel_id=1, source_target_pairs={{0,3},{1,2},{2,1},{3,0},{4,7},{5,6},{6,5},{7,4},{8,11},{9,10},{10,... | collective-permute-start | bytes 786440 | tf_op jit(solution)/shard_map/ppermute | solution.py:29
  78.8 15.7 %collective-permute-start.27 = (bf16[4,128,256]{2,1,0:T(8,128)(2,1)S(1)}, bf16[4,128,256]{2,1,0:T(8,128)(2,1)S(1)}, u32[]{:S(2)}, u32[]{:S(2)}) collective-permute-start(bf16[4,128,256]{2,1,0:T(8,128)(2,1)S(1)} %collective-permute-done.25.refs_6_), channel_id=1, source_target_pairs={{0,2},{1,3},{2,0},{3,1},{4,6},{5,7},{6,4},{7,5},{8,10},{9,11},{10,... | collective-permute-start | bytes 786440 | tf_op jit(solution)/shard_map/ppermute | solution.py:29
  84.3 13.0 %collective-permute-start.26 = (bf16[4,128,256]{2,1,0:T(8,128)(2,1)S(1)}, bf16[4,128,256]{2,1,0:T(8,128)(2,1)S(1)}, u32[]{:S(2)}, u32[]{:S(2)}) collective-permute-start(bf16[4,128,256]{2,1,0:T(8,128)(2,1)S(1)} %collective-permute-done.25.refs_6_), channel_id=1, source_target_pairs={{0,1},{1,0},{2,3},{3,2},{4,5},{5,4},{6,7},{7,6},{8,9},{9,8},{10,11... | collective-permute-start | bytes 786440 | tf_op jit(solution)/shard_map/ppermute | solution.py:29
  111.7 4.5 %collective-permute-start.29 = (bf16[8,4,128,256]{3,2,1,0:T(8,128)(2,1)}, bf16[8,4,128,256]{3,2,1,0:T(8,128)(2,1)S(1)}, u32[]{:S(2)}, u32[]{:S(2)}) collective-permute-start(bf16[8,4,128,256]{3,2,1,0:T(8,128)(2,1)} %get-tuple-element.27), channel_id=1, source_target_pairs={{0,8},{8,0},{16,24},{24,16},{32,40},{40,32},{48,56},{56,48},{64,72... | collective-permute-start | bytes 6291464 | tf_op jit(solution)/shard_map/ppermute | solution.py:25
  116.1 1.6 copy-start.4
  117.7 33.1 %collective-permute-start.35 = (bf16[4,128,256]{2,1,0:T(8,128)(2,1)}, bf16[4,128,256]{2,1,0:T(8,128)(2,1)}, u32[]{:S(2)}, u32[]{:S(2)}) collective-permute-start(bf16[4,128,256]{2,1,0:T(8,128)(2,1)} %get-tuple-element.30), channel_id=1, source_target_pairs={{0,64},{8,72},{16,80},{24,88},{32,96},{40,104},{48,112},{56,120},{... | collective-permute-start | bytes 786440 | tf_op jit(solution)/shard_map/ppermute | solution.py:25
  124.8 28.2 %collective-permute-start.34 = (bf16[4,128,256]{2,1,0:T(8,128)(2,1)}, bf16[4,128,256]{2,1,0:T(8,128)(2,1)}, u32[]{:S(2)}, u32[]{:S(2)}) collective-permute-start(bf16[4,128,256]{2,1,0:T(8,128)(2,1)} %get-tuple-element.31), channel_id=1, source_target_pairs={{0,96},{8,104},{16,112},{24,120},{32,64},{40,72},{48,80},{56,88},{... | collective-permute-start | bytes 786440 | tf_op jit(solution)/shard_map/ppermute | solution.py:25
  124.8 28.2 %collective-permute-start.33 = (bf16[4,128,256]{2,1,0:T(8,128)(2,1)}, bf16[4,128,256]{2,1,0:T(8,128)(2,1)}, u32[]{:S(2)}, u32[]{:S(2)}) collective-permute-start(bf16[4,128,256]{2,1,0:T(8,128)(2,1)} %get-tuple-element.32), channel_id=1, source_target_pairs={{0,32},{8,40},{16,48},{24,56},{32,0},{40,8},{48,16},{56,24},{64,96... | collective-permute-start | bytes 786440 | tf_op jit(solution)/shard_map/ppermute | solution.py:25
  148.2 25.2 %collective-permute-start.30 = (bf16[4,128,256]{2,1,0:T(8,128)(2,1)S(1)}, bf16[4,128,256]{2,1,0:T(8,128)(2,1)}, u32[]{:S(2)}, u32[]{:S(2)}) collective-permute-start(bf16[4,128,256]{2,1,0:T(8,128)(2,1)S(1)} %get-tuple-element.29), channel_id=1, source_target_pairs={{0,32},{8,40},{16,48},{24,56},{32,0},{40,8},{48,16},{56,24},{64,96... | collective-permute-start | bytes 786440 | tf_op jit(solution)/shard_map/ppermute | solution.py:25
  148.9 24.5 %collective-permute-start.32 = (bf16[4,128,256]{2,1,0:T(8,128)(2,1)S(1)}, bf16[4,128,256]{2,1,0:T(8,128)(2,1)}, u32[]{:S(2)}, u32[]{:S(2)}) collective-permute-start(bf16[4,128,256]{2,1,0:T(8,128)(2,1)S(1)} %get-tuple-element.33), channel_id=1, source_target_pairs={{0,64},{8,72},{16,80},{24,88},{32,96},{40,104},{48,112},{56,120},{... | collective-permute-start | bytes 786440 | tf_op jit(solution)/shard_map/ppermute | solution.py:25
  150.8 22.6 %collective-permute-start.31 = (bf16[4,128,256]{2,1,0:T(8,128)(2,1)S(1)}, bf16[4,128,256]{2,1,0:T(8,128)(2,1)}, u32[]{:S(2)}, u32[]{:S(2)}) collective-permute-start(bf16[4,128,256]{2,1,0:T(8,128)(2,1)S(1)} %get-tuple-element.34), channel_id=1, source_target_pairs={{0,96},{8,104},{16,112},{24,120},{32,64},{40,72},{48,80},{56,88},{... | collective-permute-start | bytes 786440 | tf_op jit(solution)/shard_map/ppermute | solution.py:25
  155.0 18.4 %collective-permute-start.36 = (bf16[4,128,256]{2,1,0:T(8,128)(2,1)}, bf16[4,128,256]{2,1,0:T(8,128)(2,1)}, u32[]{:S(2)}, u32[]{:S(2)}) collective-permute-start(bf16[4,128,256]{2,1,0:T(8,128)(2,1)} %fusion.4), channel_id=1, source_target_pairs={{0,16},{8,24},{16,0},{24,8},{32,48},{40,56},{48,32},{56,40},{64,80... | collective-permute-start | bytes 786440 | tf_op jit(solution)/shard_map/ppermute | solution.py:25

commit v2 on v1

--- a/solution.py
+++ b/solution.py
@@ -49,7 +49,7 @@
     entries = jnp.sum(jnp.where(hit, entry[None, :], 0), axis=1) + source_total
     first = jnp.arange(position_total // group, dtype=jnp.int32) * group
     group_targets = jnp.sum((ends[None, :] <= first[:, None]).astype(jnp.int32), axis=1)
-    chunks = (ends[-1:] + chunk - 1) // chunk
+    chunks = (jnp.sum(padded, keepdims=True) + chunk - 1) // chunk
     return jnp.concatenate([entries, group_targets, chunks])
 
 
@@ -131,7 +131,7 @@
         done += count
 
 
-def spmm(plan, blocks, pieces, target_total, position_total, out_shapes, transposed):
+def spmm(plan, blocks, pieces, target_total, position_total, out_shapes, transposed, grant):
     piece_total = len(pieces)
     source_total = 4 * piece_total
     width = pieces[0].shape[-1]
@@ -150,7 +150,7 @@
             pltpu.SemaphoreType.DMA((buffers,)),
             pltpu.SemaphoreType.DMA((piece_total,)),
         ],
-        compiler_params=pltpu.CompilerParams(vmem_limit_bytes=48 << 20),
+        compiler_params=pltpu.CompilerParams(vmem_limit_bytes=grant << 20),
         cost_estimate=pl.CostEstimate(
             flops=2 * 512 * 128 * 128 * width, bytes_accessed=24 << 20, transcendentals=0
         ),
@@ -182,6 +182,54 @@
     return sums
 
 
+def together(*values):
+    return lax.optimization_barrier(values)
+
+
+def gather_near(own, swap, follow=(), state=None):
+    two, beside = swap(own, 2, 0), swap(own, 0, 1)
+    if follow:
+        own, two, beside, state = together(own, two, beside, follow[0](state))
+    one, three = swap(own, 1, 0), swap(own, 3, 0)
+    second = [swap(beside, 1, 0), swap(beside, 3, 0), swap(two, 0, 1)]
+    if follow:
+        *second, one, three, state = together(*second, one, three, follow[1](state))
+    return [[own, one, two, three], [beside, second[0], second[2], second[1]]], state
+
+
+def scatter_near(parts, swap, follow=(), state=None):
+    here, there = parts
+    opposite = swap(there[2], 0, 1)
+    edges = [swap(there[ring], ring, 0) for ring in (1, 3)]
+    if follow:
+        state = follow[0](state)
+    side = add_up(there[0], *edges).astype(bf16)
+    corner = add_up(here[2], opposite).astype(bf16)
+    one, three = here[1], here[3]
+    if follow:
+        side, corner, one, three, state = together(side, corner, one, three, state)
+    near = [swap(one, 1, 0), swap(three, 3, 0)]
+    beside, far = swap(side, 0, 1), swap(corner, 2, 0)
+    if follow:
+        state = follow[1](state)
+    return [here[0], *near, beside, far], state
+
+
+def ring_sum(value, swaps):
+    rounded = value.astype(bf16)
+    one, two, three = [swap(rounded).astype(f32) for swap in swaps]
+    return (rounded.astype(f32) + one) + (two + three)
+
+
+def all_swap(value, row_mask, col_mask):
+    pairs = [(index, index ^ (8 * row_mask + col_mask)) for index in range(128)]
+    return lax.ppermute(value, ("row", "col"), pairs)
+
+
+def cut(array, part, count):
+    return lax.dynamic_slice_in_dim(array, part * count, count, 0)
+
+
 def per_device(
     features_in, weight, bias_vector, cotangent, adjacency, block_rows, block_cols, counts
 ):
@@ -202,18 +250,14 @@
     backward_plan = slot_plan(col_place, row_place, live, 64, 32, slot_total + 192)
 
     own = features_in.reshape(piece)
-    beside = row_swap(own, 2)
-    near = [own, beside]
-    for y in (1, 3, 2):
-        near += [row_swap(own, 4 * y), row_swap(beside, 4 * y)]
-    near = near[:2] + near[2:4] + near[6:8] + near[4:6]
+    near, _ = gather_near(own, lambda value, ring, z: row_swap(value, 4 * ring + 2 * z))
+    near = [near[z][ring] for ring in range(4) for z in range(2)]
     gathered = near + [row_swap(part, 1) for part in near]
 
-    parts = spmm(forward_plan, blocks, gathered, 32, slot_total + 96, [piece] * 8, False)
-    across = [col_swap(parts[4 + x], x) for x in (1, 3, 2)]
-    here = [col_swap(parts[x], x) for x in (1, 3, 2)]
-    across_sum = add_up(parts[4], *across).astype(bf16)
-    from_across = col_swap(across_sum, 4)
+    parts = spmm(forward_plan, blocks, gathered, 32, slot_total + 96, [piece] * 8, False, 48)
+    terms, _ = scatter_near(
+        [parts[:4], parts[4:]], lambda value, ring, z: col_swap(value, ring + 4 * z)
+    )
 
     output, sent, weight_grad = pl.pallas_call(
         node_kernel,
@@ -223,37 +267,49 @@
             jax.ShapeDtypeStruct((width, width), f32),
         ],
         compiler_params=pltpu.CompilerParams(vmem_limit_bytes=32 << 20),
-    )(parts[0], *here, from_across, weight, bias_vector[None, :], cotangent)
-
-    beside = col_swap(sent, 4)
-    x_order = (1, 3, 2)
-    from_here = {x: col_swap(sent, x) for x in x_order}
-    from_there = {x: col_swap(beside, x) for x in x_order}
-    spread = [sent] + [from_here[x] for x in (1, 2, 3)]
-    spread += [beside] + [from_there[x] for x in (1, 2, 3)]
-
-    device_total = 128
-    scatter = lax.all_to_all(
-        weight_grad.reshape(device_total, -1), ("row", "col"), 0, 0, tiled=True
-    )
-    scattered = jnp.sum(scatter, axis=0, keepdims=True) * (
-        1.0 / math.sqrt(node_dev * device_total)
-    )
-    grad_w = lax.all_to_all(
-        jnp.broadcast_to(scattered, scatter.shape), ("row", "col"), 0, 0, tiled=True
-    ).reshape(width, width)
-
-    halves = spmm(
-        backward_plan, blocks, spread, 64, slot_total + 192, [(8,) + piece] * 2, True
-    )
-    mine, theirs = halves
-    swapped = row_swap(theirs, 1)
+    )(*terms, weight, bias_vector[None, :], cotangent)
+
+    core = row_index & 1
+    count = width // 2
+    spread, half = gather_near(
+        sent,
+        lambda value, ring, z: col_swap(value, ring + 4 * z),
+        (
+            lambda full: cut(full, core, count) + row_swap(cut(full, core ^ 1, count), 1),
+            lambda part: ring_sum(part, [lambda v, k=k: row_swap(v, 4 * k) for k in (1, 2, 3)]),
+        ),
+        weight_grad,
+    )
+
+    mine, theirs = spmm(
+        backward_plan,
+        blocks,
+        spread[0] + spread[1],
+        64,
+        slot_total + 192,
+        [(8,) + piece] * 2,
+        True,
+        42,
+    )
+    half = ring_sum(
+        half, [lambda v, m=m: all_swap(v, *m) for m in ((2, 0), (0, 4), (2, 4))]
+    )
+    swapped, half = together(row_swap(theirs, 1), half)
     summed = [add_up(mine[index], swapped[index]).astype(bf16) for index in range(8)]
-    across = [row_swap(summed[2 * y + 1], 4 * y) for y in (1, 3, 2)]
-    here = [row_swap(summed[2 * y], 4 * y) for y in (1, 3, 2)]
-    across_sum = add_up(summed[1], *across).astype(bf16)
-    from_across = row_swap(across_sum, 2)
-    grad_x = add_up(summed[0], *here, from_across).astype(bf16).reshape(node_dev, width)
+    terms, other = scatter_near(
+        [summed[0::2], summed[1::2]],
+        lambda value, ring, z: row_swap(value, 4 * ring + 2 * z),
+        (
+            lambda part: ring_sum(part, [lambda v, k=k: col_swap(v, k) for k in (1, 2, 3)]),
+            lambda part: (part, row_swap(part, 1)),
+        ),
+        half,
+    )
+    half, other = [part * (1.0 / math.sqrt(node_dev * 128)) for part in other]
+    grad_w = jnp.concatenate(
+        [jnp.where(core == 0, half, other), jnp.where(core == 0, other, half)], axis=0
+    )
+    grad_x = add_up(*terms).astype(bf16).reshape(node_dev, width)
     return (output, grad_x, grad_w)
 
 

time: 178 us -> 156 us (0.88)
  blocking collectives: 38.9 us -> 0 us
  starting transfers between devices: 45.3 us -> 59.9 us
  waiting for transfers between devices: 50.1 us -> 56.4 us
  other arithmetic: 10.1 us -> 8.21 us
    all_to_all x2 -> x0, blocking collectives: 38.9 us -> none  [the longest x1 22.9 us: per_device(): lax.all_to_all(weight_grad.reshape(device_total, -1), ('row', 'col'), 0,...]
    ppermute x23 -> x28, waiting for transfers between devices: 16.7 us -> 25.9 us  [row_swap(): return lax.ppermute(value, 'row', xor_pairs(16, mask))]
    ppermute x14 -> x17, starting transfers between devices: 19 us -> 27.2 us  [col_swap(): return lax.ppermute(value, 'col', xor_pairs(8, mask))]
    ppermute x14 -> x17, waiting for transfers between devices: 33.3 us -> 25.9 us  [col_swap(): return lax.ppermute(value, 'col', xor_pairs(8, mask))]
    ppermute x0 -> x3, starting transfers between devices: none -> 4.76 us  [all_swap(): return lax.ppermute(value, ('row', 'col'), pairs)]
    ppermute x0 -> x3, waiting for transfers between devices: none -> 4.66 us  [all_swap(): return lax.ppermute(value, ('row', 'col'), pairs)]
    convert_element_type x3 -> x4, other arithmetic: 4.37 us -> 2.26 us  [the longest x1 1.85 us: per_device(): grad_x = add_up(*terms).astype(bf16).reshape(node_dev, width)]
    ppermute x23 -> x28, starting transfers between devices: 26.4 us -> 27.9 us  [row_swap(): return lax.ppermute(value, 'row', xor_pairs(16, mask))]
  transfers between devices with their start and end apart: 37 -> 48, of which waited for: 16 -> 21; matrix products, arithmetic and copies ran while one was open for 5% -> 4% of each run, Pallas kernels for 0% -> 0%
where the time goes in v2:
time: 156 us; the launch traced here: 154 us
  starting transfers between devices  59.9 us (38%)
  waiting for transfers between devices  56.4 us (36%)
  Pallas kernels  23.5 us (15%)
  other arithmetic  8.21 us (5%)
  between operations  2.89 us (2%)
  local copies, waits for them, and re-layouts  2.87 us (2%)
    ppermute x28, starting transfers between devices, row_swap(): return lax.ppermute(value, 'row', xor_pairs(16, mask))  27.9 us
    ppermute x17, starting transfers between devices, col_swap(): return lax.ppermute(value, 'col', xor_pairs(8, mask))  27.2 us
    ppermute x28, waiting for transfers between devices, row_swap(): return lax.ppermute(value, 'row', xor_pairs(16, mask))  25.9 us
    ppermute x17, waiting for transfers between devices, col_swap(): return lax.ppermute(value, 'col', xor_pairs(8, mask))  25.9 us
    pallas_call x2, Pallas kernels, spmm(): pl.pallas_call(functools.partial(spmm_kernel, piece_total, position_total...  22.4 us
    ppermute x3, starting transfers between devices, all_swap(): return lax.ppermute(value, ('row', 'col'), pairs)  4.76 us
    ppermute x3, waiting for transfers between devices, all_swap(): return lax.ppermute(value, ('row', 'col'), pairs)  4.66 us
  transfers between devices with their start and end apart: 48, of which 21 were waited for; matrix products, arithmetic and copies ran while one was open for 4% of the time, Pallas kernels for 0%

profile of v2, /device:TPU:2, one launch (start us, length us, event | category | flops | bytes accessed | tf_op | source)
XLA Modules:
  0.0 153.8 jit_solution(15255961792344967882)
XLA Ops:
  0.7 3.1 %collective-permute-start.5 = (bf16[4,128,256]{2,1,0:T(8,128)(2,1)}, bf16[4,128,256]{2,1,0:T(8,128)(2,1)S(1)}, u32[]{:S(2)}, u32[]{:S(2)}) collective-permute-start(bf16[4,128,256]{2,1,0:T(8,128)(2,1)} %bitcast.38), channel_id=1, source_target_pairs={{0,96},{8,104},{16,112},{24,120},{32,64},{40,72},{48,80},{56,88},{... | collective-permute-start | bytes 786440 | tf_op jit(solution)/shard_map/ppermute | solution.py:25
  3.8 0.6 collective-permute-start.3
  4.4 0.5 collective-permute-start.1
  4.9 3.9 %collective-permute-start = (bf16[4,128,256]{2,1,0:T(8,128)(2,1)}, bf16[4,128,256]{2,1,0:T(8,128)(2,1)S(1)}, u32[]{:S(2)}, u32[]{:S(2)}) collective-permute-start(bf16[4,128,256]{2,1,0:T(8,128)(2,1)} %bitcast.41), channel_id=1, source_target_pairs={{0,16},{8,24},{16,0},{24,8},{32,48},{40,56},{48,32},{56,40},{64,80... | collective-permute-start | bytes 786440 | tf_op jit(solution)/shard_map/ppermute | solution.py:25
  9.4 0.7 shift-left_or_fusion
  10.6 0.7 fusion.22
  11.4 0.7 and_or_fusion
  12.6 0.6 fusion.20
  13.3 1.4 collective-permute-done.3.refs_6_
  14.7 3.9 %collective-permute-start.4 = (bf16[4,128,256]{2,1,0:T(8,128)(2,1)S(1)}, bf16[4,128,256]{2,1,0:T(8,128)(2,1)S(1)}, u32[]{:S(2)}, u32[]{:S(2)}) collective-permute-start(bf16[4,128,256]{2,1,0:T(8,128)(2,1)S(1)} %collective-permute-done.3.refs_6_), channel_id=1, source_target_pairs={{0,16},{8,24},{16,0},{24,8},{32,48},{40,56},{48,32},{56,40},{64,80... | collective-permute-start | bytes 786440 | tf_op jit(solution)/shard_map/ppermute | solution.py:25
  18.8 0.4 collective-permute-start.2
  19.4 1.3 collective-permute-done.13.refs_16_
  20.9 0.4 collective-permute-start.9
  21.3 4.3 %collective-permute-done.4.refs_7_ = bf16[4,128,256]{2,1,0:T(8,128)(2,1)S(1)} collective-permute-done((bf16[4,128,256]{2,1,0:T(8,128)(2,1)S(1)}, bf16[4,128,256]{2,1,0:T(8,128)(2,1)S(1)}, u32[]{:S(2)}, u32[]{:S(2)}) %collective-permute-start.4) | collective-permute-done | bytes 262176 | tf_op jit(solution)/shard_map/ppermute | solution.py:25
  25.6 2.7 %collective-permute-done.6.refs_9_ = bf16[4,128,256]{2,1,0:T(8,128)(2,1)S(1)} collective-permute-done((bf16[4,128,256]{2,1,0:T(8,128)(2,1)S(1)}, bf16[4,128,256]{2,1,0:T(8,128)(2,1)S(1)}, u32[]{:S(2)}, u32[]{:S(2)}) %collective-permute-start.6) | collective-permute-done | bytes 262176 | tf_op jit(solution)/shard_map/ppermute | solution.py:25
  28.3 0.5 collective-permute-start.10
  29.9 0.4 collective-permute-done.10.refs_13_
  30.3 0.9 copy-done
  31.3 9.4 %shard_map.103 = (bf16[4,128,256]{2,1,0:T(8,128)(2,1)S(1)}, bf16[4,128,256]{2,1,0:T(8,128)(2,1)}, bf16[4,128,256]{2,1,0:T(8,128)(2,1)S(1)}, bf16[4,128,256]{2,1,...) custom-call(s32[761]{0:T(1024)S(1)} %pad_add_fusion.refs_0_, ...), custom_call_target="tpu_custom_call" | custom-call | flops 4294967296 | bytes 25165824 | tf_op jit(solution)/shard_map/pallas_call | solution.py:139
  40.7 0.9 collective-permute-start.17
  41.6 7.3 %collective-permute-start.18 = (bf16[4,128,256]{2,1,0:T(8,128)(2,1)S(1)}, bf16[4,128,256]{2,1,0:T(8,128)(2,1)S(1)}, u32[]{:S(2)}, u32[]{:S(2)}) collective-permute-start(bf16[4,128,256]{2,1,0:T(8,128)(2,1)S(1)} %get-tuple-element.38), channel_id=1, source_target_pairs={{0,3},{1,2},{2,1},{3,0},{4,7},{5,6},{6,5},{7,4},{8,11},{9,10},{10,... | collective-permute-start | bytes 786440 | tf_op jit(solution)/shard_map/ppermute | solution.py:29
  48.9 0.7 collective-permute-start.15
  49.6 6.5 %collective-permute-done.18 = bf16[4,128,256]{2,1,0:T(8,128)(2,1)S(1)} collective-permute-done((bf16[4,128,256]{2,1,0:T(8,128)(2,1)S(1)}, bf16[4,128,256]{2,1,0:T(8,128)(2,1)S(1)}, u32[]{:S(2)}, u32[]{:S(2)}) %collective-permute-start.18) | collective-permute-done | bytes 262176 | tf_op jit(solution)/shard_map/ppermute | solution.py:29
  56.4 2.8 %collective-permute-start.21 = (bf16[4,128,256]{2,1,0:T(8,128)(2,1)S(1)}, bf16[4,128,256]{2,1,0:T(8,128)(2,1)S(1)}, u32[]{:S(2)}, u32[]{:S(2)}) collective-permute-start(bf16[4,128,256]{2,1,0:T(8,128)(2,1)S(1)} %add_convert_fusion.8), channel_id=1, source_target_pairs={{0,2},{1,3},{2,0},{3,1},{4,6},{5,7},{6,4},{7,5},{8,10},{9,11},{10,... | collective-permute-start | bytes 786440 | tf_op jit(solution)/shard_map/ppermute | solution.py:29
  59.4 5.7 %collective-permute-done.16.p2 = bf16[4,128,256]{2,1,0:T(8,128)(2,1)S(1)} collective-permute-done((bf16[4,128,256]{2,1,0:T(8,128)(2,1)}, bf16[4,128,256]{2,1,0:T(8,128)(2,1)S(1)}, u32[]{:S(2)}, u32[]{:S(2)}) %collective-permute-start.16) | collective-permute-done | bytes 262176 | tf_op jit(solution)/shard_map/ppermute | solution.py:29
  65.1 0.9 copy-done.1
  66.1 0.9 copy-done.3
  67.0 1.1 shard_map.104
  68.2 1.4 collective-permute-start.23
  69.6 2.7 %collective-permute-start.22 = (bf16[4,128,256]{2,1,0:T(8,128)(2,1)S(1)}, bf16[4,128,256]{2,1,0:T(8,128)(2,1)S(1)}, u32[]{:S(2)}, u32[]{:S(2)}) collective-permute-start(bf16[4,128,256]{2,1,0:T(8,128)(2,1)S(1)} %get-tuple-element.44.refs_2_), channel_id=1, source_target_pairs={{0,2},{1,3},{2,0},{3,1},{4,6},{5,7},{6,4},{7,5},{8,10},{9,11},{10,... | collective-permute-start | bytes 786440 | tf_op jit(solution)/shard_map/ppermute | solution.py:29
  72.9 4.0 %collective-permute-done.23.refs_6_ = bf16[4,128,256]{2,1,0:T(8,128)(2,1)S(1)} collective-permute-done((bf16[4,128,256]{2,1,0:T(8,128)(2,1)S(1)}, bf16[4,128,256]{2,1,0:T(8,128)(2,1)S(1)}, u32[]{:S(2)}, u32[]{:S(2)}) %collective-permute-start.23) | collective-permute-done | bytes 262176 | tf_op jit(solution)/shard_map/ppermute | solution.py:29
  76.9 2.5 %collective-permute-done.22.refs_4_ = bf16[4,128,256]{2,1,0:T(8,128)(2,1)S(1)} collective-permute-done((bf16[4,128,256]{2,1,0:T(8,128)(2,1)S(1)}, bf16[4,128,256]{2,1,0:T(8,128)(2,1)S(1)}, u32[]{:S(2)}, u32[]{:S(2)}) %collective-permute-start.22) | collective-permute-done | bytes 262176 | tf_op jit(solution)/shard_map/ppermute | solution.py:29
  79.4 1.2 collective-permute-start.31
  80.7 2.2 %collective-permute-start.30 = (bf16[128,256]{1,0:T(8,128)(2,1)S(1)}, bf16[128,256]{1,0:T(8,128)(2,1)S(1)}, u32[]{:S(2)}, u32[]{:S(2)}) collective-permute-start(bf16[128,256]{1,0:T(8,128)(2,1)S(1)} %dynamic-slice_add_fusion), channel_id=1, source_target_pairs={{0,32},{8,40},{16,48},{24,56},{32,0},{40,8},{48,16},{56,24},{64,96... | collective-permute-start | bytes 196616 | tf_op jit(solution)/shard_map/ppermute | solution.py:25
  82.9 0.6 collective-permute-start.32
  83.6 1.8 %collective-permute-start.29 = (bf16[4,128,256]{2,1,0:T(8,128)(2,1)S(1)}, bf16[4,128,256]{2,1,0:T(8,128)(2,1)S(1)}, u32[]{:S(2)}, u32[]{:S(2)}) collective-permute-start(bf16[4,128,256]{2,1,0:T(8,128)(2,1)S(1)} %get-tuple-element.44.refs_2_), channel_id=1, source_target_pairs={{0,3},{1,2},{2,1},{3,0},{4,7},{5,6},{6,5},{7,4},{8,11},{9,10},{10,... | collective-permute-start | bytes 786440 | tf_op jit(solution)/shard_map/ppermute | solution.py:29
  85.5 2.1 %collective-permute-start.28 = (bf16[4,128,256]{2,1,0:T(8,128)(2,1)S(1)}, bf16[4,128,256]{2,1,0:T(8,128)(2,1)S(1)}, u32[]{:S(2)}, u32[]{:S(2)}) collective-permute-start(bf16[4,128,256]{2,1,0:T(8,128)(2,1)S(1)} %get-tuple-element.44.refs_2_), channel_id=1, source_target_pairs={{0,1},{1,0},{2,3},{3,2},{4,5},{5,4},{6,7},{7,6},{8,9},{9,8},{10,11... | collective-permute-start | bytes 786440 | tf_op jit(solution)/shard_map/ppermute | solution.py:29
  87.6 1.0 collective-permute-start.26
  88.5 0.6 collective-permute-start.25
  89.1 1.4 collective-permute-start.27
  90.7 4.8 %collective-permute-done.27.refs_8_ = bf16[4,128,256]{2,1,0:T(8,128)(2,1)S(1)} collective-permute-done((bf16[4,128,256]{2,1,0:T(8,128)(2,1)S(1)}, bf16[4,128,256]{2,1,0:T(8,128)(2,1)S(1)}, u32[]{:S(2)}, u32[]{:S(2)}) %collective-permute-start.27) | collective-permute-done | bytes 262176 | tf_op jit(solution)/shard_map/ppermute | solution.py:29
  95.5 0.5 collective-permute-done.26.refs_9_
  96.0 1.8 %collective-permute-done.25.refs_7_ = bf16[4,128,256]{2,1,0:T(8,128)(2,1)S(1)} collective-permute-done((bf16[4,128,256]{2,1,0:T(8,128)(2,1)S(1)}, bf16[4,128,256]{2,1,0:T(8,128)(2,1)S(1)}, u32[]{:S(2)}, u32[]{:S(2)}) %collective-permute-start.25) | collective-permute-done | bytes 262176 | tf_op jit(solution)/shard_map/ppermute | solution.py:29
  97.8 13.0 %shard_map.105 = (bf16[8,4,128,256]{3,2,1,0:T(8,128)(2,1)S(1)}, bf16[8,4,128,256]{3,2,1,0:T(8,128)(2,1)S(1)}) custom-call(s32[881]{0:T(1024)S(1)} %pad_add_fusion.1.refs_0_, bf16[512,128,128]{2,1,0:T(8,128)(2,1)} %bitcast.45, bf16[4,128,256]{2,1,0:T(8,128)(2,1)S(1)} %get-tuple-element.44.refs_2_, bf16[4,128,256]{2,1,0:T(8,128)(2,1)S(1)} %collective-permute-done.28.refs_3_, ...), custom_call_target="tpu_custom_call" | custom-call | flops 4294967296 | bytes 25165824 | tf_op jit(solution)/shard_map/pallas_call | solution.py:139
  111.0 3.9 %collective-permute-start.34 = (bf16[128,256]{1,0:T(8,128)(2,1)S(1)}, bf16[128,256]{1,0:T(8,128)(2,1)S(1)}, u32[]{:S(2)}, u32[]{:S(2)}) collective-permute-start(bf16[128,256]{1,0:T(8,128)(2,1)S(1)} %add_add_fusion.2), channel_id=1, source_target_pairs={{0,16},{1,17},{2,18},{3,19},{4,20},{5,21},{6,22},{7,23},{8,24},{9,... | collective-permute-start | bytes 196616 | tf_op jit(solution)/shard_map/ppermute | solution.py:226
  114.9 0.8 collective-permute-start.36
  115.8 2.5 %collective-permute-done.34 = bf16[128,256]{1,0:T(8,128)(2,1)S(1)} collective-permute-done((bf16[128,256]{1,0:T(8,128)(2,1)S(1)}, bf16[128,256]{1,0:T(8,128)(2,1)S(1)}, u32[]{:S(2)}, u32[]{:S(2)}) %collective-permute-start.34) | collective-permute-done | bytes 65568 | tf_op jit(solution)/shard_map/ppermute | solution.py:226
  118.4 2.0 %collective-permute-done.36 = bf16[128,256]{1,0:T(8,128)(2,1)S(1)} collective-permute-done((bf16[128,256]{1,0:T(8,128)(2,1)S(1)}, bf16[128,256]{1,0:T(8,128)(2,1)S(1)}, u32[]{:S(2)}, u32[]{:S(2)}) %collective-permute-start.36) | collective-permute-done | bytes 65568 | tf_op jit(solution)/shard_map/ppermute | solution.py:226
  120.4 1.8 %collective-permute-start.41 = (bf16[128,256]{1,0:T(8,128)(2,1)S(1)}, bf16[128,256]{1,0:T(8,128)(2,1)S(1)}, u32[]{:S(2)}, u32[]{:S(2)}) collective-permute-start(bf16[128,256]{1,0:T(8,128)(2,1)S(1)} %add_add_fusion.1), channel_id=1, source_target_pairs={{0,2},{1,3},{2,0},{3,1},{4,6},{5,7},{6,4},{7,5},{8,10},{9,11},{10,... | collective-permute-start | bytes 196616 | tf_op jit(solution)/shard_map/ppermute | solution.py:29
  122.2 2.7 %collective-permute-start.40 = (bf16[128,256]{1,0:T(8,128)(2,1)S(1)}, bf16[128,256]{1,0:T(8,128)(2,1)S(1)}, u32[]{:S(2)}, u32[]{:S(2)}) collective-permute-start(bf16[128,256]{1,0:T(8,128)(2,1)S(1)} %add_add_fusion.1), channel_id=1, source_target_pairs={{0,1},{1,0},{2,3},{3,2},{4,5},{5,4},{6,7},{7,6},{8,9},{9,8},{10,11... | collective-permute-start | bytes 196616 | tf_op jit(solution)/shard_map/ppermute | solution.py:29
  124.9 0.4 fusion.16
  125.3 0.4 collective-permute-start.39
  125.7 3.7 %collective-permute-start.38 = (bf16[4,128,256]{2,1,0:T(8,128)(2,1)S(1)}, bf16[4,128,256]{2,1,0:T(8,128)(2,1)S(1)}, u32[]{:S(2)}, u32[]{:S(2)}) collective-permute-start(bf16[4,128,256]{2,1,0:T(8,128)(2,1)S(1)} %get-tuple-element.66), channel_id=1, source_target_pairs={{0,96},{8,104},{16,112},{24,120},{32,64},{40,72},{48,80},{56,88},{... | collective-permute-start | bytes 786440 | tf_op jit(solution)/shard_map/ppermute | solution.py:25
  129.5 4.0 %collective-permute-done.39 = bf16[4,128,256]{2,1,0:T(8,128)(2,1)S(1)} collective-permute-done((bf16[4,128,256]{2,1,0:T(8,128)(2,1)S(1)}, bf16[4,128,256]{2,1,0:T(8,128)(2,1)S(1)}, u32[]{:S(2)}, u32[]{:S(2)}) %collective-permute-start.39) | collective-permute-done | bytes 262176 | tf_op jit(solution)/shard_map/ppermute | solution.py:25
  133.4 1.1 collective-permute-done.38
  134.5 1.5 collective-permute-done.37
  136.4 0.4 collective-permute-start.43
  136.7 1.3 collective-permute-start.44
  138.0 1.7 %collective-permute-start.45 = (bf16[4,128,256]{2,1,0:T(8,128)(2,1)S(1)}, bf16[4,128,256]{2,1,0:T(8,128)(2,1)S(1)}, u32[]{:S(2)}, u32[]{:S(2)}) collective-permute-start(bf16[4,128,256]{2,1,0:T(8,128)(2,1)S(1)} %get-tuple-element.60), channel_id=1, source_target_pairs={{0,16},{8,24},{16,0},{24,8},{32,48},{40,56},{48,32},{56,40},{64,80... | collective-permute-start | bytes 786440 | tf_op jit(solution)/shard_map/ppermute | solution.py:25
  139.7 2.5 %collective-permute-start.46 = (bf16[4,128,256]{2,1,0:T(8,128)(2,1)S(1)}, bf16[4,128,256]{2,1,0:T(8,128)(2,1)S(1)}, u32[]{:S(2)}, u32[]{:S(2)}) collective-permute-start(bf16[4,128,256]{2,1,0:T(8,128)(2,1)S(1)} %get-tuple-element.61), channel_id=1, source_target_pairs={{0,64},{8,72},{16,80},{24,88},{32,96},{40,104},{48,112},{56,120},{... | collective-permute-start | bytes 786440 | tf_op jit(solution)/shard_map/ppermute | solution.py:25
  142.3 0.7 pad_maximum_fusion
  143.0 2.6 %collective-permute-done.43 = bf16[4,128,256]{2,1,0:T(8,128)(2,1)S(1)} collective-permute-done((bf16[4,128,256]{2,1,0:T(8,128)(2,1)S(1)}, bf16[4,128,256]{2,1,0:T(8,128)(2,1)S(1)}, u32[]{:S(2)}, u32[]{:S(2)}) %collective-permute-start.43) | collective-permute-done | bytes 262176 | tf_op jit(solution)/shard_map/ppermute | solution.py:25
  145.5 6.4 %collective-permute-done.44 = bf16[4,128,256]{2,1,0:T(8,128)(2,1)S(1)} collective-permute-done((bf16[4,128,256]{2,1,0:T(8,128)(2,1)S(1)}, bf16[4,128,256]{2,1,0:T(8,128)(2,1)S(1)}, u32[]{:S(2)}, u32[]{:S(2)}) %collective-permute-start.44) | collective-permute-done | bytes 262176 | tf_op jit(solution)/shard_map/ppermute | solution.py:25
  151.9 1.9 %fusion.8 = bf16[4,128,256]{2,1,0:T(8,128)(2,1)} fusion(bf16[4,128,256]{2,1,0:T(8,128)(2,1)S(1)} %collective-permute-done.46, bf16[4,128,256]{2,1,0:T(8,128)(2,1)S(1)} %collective-permute-done.45, bf16[4,128,256]{2,1,0:T(8,128)(2,1)S(1)} %collective-permute-done.44, bf16[4,128,256]{2,1,0:T(8,128)(2,1)S(1)} %collective-permute-done.43, ...), kind=kLoop, calls=%fused_computation.18 | loop fusion | flops 1835008 | bytes 1835008 | tf_op jit(solution)/shard_map/convert_element_type | solution.py:312
  (88 shorter events, 3.9 us)
Async XLA Ops:
  0.6 14.1 %collective-permute-start.7 = (bf16[4,128,256]{2,1,0:T(8,128)(2,1)}, bf16[4,128,256]{2,1,0:T(8,128)(2,1)S(1)}, u32[]{:S(2)}, u32[]{:S(2)}) collective-permute-start(bf16[4,128,256]{2,1,0:T(8,128)(2,1)} %bitcast.37), channel_id=1, source_target_pairs={{0,8},{8,0},{16,24},{24,16},{32,40},{40,32},{48,56},{56,48},{64,72... | collective-permute-start | bytes 786440 | tf_op jit(solution)/shard_map/ppermute | solution.py:25
  0.7 18.1 %collective-permute-start.5 = (bf16[4,128,256]{2,1,0:T(8,128)(2,1)}, bf16[4,128,256]{2,1,0:T(8,128)(2,1)S(1)}, u32[]{:S(2)}, u32[]{:S(2)}) collective-permute-start(bf16[4,128,256]{2,1,0:T(8,128)(2,1)} %bitcast.38), channel_id=1, source_target_pairs={{0,96},{8,104},{16,112},{24,120},{32,64},{40,72},{48,80},{56,88},{... | collective-permute-start | bytes 786440 | tf_op jit(solution)/shard_map/ppermute | solution.py:25
  3.8 10.9 %collective-permute-start.3 = (bf16[4,128,256]{2,1,0:T(8,128)(2,1)}, bf16[4,128,256]{2,1,0:T(8,128)(2,1)S(1)}, u32[]{:S(2)}, u32[]{:S(2)}) collective-permute-start(bf16[4,128,256]{2,1,0:T(8,128)(2,1)} %bitcast.39), channel_id=1, source_target_pairs={{0,64},{8,72},{16,80},{24,88},{32,96},{40,104},{48,112},{56,120},{... | collective-permute-start | bytes 786440 | tf_op jit(solution)/shard_map/ppermute | solution.py:25
  4.4 14.8 %collective-permute-start.1 = (bf16[4,128,256]{2,1,0:T(8,128)(2,1)}, bf16[4,128,256]{2,1,0:T(8,128)(2,1)S(1)}, u32[]{:S(2)}, u32[]{:S(2)}) collective-permute-start(bf16[4,128,256]{2,1,0:T(8,128)(2,1)} %bitcast.40), channel_id=1, source_target_pairs={{0,32},{8,40},{16,48},{24,56},{32,0},{40,8},{48,16},{56,24},{64,96... | collective-permute-start | bytes 786440 | tf_op jit(solution)/shard_map/ppermute | solution.py:25
  4.9 13.7 %collective-permute-start = (bf16[4,128,256]{2,1,0:T(8,128)(2,1)}, bf16[4,128,256]{2,1,0:T(8,128)(2,1)S(1)}, u32[]{:S(2)}, u32[]{:S(2)}) collective-permute-start(bf16[4,128,256]{2,1,0:T(8,128)(2,1)} %bitcast.41), channel_id=1, source_target_pairs={{0,16},{8,24},{16,0},{24,8},{32,48},{40,56},{48,32},{56,40},{64,80... | collective-permute-start | bytes 786440 | tf_op jit(solution)/shard_map/ppermute | solution.py:25
  14.7 6.2 %collective-permute-start.11 = (bf16[4,128,256]{2,1,0:T(8,128)(2,1)S(1)}, bf16[4,128,256]{2,1,0:T(8,128)(2,1)S(1)}, u32[]{:S(2)}, u32[]{:S(2)}) collective-permute-start(bf16[4,128,256]{2,1,0:T(8,128)(2,1)S(1)} %collective-permute-done.3.refs_6_), channel_id=1, source_target_pairs={{0,8},{8,0},{16,24},{24,16},{32,40},{40,32},{48,56},{56,48},{64,72... | collective-permute-start | bytes 786440 | tf_op jit(solution)/shard_map/ppermute | solution.py:25
  14.7 10.9 %collective-permute-start.4 = (bf16[4,128,256]{2,1,0:T(8,128)(2,1)S(1)}, bf16[4,128,256]{2,1,0:T(8,128)(2,1)S(1)}, u32[]{:S(2)}, u32[]{:S(2)}) collective-permute-start(bf16[4,128,256]{2,1,0:T(8,128)(2,1)S(1)} %collective-permute-done.3.refs_6_), channel_id=1, source_target_pairs={{0,16},{8,24},{16,0},{24,8},{32,48},{40,56},{48,32},{56,40},{64,80... | collective-permute-start | bytes 786440 | tf_op jit(solution)/shard_map/ppermute | solution.py:25
  18.6 9.6 %collective-permute-start.6 = (bf16[4,128,256]{2,1,0:T(8,128)(2,1)S(1)}, bf16[4,128,256]{2,1,0:T(8,128)(2,1)S(1)}, u32[]{:S(2)}, u32[]{:S(2)}) collective-permute-start(bf16[4,128,256]{2,1,0:T(8,128)(2,1)S(1)} %collective-permute-done.refs_3_), channel_id=1, source_target_pairs={{0,96},{8,104},{16,112},{24,120},{32,64},{40,72},{48,80},{56,88},{... | collective-permute-start | bytes 786440 | tf_op jit(solution)/shard_map/ppermute | solution.py:25
  18.8 9.4 %collective-permute-start.2 = (bf16[4,128,256]{2,1,0:T(8,128)(2,1)S(1)}, bf16[4,128,256]{2,1,0:T(8,128)(2,1)S(1)}, u32[]{:S(2)}, u32[]{:S(2)}) collective-permute-start(bf16[4,128,256]{2,1,0:T(8,128)(2,1)S(1)} %collective-permute-done.refs_3_), channel_id=1, source_target_pairs={{0,32},{8,40},{16,48},{24,56},{32,0},{40,8},{48,16},{56,24},{64,96... | collective-permute-start | bytes 786440 | tf_op jit(solution)/shard_map/ppermute | solution.py:25
  19.2 1.5 collective-permute-start.13
  20.8 8.9 %collective-permute-start.8 = (bf16[4,128,256]{2,1,0:T(8,128)(2,1)S(1)}, bf16[4,128,256]{2,1,0:T(8,128)(2,1)S(1)}, u32[]{:S(2)}, u32[]{:S(2)}) collective-permute-start(bf16[4,128,256]{2,1,0:T(8,128)(2,1)S(1)} %collective-permute-done.refs_3_), channel_id=1, source_target_pairs={{0,8},{8,0},{16,24},{24,16},{32,40},{40,32},{48,56},{56,48},{64,72... | collective-permute-start | bytes 786440 | tf_op jit(solution)/shard_map/ppermute | solution.py:25
  20.9 8.7 %collective-permute-start.9 = (bf16[4,128,256]{2,1,0:T(8,128)(2,1)S(1)}, bf16[4,128,256]{2,1,0:T(8,128)(2,1)S(1)}, u32[]{:S(2)}, u32[]{:S(2)}) collective-permute-start(bf16[4,128,256]{2,1,0:T(8,128)(2,1)S(1)} %collective-permute-done.1.refs_4_), channel_id=1, source_target_pairs={{0,8},{8,0},{16,24},{24,16},{32,40},{40,32},{48,56},{56,48},{64,72... | collective-permute-start | bytes 786440 | tf_op jit(solution)/shard_map/ppermute | solution.py:25
  25.6 4.0 %collective-permute-start.12 = (bf16[4,128,256]{2,1,0:T(8,128)(2,1)S(1)}, bf16[4,128,256]{2,1,0:T(8,128)(2,1)S(1)}, u32[]{:S(2)}, u32[]{:S(2)}) collective-permute-start(bf16[4,128,256]{2,1,0:T(8,128)(2,1)S(1)} %collective-permute-done.4.refs_7_), channel_id=1, source_target_pairs={{0,8},{8,0},{16,24},{24,16},{32,40},{40,32},{48,56},{56,48},{64,72... | collective-permute-start | bytes 786440 | tf_op jit(solution)/shard_map/ppermute | solution.py:25
  28.3 1.7 %collective-permute-start.14 = (bf16[4,128,256]{2,1,0:T(8,128)(2,1)S(1)}, bf16[4,128,256]{2,1,0:T(8,128)(2,1)}, u32[]{:S(2)}, u32[]{:S(2)}) collective-permute-start(bf16[4,128,256]{2,1,0:T(8,128)(2,1)S(1)} %collective-permute-done.6.refs_9_), channel_id=1, source_target_pairs={{0,8},{8,0},{16,24},{24,16},{32,40},{40,32},{48,56},{56,48},{64,72... | collective-permute-start | bytes 786440 | tf_op jit(solution)/shard_map/ppermute | solution.py:25
  28.3 2.0 %collective-permute-start.10 = (bf16[4,128,256]{2,1,0:T(8,128)(2,1)S(1)}, bf16[4,128,256]{2,1,0:T(8,128)(2,1)}, u32[]{:S(2)}, u32[]{:S(2)}) collective-permute-start(bf16[4,128,256]{2,1,0:T(8,128)(2,1)S(1)} %collective-permute-done.2.refs_5_), channel_id=1, source_target_pairs={{0,8},{8,0},{16,24},{24,16},{32,40},{40,32},{48,56},{56,48},{64,72... | collective-permute-start | bytes 786440 | tf_op jit(solution)/shard_map/ppermute | solution.py:25
  30.3 1.0 copy-start
  31.3 33.8 %copy-start.4 = (bf16[256,256]{1,0:T(8,128)(2,1)S(1)}, bf16[256,256]{1,0:T(8,128)(2,1)}, u32[]{:S(2)}) copy-start(bf16[256,256]{1,0:T(8,128)(2,1)} %weight.1) | copy-start | bytes 393220
  31.3 33.8 %copy-start.5 = (f32[256]{0:T(256)S(1)}, f32[256]{0:T(256)}, u32[]{:S(2)}) copy-start(f32[256]{0:T(256)} %param.10) | copy-start | bytes 3076
  40.7 15.7 %copy-start.2 = (bf16[4,128,256]{2,1,0:T(8,128)(2,1)}, bf16[4,128,256]{2,1,0:T(8,128)(2,1)S(1)}, u32[]{:S(2)}) copy-start(bf16[4,128,256]{2,1,0:T(8,128)(2,1)S(1)} %get-tuple-element.33.p0) | copy-start | bytes 786436
  40.7 8.9 %collective-permute-start.17 = (bf16[4,128,256]{2,1,0:T(8,128)(2,1)S(1)}, bf16[4,128,256]{2,1,0:T(8,128)(2,1)S(1)}, u32[]{:S(2)}, u32[]{:S(2)}) collective-permute-start(bf16[4,128,256]{2,1,0:T(8,128)(2,1)S(1)} %get-tuple-element.37), channel_id=1, source_target_pairs={{0,1},{1,0},{2,3},{3,2},{4,5},{5,4},{6,7},{7,6},{8,9},{9,8},{10,11... | collective-permute-start | bytes 786440 | tf_op jit(solution)/shard_map/ppermute | solution.py:29
  41.6 14.6 %collective-permute-start.18 = (bf16[4,128,256]{2,1,0:T(8,128)(2,1)S(1)}, bf16[4,128,256]{2,1,0:T(8,128)(2,1)S(1)}, u32[]{:S(2)}, u32[]{:S(2)}) collective-permute-start(bf16[4,128,256]{2,1,0:T(8,128)(2,1)S(1)} %get-tuple-element.38), channel_id=1, source_target_pairs={{0,3},{1,2},{2,1},{3,0},{4,7},{5,6},{6,5},{7,4},{8,11},{9,10},{10,... | collective-permute-start | bytes 786440 | tf_op jit(solution)/shard_map/ppermute | solution.py:29
  48.9 7.4 %collective-permute-start.20 = (bf16[4,128,256]{2,1,0:T(8,128)(2,1)S(1)}, bf16[4,128,256]{2,1,0:T(8,128)(2,1)S(1)}, u32[]{:S(2)}, u32[]{:S(2)}) collective-permute-start(bf16[4,128,256]{2,1,0:T(8,128)(2,1)S(1)} %get-tuple-element.40), channel_id=1, source_target_pairs={{0,4},{1,5},{2,6},{3,7},{4,0},{5,1},{6,2},{7,3},{8,12},{9,13},{10,... | collective-permute-start | bytes 786440 | tf_op jit(solution)/shard_map/ppermute | solution.py:29
  48.9 10.5 %collective-permute-start.15 = (bf16[4,128,256]{2,1,0:T(8,128)(2,1)}, bf16[4,128,256]{2,1,0:T(8,128)(2,1)S(1)}, u32[]{:S(2)}, u32[]{:S(2)}) collective-permute-start(bf16[4,128,256]{2,1,0:T(8,128)(2,1)} %get-tuple-element.34), channel_id=1, source_target_pairs={{0,1},{1,0},{2,3},{3,2},{4,5},{5,4},{6,7},{7,6},{8,9},{9,8},{10,11... | collective-permute-start | bytes 786440 | tf_op jit(solution)/shard_map/ppermute | solution.py:29
  49.6 15.5 %collective-permute-start.16 = (bf16[4,128,256]{2,1,0:T(8,128)(2,1)}, bf16[4,128,256]{2,1,0:T(8,128)(2,1)S(1)}, u32[]{:S(2)}, u32[]{:S(2)}) collective-permute-start(bf16[4,128,256]{2,1,0:T(8,128)(2,1)} %get-tuple-element.35), channel_id=1, source_target_pairs={{0,3},{1,2},{2,1},{3,0},{4,7},{5,6},{6,5},{7,4},{8,11},{9,10},{10,... | collective-permute-start | bytes 786440 | tf_op jit(solution)/shard_map/ppermute | solution.py:29
  56.2 8.8 %collective-permute-start.19 = (bf16[4,128,256]{2,1,0:T(8,128)(2,1)S(1)}, bf16[4,128,256]{2,1,0:T(8,128)(2,1)S(1)}, u32[]{:S(2)}, u32[]{:S(2)}) collective-permute-start(bf16[4,128,256]{2,1,0:T(8,128)(2,1)S(1)} %add_convert_fusion.9), channel_id=1, source_target_pairs={{0,4},{1,5},{2,6},{3,7},{4,0},{5,1},{6,2},{7,3},{8,12},{9,13},{10,... | collective-permute-start | bytes 786440 | tf_op jit(solution)/shard_map/ppermute | solution.py:29
  56.4 8.7 %collective-permute-start.21 = (bf16[4,128,256]{2,1,0:T(8,128)(2,1)S(1)}, bf16[4,128,256]{2,1,0:T(8,128)(2,1)S(1)}, u32[]{:S(2)}, u32[]{:S(2)}) collective-permute-start(bf16[4,128,256]{2,1,0:T(8,128)(2,1)S(1)} %add_convert_fusion.8), channel_id=1, source_target_pairs={{0,2},{1,3},{2,0},{3,1},{4,6},{5,7},{6,4},{7,5},{8,10},{9,11},{10,... | collective-permute-start | bytes 786440 | tf_op jit(solution)/shard_map/ppermute | solution.py:29
  65.1 1.0 copy-start.1
  66.1 0.9 copy-start.3
  68.1 4.8 %collective-permute-start.24 = (f32[128,256]{1,0:T(8,128)S(1)}, f32[128,256]{1,0:T(8,128)S(1)}, u32[]{:S(2)}, u32[]{:S(2)}) collective-permute-start(f32[128,256]{1,0:T(8,128)S(1)} %constant_dynamic-slice_fusion), channel_id=1, source_target_pairs={{0,8},{8,0},{16,24},{24,16},{32,40},{40,32},{48,56},{56,48},{64,72... | collective-permute-start | bytes 393224 | tf_op jit(solution)/shard_map/ppermute | solution.py:25
  68.2 8.7 %collective-permute-start.23 = (bf16[4,128,256]{2,1,0:T(8,128)(2,1)S(1)}, bf16[4,128,256]{2,1,0:T(8,128)(2,1)S(1)}, u32[]{:S(2)}, u32[]{:S(2)}) collective-permute-start(bf16[4,128,256]{2,1,0:T(8,128)(2,1)S(1)} %get-tuple-element.44.refs_2_), channel_id=1, source_target_pairs={{0,4},{1,5},{2,6},{3,7},{4,0},{5,1},{6,2},{7,3},{8,12},{9,13},{10,... | collective-permute-start | bytes 786440 | tf_op jit(solution)/shard_map/ppermute | solution.py:29
  69.6 9.9 %collective-permute-start.22 = (bf16[4,128,256]{2,1,0:T(8,128)(2,1)S(1)}, bf16[4,128,256]{2,1,0:T(8,128)(2,1)S(1)}, u32[]{:S(2)}, u32[]{:S(2)}) collective-permute-start(bf16[4,128,256]{2,1,0:T(8,128)(2,1)S(1)} %get-tuple-element.44.refs_2_), channel_id=1, source_target_pairs={{0,2},{1,3},{2,0},{3,1},{4,6},{5,7},{6,4},{7,5},{8,10},{9,11},{10,... | collective-permute-start | bytes 786440 | tf_op jit(solution)/shard_map/ppermute | solution.py:29
  79.4 8.1 %collective-permute-start.31 = (bf16[128,256]{1,0:T(8,128)(2,1)S(1)}, bf16[128,256]{1,0:T(8,128)(2,1)S(1)}, u32[]{:S(2)}, u32[]{:S(2)}) collective-permute-start(bf16[128,256]{1,0:T(8,128)(2,1)S(1)} %dynamic-slice_add_fusion), channel_id=1, source_target_pairs={{0,64},{8,72},{16,80},{24,88},{32,96},{40,104},{48,112},{56,120},{... | collective-permute-start | bytes 196616 | tf_op jit(solution)/shard_map/ppermute | solution.py:25
  80.7 7.8 %collective-permute-start.30 = (bf16[128,256]{1,0:T(8,128)(2,1)S(1)}, bf16[128,256]{1,0:T(8,128)(2,1)S(1)}, u32[]{:S(2)}, u32[]{:S(2)}) collective-permute-start(bf16[128,256]{1,0:T(8,128)(2,1)S(1)} %dynamic-slice_add_fusion), channel_id=1, source_target_pairs={{0,32},{8,40},{16,48},{24,56},{32,0},{40,8},{48,16},{56,24},{64,96... | collective-permute-start | bytes 196616 | tf_op jit(solution)/shard_map/ppermute | solution.py:25
  82.9 6.2 %collective-permute-start.32 = (bf16[128,256]{1,0:T(8,128)(2,1)S(1)}, bf16[128,256]{1,0:T(8,128)(2,1)S(1)}, u32[]{:S(2)}, u32[]{:S(2)}) collective-permute-start(bf16[128,256]{1,0:T(8,128)(2,1)S(1)} %dynamic-slice_add_fusion), channel_id=1, source_target_pairs={{0,96},{8,104},{16,112},{24,120},{32,64},{40,72},{48,80},{56,88},{... | collective-permute-start | bytes 196616 | tf_op jit(solution)/shard_map/ppermute | solution.py:25
  83.6 11.9 %collective-permute-start.29 = (bf16[4,128,256]{2,1,0:T(8,128)(2,1)S(1)}, bf16[4,128,256]{2,1,0:T(8,128)(2,1)S(1)}, u32[]{:S(2)}, u32[]{:S(2)}) collective-permute-start(bf16[4,128,256]{2,1,0:T(8,128)(2,1)S(1)} %get-tuple-element.44.refs_2_), channel_id=1, source_target_pairs={{0,3},{1,2},{2,1},{3,0},{4,7},{5,6},{6,5},{7,4},{8,11},{9,10},{10,... | collective-permute-start | bytes 786440 | tf_op jit(solution)/shard_map/ppermute | solution.py:29
  85.5 10.1 %collective-permute-start.28 = (bf16[4,128,256]{2,1,0:T(8,128)(2,1)S(1)}, bf16[4,128,256]{2,1,0:T(8,128)(2,1)S(1)}, u32[]{:S(2)}, u32[]{:S(2)}) collective-permute-start(bf16[4,128,256]{2,1,0:T(8,128)(2,1)S(1)} %get-tuple-element.44.refs_2_), channel_id=1, source_target_pairs={{0,1},{1,0},{2,3},{3,2},{4,5},{5,4},{6,7},{7,6},{8,9},{9,8},{10,11... | collective-permute-start | bytes 786440 | tf_op jit(solution)/shard_map/ppermute | solution.py:29
  87.6 8.5 %collective-permute-start.26 = (bf16[4,128,256]{2,1,0:T(8,128)(2,1)S(1)}, bf16[4,128,256]{2,1,0:T(8,128)(2,1)S(1)}, u32[]{:S(2)}, u32[]{:S(2)}) collective-permute-start(bf16[4,128,256]{2,1,0:T(8,128)(2,1)S(1)} %collective-permute-done.23.refs_6_), channel_id=1, source_target_pairs={{0,3},{1,2},{2,1},{3,0},{4,7},{5,6},{6,5},{7,4},{8,11},{9,10},{10,... | collective-permute-start | bytes 786440 | tf_op jit(solution)/shard_map/ppermute | solution.py:29
  88.5 9.3 %collective-permute-start.25 = (bf16[4,128,256]{2,1,0:T(8,128)(2,1)S(1)}, bf16[4,128,256]{2,1,0:T(8,128)(2,1)S(1)}, u32[]{:S(2)}, u32[]{:S(2)}) collective-permute-start(bf16[4,128,256]{2,1,0:T(8,128)(2,1)S(1)} %collective-permute-done.23.refs_6_), channel_id=1, source_target_pairs={{0,1},{1,0},{2,3},{3,2},{4,5},{5,4},{6,7},{7,6},{8,9},{9,8},{10,11... | collective-permute-start | bytes 786440 | tf_op jit(solution)/shard_map/ppermute | solution.py:29
  89.1 6.4 %collective-permute-start.27 = (bf16[4,128,256]{2,1,0:T(8,128)(2,1)S(1)}, bf16[4,128,256]{2,1,0:T(8,128)(2,1)S(1)}, u32[]{:S(2)}, u32[]{:S(2)}) collective-permute-start(bf16[4,128,256]{2,1,0:T(8,128)(2,1)S(1)} %collective-permute-done.22.refs_4_), channel_id=1, source_target_pairs={{0,4},{1,5},{2,6},{3,7},{4,0},{5,1},{6,2},{7,3},{8,12},{9,13},{10,... | collective-permute-start | bytes 786440 | tf_op jit(solution)/shard_map/ppermute | solution.py:29
  110.8 9.6 %collective-permute-start.33 = (bf16[8,4,128,256]{3,2,1,0:T(8,128)(2,1)S(1)}, bf16[8,4,128,256]{3,2,1,0:T(8,128)(2,1)S(1)}, u32[]{:S(2)}, u32[]{:S(2)}) collective-permute-start(bf16[8,4,128,256]{3,2,1,0:T(8,128)(2,1)S(1)} %get-tuple-element.54), channel_id=1, source_target_pairs={{0,8},{8,0},{16,24},{24,16},{32,40},{40,32},{48,56},{56,48},{64,72... | collective-permute-start | bytes 6291464 | tf_op jit(solution)/shard_map/ppermute | solution.py:25
  110.9 4.9 %collective-permute-start.35 = (bf16[128,256]{1,0:T(8,128)(2,1)S(1)}, bf16[128,256]{1,0:T(8,128)(2,1)S(1)}, u32[]{:S(2)}, u32[]{:S(2)}) collective-permute-start(bf16[128,256]{1,0:T(8,128)(2,1)S(1)} %add_add_fusion.2), channel_id=1, source_target_pairs={{0,4},{1,5},{2,6},{3,7},{4,0},{5,1},{6,2},{7,3},{8,12},{9,13},{10,... | collective-permute-start | bytes 196616 | tf_op jit(solution)/shard_map/ppermute | solution.py:226
  111.0 7.4 %collective-permute-start.34 = (bf16[128,256]{1,0:T(8,128)(2,1)S(1)}, bf16[128,256]{1,0:T(8,128)(2,1)S(1)}, u32[]{:S(2)}, u32[]{:S(2)}) collective-permute-start(bf16[128,256]{1,0:T(8,128)(2,1)S(1)} %add_add_fusion.2), channel_id=1, source_target_pairs={{0,16},{1,17},{2,18},{3,19},{4,20},{5,21},{6,22},{7,23},{8,24},{9,... | collective-permute-start | bytes 196616 | tf_op jit(solution)/shard_map/ppermute | solution.py:226
  114.9 5.5 %collective-permute-start.36 = (bf16[128,256]{1,0:T(8,128)(2,1)S(1)}, bf16[128,256]{1,0:T(8,128)(2,1)S(1)}, u32[]{:S(2)}, u32[]{:S(2)}) collective-permute-start(bf16[128,256]{1,0:T(8,128)(2,1)S(1)} %add_add_fusion.2), channel_id=1, source_target_pairs={{0,20},{1,21},{2,22},{3,23},{4,16},{5,17},{6,18},{7,19},{8,28},{9,... | collective-permute-start | bytes 196616 | tf_op jit(solution)/shard_map/ppermute | solution.py:226
  120.4 15.6 %copy-start.6 = (bf16[8,4,128,256]{3,2,1,0:T(8,128)(2,1)}, bf16[8,4,128,256]{3,2,1,0:T(8,128)(2,1)S(1)}, u32[]{:S(2)}) copy-start(bf16[8,4,128,256]{3,2,1,0:T(8,128)(2,1)S(1)} %collective-permute-done.33) | copy-start | bytes 6291460
  120.4 9.0 %collective-permute-start.41 = (bf16[128,256]{1,0:T(8,128)(2,1)S(1)}, bf16[128,256]{1,0:T(8,128)(2,1)S(1)}, u32[]{:S(2)}, u32[]{:S(2)}) collective-permute-start(bf16[128,256]{1,0:T(8,128)(2,1)S(1)} %add_add_fusion.1), channel_id=1, source_target_pairs={{0,2},{1,3},{2,0},{3,1},{4,6},{5,7},{6,4},{7,5},{8,10},{9,11},{10,... | collective-permute-start | bytes 196616 | tf_op jit(solution)/shard_map/ppermute | solution.py:29
  122.2 7.2 %collective-permute-start.40 = (bf16[128,256]{1,0:T(8,128)(2,1)S(1)}, bf16[128,256]{1,0:T(8,128)(2,1)S(1)}, u32[]{:S(2)}, u32[]{:S(2)}) collective-permute-start(bf16[128,256]{1,0:T(8,128)(2,1)S(1)} %add_add_fusion.1), channel_id=1, source_target_pairs={{0,1},{1,0},{2,3},{3,2},{4,5},{5,4},{6,7},{7,6},{8,9},{9,8},{10,11... | collective-permute-start | bytes 196616 | tf_op jit(solution)/shard_map/ppermute | solution.py:29
  124.9 4.5 %collective-permute-start.42 = (bf16[128,256]{1,0:T(8,128)(2,1)S(1)}, bf16[128,256]{1,0:T(8,128)(2,1)S(1)}, u32[]{:S(2)}, u32[]{:S(2)}) collective-permute-start(bf16[128,256]{1,0:T(8,128)(2,1)S(1)} %add_add_fusion.1), channel_id=1, source_target_pairs={{0,3},{1,2},{2,1},{3,0},{4,7},{5,6},{6,5},{7,4},{8,11},{9,10},{10,... | collective-permute-start | bytes 196616 | tf_op jit(solution)/shard_map/ppermute | solution.py:29
  125.3 8.1 %collective-permute-start.39 = (bf16[4,128,256]{2,1,0:T(8,128)(2,1)S(1)}, bf16[4,128,256]{2,1,0:T(8,128)(2,1)S(1)}, u32[]{:S(2)}, u32[]{:S(2)}) collective-permute-start(bf16[4,128,256]{2,1,0:T(8,128)(2,1)S(1)} %get-tuple-element.65), channel_id=1, source_target_pairs={{0,16},{8,24},{16,0},{24,8},{32,48},{40,56},{48,32},{56,40},{64,80... | collective-permute-start | bytes 786440 | tf_op jit(solution)/shard_map/ppermute | solution.py:25
  125.7 8.8 %collective-permute-start.38 = (bf16[4,128,256]{2,1,0:T(8,128)(2,1)S(1)}, bf16[4,128,256]{2,1,0:T(8,128)(2,1)S(1)}, u32[]{:S(2)}, u32[]{:S(2)}) collective-permute-start(bf16[4,128,256]{2,1,0:T(8,128)(2,1)S(1)} %get-tuple-element.66), channel_id=1, source_target_pairs={{0,96},{8,104},{16,112},{24,120},{32,64},{40,72},{48,80},{56,88},{... | collective-permute-start | bytes 786440 | tf_op jit(solution)/shard_map/ppermute | solution.py:25
  129.4 6.6 %collective-permute-start.37 = (bf16[4,128,256]{2,1,0:T(8,128)(2,1)S(1)}, bf16[4,128,256]{2,1,0:T(8,128)(2,1)S(1)}, u32[]{:S(2)}, u32[]{:S(2)}) collective-permute-start(bf16[4,128,256]{2,1,0:T(8,128)(2,1)S(1)} %get-tuple-element.67), channel_id=1, source_target_pairs={{0,32},{8,40},{16,48},{24,56},{32,0},{40,8},{48,16},{56,24},{64,96... | collective-permute-start | bytes 786440 | tf_op jit(solution)/shard_map/ppermute | solution.py:25
  136.3 6.0 %collective-permute-start.47 = (f32[128,256]{1,0:T(8,128)S(1)}, f32[128,256]{1,0:T(8,128)S(1)}, u32[]{:S(2)}, u32[]{:S(2)}) collective-permute-start(f32[128,256]{1,0:T(8,128)S(1)} %add_add_fusion), channel_id=1, source_target_pairs={{0,8},{8,0},{16,24},{24,16},{32,40},{40,32},{48,56},{56,48},{64,72... | collective-permute-start | bytes 393224 | tf_op jit(solution)/shard_map/ppermute | solution.py:25
  136.4 9.2 %collective-permute-start.43 = (bf16[4,128,256]{2,1,0:T(8,128)(2,1)S(1)}, bf16[4,128,256]{2,1,0:T(8,128)(2,1)S(1)}, u32[]{:S(2)}, u32[]{:S(2)}) collective-permute-start(bf16[4,128,256]{2,1,0:T(8,128)(2,1)S(1)} %get-tuple-element.58), channel_id=1, source_target_pairs={{0,32},{8,40},{16,48},{24,56},{32,0},{40,8},{48,16},{56,24},{64,96... | collective-permute-start | bytes 786440 | tf_op jit(solution)/shard_map/ppermute | solution.py:25
  136.7 15.2 %collective-permute-start.44 = (bf16[4,128,256]{2,1,0:T(8,128)(2,1)S(1)}, bf16[4,128,256]{2,1,0:T(8,128)(2,1)S(1)}, u32[]{:S(2)}, u32[]{:S(2)}) collective-permute-start(bf16[4,128,256]{2,1,0:T(8,128)(2,1)S(1)} %get-tuple-element.59), channel_id=1, source_target_pairs={{0,96},{8,104},{16,112},{24,120},{32,64},{40,72},{48,80},{56,88},{... | collective-permute-start | bytes 786440 | tf_op jit(solution)/shard_map/ppermute | solution.py:25
  138.0 13.9 %collective-permute-start.45 = (bf16[4,128,256]{2,1,0:T(8,128)(2,1)S(1)}, bf16[4,128,256]{2,1,0:T(8,128)(2,1)S(1)}, u32[]{:S(2)}, u32[]{:S(2)}) collective-permute-start(bf16[4,128,256]{2,1,0:T(8,128)(2,1)S(1)} %get-tuple-element.60), channel_id=1, source_target_pairs={{0,16},{8,24},{16,0},{24,8},{32,48},{40,56},{48,32},{56,40},{64,80... | collective-permute-start | bytes 786440 | tf_op jit(solution)/shard_map/ppermute | solution.py:25
  139.7 12.2 %collective-permute-start.46 = (bf16[4,128,256]{2,1,0:T(8,128)(2,1)S(1)}, bf16[4,128,256]{2,1,0:T(8,128)(2,1)S(1)}, u32[]{:S(2)}, u32[]{:S(2)}) collective-permute-start(bf16[4,128,256]{2,1,0:T(8,128)(2,1)S(1)} %get-tuple-element.61), channel_id=1, source_target_pairs={{0,64},{8,72},{16,80},{24,88},{32,96},{40,104},{48,112},{56,120},{... | collective-permute-start | bytes 786440 | tf_op jit(solution)/shard_map/ppermute | solution.py:25

commit v3 on v2

--- a/solution.py
+++ b/solution.py
@@ -226,10 +226,6 @@
     return lax.ppermute(value, ("row", "col"), pairs)
 
 
-def cut(array, part, count):
-    return lax.dynamic_slice_in_dim(array, part * count, count, 0)
-
-
 def per_device(
     features_in, weight, bias_vector, cotangent, adjacency, block_rows, block_cols, counts
 ):
@@ -269,14 +265,14 @@
         compiler_params=pltpu.CompilerParams(vmem_limit_bytes=32 << 20),
     )(*terms, weight, bias_vector[None, :], cotangent)
 
-    core = row_index & 1
-    count = width // 2
-    spread, half = gather_near(
+    spread, weight_sum = gather_near(
         sent,
         lambda value, ring, z: col_swap(value, ring + 4 * z),
         (
-            lambda full: cut(full, core, count) + row_swap(cut(full, core ^ 1, count), 1),
             lambda part: ring_sum(part, [lambda v, k=k: row_swap(v, 4 * k) for k in (1, 2, 3)]),
+            lambda part: ring_sum(
+                part, [lambda v, m=m: all_swap(v, *m) for m in ((2, 0), (0, 4), (2, 4))]
+            ),
         ),
         weight_grad,
     )
@@ -291,24 +287,20 @@
         True,
         42,
     )
-    half = ring_sum(
-        half, [lambda v, m=m: all_swap(v, *m) for m in ((2, 0), (0, 4), (2, 4))]
-    )
-    swapped, half = together(row_swap(theirs, 1), half)
+    rounded = weight_sum.astype(bf16)
+    weight_sum = rounded.astype(f32) + row_swap(rounded, 1).astype(f32)
+    swapped, weight_sum = together(row_swap(theirs, 1), weight_sum)
     summed = [add_up(mine[index], swapped[index]).astype(bf16) for index in range(8)]
-    terms, other = scatter_near(
+    terms, weight_sum = scatter_near(
         [summed[0::2], summed[1::2]],
         lambda value, ring, z: row_swap(value, 4 * ring + 2 * z),
         (
             lambda part: ring_sum(part, [lambda v, k=k: col_swap(v, k) for k in (1, 2, 3)]),
-            lambda part: (part, row_swap(part, 1)),
+            lambda part: part,
         ),
-        half,
-    )
-    half, other = [part * (1.0 / math.sqrt(node_dev * 128)) for part in other]
-    grad_w = jnp.concatenate(
-        [jnp.where(core == 0, half, other), jnp.where(core == 0, other, half)], axis=0
-    )
+        weight_sum,
+    )
+    grad_w = weight_sum * (1.0 / math.sqrt(node_dev * 128))
     grad_x = add_up(*terms).astype(bf16).reshape(node_dev, width)
     return (output, grad_x, grad_w)
 

time: 156 us -> 148 us (0.949)
  waiting for transfers between devices: 56.4 us -> 44.2 us
  starting transfers between devices: 59.9 us -> 69.6 us
  Pallas kernels: 23.5 us -> 20.9 us
  local copies, waits for them, and re-layouts: 2.87 us -> 0.96 us
    ppermute x17, waiting for transfers between devices: 25.9 us -> 17.4 us  [col_swap(): return lax.ppermute(value, 'col', xor_pairs(8, mask))]
    ppermute x17, starting transfers between devices: 27.2 us -> 33.3 us  [col_swap(): return lax.ppermute(value, 'col', xor_pairs(8, mask))]
    ppermute x3, waiting for transfers between devices: 4.66 us -> 0.01 us  [all_swap(): return lax.ppermute(value, ('row', 'col'), pairs)]
    ppermute x28 -> x27, starting transfers between devices: 27.9 us -> 31.6 us  [row_swap(): return lax.ppermute(value, 'row', xor_pairs(16, mask))]
    pallas_call x2, Pallas kernels: 22.4 us -> 19.8 us  [spmm(): pl.pallas_call(functools.partial(spmm_kernel, piece_total, position_total...]
    unnamed x14 -> x8, local copies, waits for them, and re-layouts: 2.86 us -> 0.96 us
    ppermute x28 -> x27, waiting for transfers between devices: 25.9 us -> 26.8 us  [row_swap(): return lax.ppermute(value, 'row', xor_pairs(16, mask))]
  transfers between devices with their start and end apart: 48 -> 47, of which waited for: 21 -> 19; matrix products, arithmetic and copies ran while one was open for 4% -> 4% of each run, Pallas kernels for 0% -> 0%
where the time goes in v3:
time: 148 us; the launch traced here: 146 us
  starting transfers between devices  69.6 us (47%)
  waiting for transfers between devices  44.2 us (30%)
  Pallas kernels  20.9 us (14%)
  other arithmetic  7.39 us (5%)
  between operations  2.82 us (2%)
    ppermute x17, starting transfers between devices, col_swap(): return lax.ppermute(value, 'col', xor_pairs(8, mask))  33.3 us
    ppermute x27, starting transfers between devices, row_swap(): return lax.ppermute(value, 'row', xor_pairs(16, mask))  31.6 us
    ppermute x27, waiting for transfers between devices, row_swap(): return lax.ppermute(value, 'row', xor_pairs(16, mask))  26.8 us
    pallas_call x2, Pallas kernels, spmm(): pl.pallas_call(functools.partial(spmm_kernel, piece_total, position_total...  19.8 us
    ppermute x17, waiting for transfers between devices, col_swap(): return lax.ppermute(value, 'col', xor_pairs(8, mask))  17.4 us
    ppermute x3, starting transfers between devices, all_swap(): return lax.ppermute(value, ('row', 'col'), pairs)  4.7 us
  transfers between devices with their start and end apart: 47, of which 19 were waited for; matrix products, arithmetic and copies ran while one was open for 4% of the time, Pallas kernels for 0%

profile of v3, /device:TPU:2, one launch (start us, length us, event | category | flops | bytes accessed | tf_op | source)
XLA Modules:
  0.0 145.8 jit_solution(3654068331446371512)
XLA Ops:
  0.7 3.1 %collective-permute-start.5 = (bf16[4,128,256]{2,1,0:T(8,128)(2,1)}, bf16[4,128,256]{2,1,0:T(8,128)(2,1)S(1)}, u32[]{:S(2)}, u32[]{:S(2)}) collective-permute-start(bf16[4,128,256]{2,1,0:T(8,128)(2,1)} %bitcast.38), channel_id=1, source_target_pairs={{0,96},{8,104},{16,112},{24,120},{32,64},{40,72},{48,80},{56,88},{... | collective-permute-start | bytes 786440 | tf_op jit(solution)/shard_map/ppermute | solution.py:25
  3.8 0.6 collective-permute-start.3
  4.4 0.5 collective-permute-start.1
  4.9 3.9 %collective-permute-start = (bf16[4,128,256]{2,1,0:T(8,128)(2,1)}, bf16[4,128,256]{2,1,0:T(8,128)(2,1)S(1)}, u32[]{:S(2)}, u32[]{:S(2)}) collective-permute-start(bf16[4,128,256]{2,1,0:T(8,128)(2,1)} %bitcast.41), channel_id=1, source_target_pairs={{0,16},{8,24},{16,0},{24,8},{32,48},{40,56},{48,32},{56,40},{64,80... | collective-permute-start | bytes 786440 | tf_op jit(solution)/shard_map/ppermute | solution.py:25
  9.4 0.7 shift-left_or_fusion
  10.6 0.6 fusion.22
  11.4 0.7 and_or_fusion
  12.6 0.6 fusion.20
  13.3 1.4 collective-permute-done.3.refs_6_
  14.7 3.9 %collective-permute-start.4 = (bf16[4,128,256]{2,1,0:T(8,128)(2,1)S(1)}, bf16[4,128,256]{2,1,0:T(8,128)(2,1)S(1)}, u32[]{:S(2)}, u32[]{:S(2)}) collective-permute-start(bf16[4,128,256]{2,1,0:T(8,128)(2,1)S(1)} %collective-permute-done.3.refs_6_), channel_id=1, source_target_pairs={{0,16},{8,24},{16,0},{24,8},{32,48},{40,56},{48,32},{56,40},{64,80... | collective-permute-start | bytes 786440 | tf_op jit(solution)/shard_map/ppermute | solution.py:25
  18.8 0.4 collective-permute-start.2
  19.4 1.3 collective-permute-done.13.refs_16_
  20.9 0.4 collective-permute-start.9
  21.3 4.3 %collective-permute-done.4.refs_7_ = bf16[4,128,256]{2,1,0:T(8,128)(2,1)S(1)} collective-permute-done((bf16[4,128,256]{2,1,0:T(8,128)(2,1)S(1)}, bf16[4,128,256]{2,1,0:T(8,128)(2,1)S(1)}, u32[]{:S(2)}, u32[]{:S(2)}) %collective-permute-start.4) | collective-permute-done | bytes 262176 | tf_op jit(solution)/shard_map/ppermute | solution.py:25
  25.6 2.7 %collective-permute-done.6.refs_9_ = bf16[4,128,256]{2,1,0:T(8,128)(2,1)S(1)} collective-permute-done((bf16[4,128,256]{2,1,0:T(8,128)(2,1)S(1)}, bf16[4,128,256]{2,1,0:T(8,128)(2,1)S(1)}, u32[]{:S(2)}, u32[]{:S(2)}) %collective-permute-start.6) | collective-permute-done | bytes 262176 | tf_op jit(solution)/shard_map/ppermute | solution.py:25
  28.3 0.5 collective-permute-start.10
  29.6 0.3 collective-permute-done.14.refs_17_
  29.9 0.4 collective-permute-done.10.refs_13_
  30.3 0.9 copy-done
  31.3 9.2 %shard_map.103 = (bf16[4,128,256]{2,1,0:T(8,128)(2,1)S(1)}, bf16[4,128,256]{2,1,0:T(8,128)(2,1)S(1)}, bf16[4,128,256]{2,1,0:T(8,128)(2,1)S(1)}, bf16[4,128,256]{...) custom-call(s32[761]{0:T(1024)S(1)} %pad_add_fusion.refs_0_, ...), custom_call_target="tpu_custom_call" | custom-call | flops 4294967296 | bytes 25165824 | tf_op jit(solution)/shard_map/pallas_call | solution.py:139
  40.7 0.6 collective-permute-start.18
  41.3 6.1 %collective-permute-start.20 = (bf16[4,128,256]{2,1,0:T(8,128)(2,1)S(1)}, bf16[4,128,256]{2,1,0:T(8,128)(2,1)S(1)}, u32[]{:S(2)}, u32[]{:S(2)}) collective-permute-start(bf16[4,128,256]{2,1,0:T(8,128)(2,1)S(1)} %get-tuple-element.40), channel_id=1, source_target_pairs={{0,4},{1,5},{2,6},{3,7},{4,0},{5,1},{6,2},{7,3},{8,12},{9,13},{10,... | collective-permute-start | bytes 786440 | tf_op jit(solution)/shard_map/ppermute | solution.py:29
  47.4 2.5 %collective-permute-start.15 = (bf16[4,128,256]{2,1,0:T(8,128)(2,1)S(1)}, bf16[4,128,256]{2,1,0:T(8,128)(2,1)S(1)}, u32[]{:S(2)}, u32[]{:S(2)}) collective-permute-start(bf16[4,128,256]{2,1,0:T(8,128)(2,1)S(1)} %get-tuple-element.34), channel_id=1, source_target_pairs={{0,1},{1,0},{2,3},{3,2},{4,5},{5,4},{6,7},{7,6},{8,9},{9,8},{10,11... | collective-permute-start | bytes 786440 | tf_op jit(solution)/shard_map/ppermute | solution.py:29
  50.0 4.5 %collective-permute-start.19 = (bf16[4,128,256]{2,1,0:T(8,128)(2,1)S(1)}, bf16[4,128,256]{2,1,0:T(8,128)(2,1)S(1)}, u32[]{:S(2)}, u32[]{:S(2)}) collective-permute-start(bf16[4,128,256]{2,1,0:T(8,128)(2,1)S(1)} %add_convert_fusion.9), channel_id=1, source_target_pairs={{0,4},{1,5},{2,6},{3,7},{4,0},{5,1},{6,2},{7,3},{8,12},{9,13},{10,... | collective-permute-start | bytes 786440 | tf_op jit(solution)/shard_map/ppermute | solution.py:29
  54.6 4.9 %collective-permute-start.21 = (bf16[4,128,256]{2,1,0:T(8,128)(2,1)S(1)}, bf16[4,128,256]{2,1,0:T(8,128)(2,1)S(1)}, u32[]{:S(2)}, u32[]{:S(2)}) collective-permute-start(bf16[4,128,256]{2,1,0:T(8,128)(2,1)S(1)} %add_convert_fusion.8), channel_id=1, source_target_pairs={{0,2},{1,3},{2,0},{3,1},{4,6},{5,7},{6,4},{7,5},{8,10},{9,11},{10,... | collective-permute-start | bytes 786440 | tf_op jit(solution)/shard_map/ppermute | solution.py:29
  59.8 1.7 %collective-permute-done.19.p3 = bf16[4,128,256]{2,1,0:T(8,128)(2,1)S(1)} collective-permute-done((bf16[4,128,256]{2,1,0:T(8,128)(2,1)S(1)}, bf16[4,128,256]{2,1,0:T(8,128)(2,1)S(1)}, u32[]{:S(2)}, u32[]{:S(2)}) %collective-permute-start.19) | collective-permute-done | bytes 262176 | tf_op jit(solution)/shard_map/ppermute | solution.py:29
  61.5 3.1 %collective-permute-done.21.p4 = bf16[4,128,256]{2,1,0:T(8,128)(2,1)S(1)} collective-permute-done((bf16[4,128,256]{2,1,0:T(8,128)(2,1)S(1)}, bf16[4,128,256]{2,1,0:T(8,128)(2,1)S(1)}, u32[]{:S(2)}, u32[]{:S(2)}) %collective-permute-start.21) | collective-permute-done | bytes 262176 | tf_op jit(solution)/shard_map/ppermute | solution.py:29
  64.6 1.1 shard_map.104
  65.7 0.4 collective-permute-start.25
  66.1 1.9 %collective-permute-start.24 = (bf16[256,256]{1,0:T(8,128)(2,1)S(1)}, bf16[256,256]{1,0:T(8,128)(2,1)S(1)}, u32[]{:S(2)}, u32[]{:S(2)}) collective-permute-start(bf16[256,256]{1,0:T(8,128)(2,1)S(1)} %convert_element_type.260), channel_id=1, source_target_pairs={{0,32},{8,40},{16,48},{24,56},{32,0},{40,8},{48,16},{56,24},{64,96... | collective-permute-start | bytes 393224 | tf_op jit(solution)/shard_map/ppermute | solution.py:25
  68.0 1.9 %collective-permute-start.26 = (bf16[256,256]{1,0:T(8,128)(2,1)S(1)}, bf16[256,256]{1,0:T(8,128)(2,1)S(1)}, u32[]{:S(2)}, u32[]{:S(2)}) collective-permute-start(bf16[256,256]{1,0:T(8,128)(2,1)S(1)} %convert_element_type.260), channel_id=1, source_target_pairs={{0,96},{8,104},{16,112},{24,120},{32,64},{40,72},{48,80},{56,88},{... | collective-permute-start | bytes 393224 | tf_op jit(solution)/shard_map/ppermute | solution.py:25
  69.9 1.3 collective-permute-start.23
  71.2 2.9 %collective-permute-start.22 = (bf16[4,128,256]{2,1,0:T(8,128)(2,1)S(1)}, bf16[4,128,256]{2,1,0:T(8,128)(2,1)S(1)}, u32[]{:S(2)}, u32[]{:S(2)}) collective-permute-start(bf16[4,128,256]{2,1,0:T(8,128)(2,1)S(1)} %get-tuple-element.44.refs_2_), channel_id=1, source_target_pairs={{0,2},{1,3},{2,0},{3,1},{4,6},{5,7},{6,4},{7,5},{8,10},{9,11},{10,... | collective-permute-start | bytes 786440 | tf_op jit(solution)/shard_map/ppermute | solution.py:29
  74.2 2.0 %collective-permute-done.23.refs_6_ = bf16[4,128,256]{2,1,0:T(8,128)(2,1)S(1)} collective-permute-done((bf16[4,128,256]{2,1,0:T(8,128)(2,1)S(1)}, bf16[4,128,256]{2,1,0:T(8,128)(2,1)S(1)}, u32[]{:S(2)}, u32[]{:S(2)}) %collective-permute-start.23) | collective-permute-done | bytes 262176 | tf_op jit(solution)/shard_map/ppermute | solution.py:29
  76.3 2.9 %collective-permute-done.22.refs_4_ = bf16[4,128,256]{2,1,0:T(8,128)(2,1)S(1)} collective-permute-done((bf16[4,128,256]{2,1,0:T(8,128)(2,1)S(1)}, bf16[4,128,256]{2,1,0:T(8,128)(2,1)S(1)}, u32[]{:S(2)}, u32[]{:S(2)}) %collective-permute-start.22) | collective-permute-done | bytes 262176 | tf_op jit(solution)/shard_map/ppermute | solution.py:29
  79.1 0.7 collective-permute-start.33
  79.8 2.4 %collective-permute-start.32 = (bf16[256,256]{1,0:T(8,128)(2,1)S(1)}, bf16[256,256]{1,0:T(8,128)(2,1)S(1)}, u32[]{:S(2)}, u32[]{:S(2)}) collective-permute-start(bf16[256,256]{1,0:T(8,128)(2,1)S(1)} %add_add_fusion.2), channel_id=1, source_target_pairs={{0,16},{1,17},{2,18},{3,19},{4,20},{5,21},{6,22},{7,23},{8,24},{9,... | collective-permute-start | bytes 393224 | tf_op jit(solution)/shard_map/ppermute | solution.py:226
  82.2 1.6 %collective-permute-start.34 = (bf16[256,256]{1,0:T(8,128)(2,1)S(1)}, bf16[256,256]{1,0:T(8,128)(2,1)S(1)}, u32[]{:S(2)}, u32[]{:S(2)}) collective-permute-start(bf16[256,256]{1,0:T(8,128)(2,1)S(1)} %add_add_fusion.2), channel_id=1, source_target_pairs={{0,20},{1,21},{2,22},{3,23},{4,16},{5,17},{6,18},{7,19},{8,28},{9,... | collective-permute-start | bytes 393224 | tf_op jit(solution)/shard_map/ppermute | solution.py:226
  84.6 2.7 %collective-permute-start.31 = (bf16[4,128,256]{2,1,0:T(8,128)(2,1)S(1)}, bf16[4,128,256]{2,1,0:T(8,128)(2,1)S(1)}, u32[]{:S(2)}, u32[]{:S(2)}) collective-permute-start(bf16[4,128,256]{2,1,0:T(8,128)(2,1)S(1)} %get-tuple-element.44.refs_2_), channel_id=1, source_target_pairs={{0,3},{1,2},{2,1},{3,0},{4,7},{5,6},{6,5},{7,4},{8,11},{9,10},{10,... | collective-permute-start | bytes 786440 | tf_op jit(solution)/shard_map/ppermute | solution.py:29
  87.3 1.5 %collective-permute-start.30 = (bf16[4,128,256]{2,1,0:T(8,128)(2,1)S(1)}, bf16[4,128,256]{2,1,0:T(8,128)(2,1)S(1)}, u32[]{:S(2)}, u32[]{:S(2)}) collective-permute-start(bf16[4,128,256]{2,1,0:T(8,128)(2,1)S(1)} %get-tuple-element.44.refs_2_), channel_id=1, source_target_pairs={{0,1},{1,0},{2,3},{3,2},{4,5},{5,4},{6,7},{7,6},{8,9},{9,8},{10,11... | collective-permute-start | bytes 786440 | tf_op jit(solution)/shard_map/ppermute | solution.py:29
  88.8 0.8 collective-permute-start.28
  89.6 0.6 collective-permute-start.27
  90.4 6.2 %collective-permute-done.29.refs_8_ = bf16[4,128,256]{2,1,0:T(8,128)(2,1)S(1)} collective-permute-done((bf16[4,128,256]{2,1,0:T(8,128)(2,1)S(1)}, bf16[4,128,256]{2,1,0:T(8,128)(2,1)S(1)}, u32[]{:S(2)}, u32[]{:S(2)}) %collective-permute-start.29) | collective-permute-done | bytes 262176 | tf_op jit(solution)/shard_map/ppermute | solution.py:29
  96.6 1.4 collective-permute-done.27.refs_7_
  98.0 10.7 %shard_map.105 = (bf16[8,4,128,256]{3,2,1,0:T(8,128)(2,1)S(1)}, bf16[8,4,128,256]{3,2,1,0:T(8,128)(2,1)S(1)}) custom-call(s32[881]{0:T(1024)S(1)} %pad_add_fusion.1.refs_0_, bf16[512,128,128]{2,1,0:T(8,128)(2,1)} %bitcast.45, bf16[4,128,256]{2,1,0:T(8,128)(2,1)S(1)} %get-tuple-element.44.refs_2_, bf16[4,128,256]{2,1,0:T(8,128)(2,1)S(1)} %collective-permute-done.30.refs_3_, ...), custom_call_target="tpu_custom_call" | custom-call | flops 4294967296 | bytes 25165824 | tf_op jit(solution)/shard_map/pallas_call | solution.py:139
  108.7 0.4 collective-permute-start.35
  109.3 3.8 %collective-permute-done.36 = bf16[256,256]{1,0:T(8,128)(2,1)S(1)} collective-permute-done((bf16[256,256]{1,0:T(8,128)(2,1)S(1)}, bf16[256,256]{1,0:T(8,128)(2,1)S(1)}, u32[]{:S(2)}, u32[]{:S(2)}) %collective-permute-start.36) | collective-permute-done | bytes 131104 | tf_op jit(solution)/shard_map/ppermute | solution.py:25
  113.2 0.4 collective-permute-start.41
  113.5 4.0 %collective-permute-start.40 = (bf16[256,256]{1,0:T(8,128)(2,1)S(1)}, bf16[256,256]{1,0:T(8,128)(2,1)S(1)}, u32[]{:S(2)}, u32[]{:S(2)}) collective-permute-start(bf16[256,256]{1,0:T(8,128)(2,1)S(1)} %convert_add_fusion.3), channel_id=1, source_target_pairs={{0,1},{1,0},{2,3},{3,2},{4,5},{5,4},{6,7},{7,6},{8,9},{9,8},{10,11... | collective-permute-start | bytes 393224 | tf_op jit(solution)/shard_map/ppermute | solution.py:29
  117.8 0.4 fusion.16
  118.3 1.1 collective-permute-start.39
  119.4 3.9 %collective-permute-start.38 = (bf16[4,128,256]{2,1,0:T(8,128)(2,1)S(1)}, bf16[4,128,256]{2,1,0:T(8,128)(2,1)S(1)}, u32[]{:S(2)}, u32[]{:S(2)}) collective-permute-start(bf16[4,128,256]{2,1,0:T(8,128)(2,1)S(1)} %get-tuple-element.66), channel_id=1, source_target_pairs={{0,96},{8,104},{16,112},{24,120},{32,64},{40,72},{48,80},{56,88},{... | collective-permute-start | bytes 786440 | tf_op jit(solution)/shard_map/ppermute | solution.py:25
  123.3 0.8 collective-permute-start.37
  124.2 3.5 %collective-permute-done.39 = bf16[4,128,256]{2,1,0:T(8,128)(2,1)S(1)} collective-permute-done((bf16[4,128,256]{2,1,0:T(8,128)(2,1)S(1)}, bf16[4,128,256]{2,1,0:T(8,128)(2,1)S(1)}, u32[]{:S(2)}, u32[]{:S(2)}) %collective-permute-start.39) | collective-permute-done | bytes 262176 | tf_op jit(solution)/shard_map/ppermute | solution.py:25
  127.6 1.4 collective-permute-done.38
  129.0 1.5 %collective-permute-done.37 = bf16[4,128,256]{2,1,0:T(8,128)(2,1)S(1)} collective-permute-done((bf16[4,128,256]{2,1,0:T(8,128)(2,1)S(1)}, bf16[4,128,256]{2,1,0:T(8,128)(2,1)S(1)}, u32[]{:S(2)}, u32[]{:S(2)}) %collective-permute-start.37) | collective-permute-done | bytes 262176 | tf_op jit(solution)/shard_map/ppermute | solution.py:25
  130.8 0.4 collective-permute-start.43
  131.1 2.6 %collective-permute-start.44 = (bf16[4,128,256]{2,1,0:T(8,128)(2,1)S(1)}, bf16[4,128,256]{2,1,0:T(8,128)(2,1)S(1)}, u32[]{:S(2)}, u32[]{:S(2)}) collective-permute-start(bf16[4,128,256]{2,1,0:T(8,128)(2,1)S(1)} %get-tuple-element.59), channel_id=1, source_target_pairs={{0,96},{8,104},{16,112},{24,120},{32,64},{40,72},{48,80},{56,88},{... | collective-permute-start | bytes 786440 | tf_op jit(solution)/shard_map/ppermute | solution.py:25
  133.8 1.8 %collective-permute-start.45 = (bf16[4,128,256]{2,1,0:T(8,128)(2,1)S(1)}, bf16[4,128,256]{2,1,0:T(8,128)(2,1)S(1)}, u32[]{:S(2)}, u32[]{:S(2)}) collective-permute-start(bf16[4,128,256]{2,1,0:T(8,128)(2,1)S(1)} %get-tuple-element.60), channel_id=1, source_target_pairs={{0,16},{8,24},{16,0},{24,8},{32,48},{40,56},{48,32},{56,40},{64,80... | collective-permute-start | bytes 786440 | tf_op jit(solution)/shard_map/ppermute | solution.py:25
  135.6 2.5 %collective-permute-start.46 = (bf16[4,128,256]{2,1,0:T(8,128)(2,1)S(1)}, bf16[4,128,256]{2,1,0:T(8,128)(2,1)S(1)}, u32[]{:S(2)}, u32[]{:S(2)}) collective-permute-start(bf16[4,128,256]{2,1,0:T(8,128)(2,1)S(1)} %get-tuple-element.61), channel_id=1, source_target_pairs={{0,64},{8,72},{16,80},{24,88},{32,96},{40,104},{48,112},{56,120},{... | collective-permute-start | bytes 786440 | tf_op jit(solution)/shard_map/ppermute | solution.py:25
  138.1 0.7 broadcast_multiply_fusion
  138.8 4.5 %collective-permute-done.44 = bf16[4,128,256]{2,1,0:T(8,128)(2,1)S(1)} collective-permute-done((bf16[4,128,256]{2,1,0:T(8,128)(2,1)S(1)}, bf16[4,128,256]{2,1,0:T(8,128)(2,1)S(1)}, u32[]{:S(2)}, u32[]{:S(2)}) %collective-permute-start.44) | collective-permute-done | bytes 262176 | tf_op jit(solution)/shard_map/ppermute | solution.py:25
  143.3 1.6 %collective-permute-done.46 = bf16[4,128,256]{2,1,0:T(8,128)(2,1)S(1)} collective-permute-done((bf16[4,128,256]{2,1,0:T(8,128)(2,1)S(1)}, bf16[4,128,256]{2,1,0:T(8,128)(2,1)S(1)}, u32[]{:S(2)}, u32[]{:S(2)}) %collective-permute-start.46) | collective-permute-done | bytes 262176 | tf_op jit(solution)/shard_map/ppermute | solution.py:25
  144.9 0.9 fusion.8
  (79 shorter events, 4.0 us)
Async XLA Ops:
  0.6 14.1 %collective-permute-start.7 = (bf16[4,128,256]{2,1,0:T(8,128)(2,1)}, bf16[4,128,256]{2,1,0:T(8,128)(2,1)S(1)}, u32[]{:S(2)}, u32[]{:S(2)}) collective-permute-start(bf16[4,128,256]{2,1,0:T(8,128)(2,1)} %bitcast.37), channel_id=1, source_target_pairs={{0,8},{8,0},{16,24},{24,16},{32,40},{40,32},{48,56},{56,48},{64,72... | collective-permute-start | bytes 786440 | tf_op jit(solution)/shard_map/ppermute | solution.py:25
  0.7 18.1 %collective-permute-start.5 = (bf16[4,128,256]{2,1,0:T(8,128)(2,1)}, bf16[4,128,256]{2,1,0:T(8,128)(2,1)S(1)}, u32[]{:S(2)}, u32[]{:S(2)}) collective-permute-start(bf16[4,128,256]{2,1,0:T(8,128)(2,1)} %bitcast.38), channel_id=1, source_target_pairs={{0,96},{8,104},{16,112},{24,120},{32,64},{40,72},{48,80},{56,88},{... | collective-permute-start | bytes 786440 | tf_op jit(solution)/shard_map/ppermute | solution.py:25
  3.8 10.9 %collective-permute-start.3 = (bf16[4,128,256]{2,1,0:T(8,128)(2,1)}, bf16[4,128,256]{2,1,0:T(8,128)(2,1)S(1)}, u32[]{:S(2)}, u32[]{:S(2)}) collective-permute-start(bf16[4,128,256]{2,1,0:T(8,128)(2,1)} %bitcast.39), channel_id=1, source_target_pairs={{0,64},{8,72},{16,80},{24,88},{32,96},{40,104},{48,112},{56,120},{... | collective-permute-start | bytes 786440 | tf_op jit(solution)/shard_map/ppermute | solution.py:25
  4.4 14.8 %collective-permute-start.1 = (bf16[4,128,256]{2,1,0:T(8,128)(2,1)}, bf16[4,128,256]{2,1,0:T(8,128)(2,1)S(1)}, u32[]{:S(2)}, u32[]{:S(2)}) collective-permute-start(bf16[4,128,256]{2,1,0:T(8,128)(2,1)} %bitcast.40), channel_id=1, source_target_pairs={{0,32},{8,40},{16,48},{24,56},{32,0},{40,8},{48,16},{56,24},{64,96... | collective-permute-start | bytes 786440 | tf_op jit(solution)/shard_map/ppermute | solution.py:25
  4.9 13.7 %collective-permute-start = (bf16[4,128,256]{2,1,0:T(8,128)(2,1)}, bf16[4,128,256]{2,1,0:T(8,128)(2,1)S(1)}, u32[]{:S(2)}, u32[]{:S(2)}) collective-permute-start(bf16[4,128,256]{2,1,0:T(8,128)(2,1)} %bitcast.41), channel_id=1, source_target_pairs={{0,16},{8,24},{16,0},{24,8},{32,48},{40,56},{48,32},{56,40},{64,80... | collective-permute-start | bytes 786440 | tf_op jit(solution)/shard_map/ppermute | solution.py:25
  14.7 6.2 %collective-permute-start.11 = (bf16[4,128,256]{2,1,0:T(8,128)(2,1)S(1)}, bf16[4,128,256]{2,1,0:T(8,128)(2,1)S(1)}, u32[]{:S(2)}, u32[]{:S(2)}) collective-permute-start(bf16[4,128,256]{2,1,0:T(8,128)(2,1)S(1)} %collective-permute-done.3.refs_6_), channel_id=1, source_target_pairs={{0,8},{8,0},{16,24},{24,16},{32,40},{40,32},{48,56},{56,48},{64,72... | collective-permute-start | bytes 786440 | tf_op jit(solution)/shard_map/ppermute | solution.py:25
  14.7 10.9 %collective-permute-start.4 = (bf16[4,128,256]{2,1,0:T(8,128)(2,1)S(1)}, bf16[4,128,256]{2,1,0:T(8,128)(2,1)S(1)}, u32[]{:S(2)}, u32[]{:S(2)}) collective-permute-start(bf16[4,128,256]{2,1,0:T(8,128)(2,1)S(1)} %collective-permute-done.3.refs_6_), channel_id=1, source_target_pairs={{0,16},{8,24},{16,0},{24,8},{32,48},{40,56},{48,32},{56,40},{64,80... | collective-permute-start | bytes 786440 | tf_op jit(solution)/shard_map/ppermute | solution.py:25
  18.6 9.6 %collective-permute-start.6 = (bf16[4,128,256]{2,1,0:T(8,128)(2,1)S(1)}, bf16[4,128,256]{2,1,0:T(8,128)(2,1)S(1)}, u32[]{:S(2)}, u32[]{:S(2)}) collective-permute-start(bf16[4,128,256]{2,1,0:T(8,128)(2,1)S(1)} %collective-permute-done.refs_3_), channel_id=1, source_target_pairs={{0,96},{8,104},{16,112},{24,120},{32,64},{40,72},{48,80},{56,88},{... | collective-permute-start | bytes 786440 | tf_op jit(solution)/shard_map/ppermute | solution.py:25
  18.8 9.4 %collective-permute-start.2 = (bf16[4,128,256]{2,1,0:T(8,128)(2,1)S(1)}, bf16[4,128,256]{2,1,0:T(8,128)(2,1)S(1)}, u32[]{:S(2)}, u32[]{:S(2)}) collective-permute-start(bf16[4,128,256]{2,1,0:T(8,128)(2,1)S(1)} %collective-permute-done.refs_3_), channel_id=1, source_target_pairs={{0,32},{8,40},{16,48},{24,56},{32,0},{40,8},{48,16},{56,24},{64,96... | collective-permute-start | bytes 786440 | tf_op jit(solution)/shard_map/ppermute | solution.py:25
  19.2 1.5 %collective-permute-start.13 = (bf16[4,128,256]{2,1,0:T(8,128)(2,1)S(1)}, bf16[4,128,256]{2,1,0:T(8,128)(2,1)S(1)}, u32[]{:S(2)}, u32[]{:S(2)}) collective-permute-start(bf16[4,128,256]{2,1,0:T(8,128)(2,1)S(1)} %collective-permute-done.5.refs_8_), channel_id=1, source_target_pairs={{0,8},{8,0},{16,24},{24,16},{32,40},{40,32},{48,56},{56,48},{64,72... | collective-permute-start | bytes 786440 | tf_op jit(solution)/shard_map/ppermute | solution.py:25
  20.8 8.9 %collective-permute-start.8 = (bf16[4,128,256]{2,1,0:T(8,128)(2,1)S(1)}, bf16[4,128,256]{2,1,0:T(8,128)(2,1)S(1)}, u32[]{:S(2)}, u32[]{:S(2)}) collective-permute-start(bf16[4,128,256]{2,1,0:T(8,128)(2,1)S(1)} %collective-permute-done.refs_3_), channel_id=1, source_target_pairs={{0,8},{8,0},{16,24},{24,16},{32,40},{40,32},{48,56},{56,48},{64,72... | collective-permute-start | bytes 786440 | tf_op jit(solution)/shard_map/ppermute | solution.py:25
  20.9 8.7 %collective-permute-start.9 = (bf16[4,128,256]{2,1,0:T(8,128)(2,1)S(1)}, bf16[4,128,256]{2,1,0:T(8,128)(2,1)S(1)}, u32[]{:S(2)}, u32[]{:S(2)}) collective-permute-start(bf16[4,128,256]{2,1,0:T(8,128)(2,1)S(1)} %collective-permute-done.1.refs_4_), channel_id=1, source_target_pairs={{0,8},{8,0},{16,24},{24,16},{32,40},{40,32},{48,56},{56,48},{64,72... | collective-permute-start | bytes 786440 | tf_op jit(solution)/shard_map/ppermute | solution.py:25
  25.6 4.0 %collective-permute-start.12 = (bf16[4,128,256]{2,1,0:T(8,128)(2,1)S(1)}, bf16[4,128,256]{2,1,0:T(8,128)(2,1)S(1)}, u32[]{:S(2)}, u32[]{:S(2)}) collective-permute-start(bf16[4,128,256]{2,1,0:T(8,128)(2,1)S(1)} %collective-permute-done.4.refs_7_), channel_id=1, source_target_pairs={{0,8},{8,0},{16,24},{24,16},{32,40},{40,32},{48,56},{56,48},{64,72... | collective-permute-start | bytes 786440 | tf_op jit(solution)/shard_map/ppermute | solution.py:25
  28.3 1.7 %collective-permute-start.14 = (bf16[4,128,256]{2,1,0:T(8,128)(2,1)S(1)}, bf16[4,128,256]{2,1,0:T(8,128)(2,1)}, u32[]{:S(2)}, u32[]{:S(2)}) collective-permute-start(bf16[4,128,256]{2,1,0:T(8,128)(2,1)S(1)} %collective-permute-done.6.refs_9_), channel_id=1, source_target_pairs={{0,8},{8,0},{16,24},{24,16},{32,40},{40,32},{48,56},{56,48},{64,72... | collective-permute-start | bytes 786440 | tf_op jit(solution)/shard_map/ppermute | solution.py:25
  28.3 2.0 %collective-permute-start.10 = (bf16[4,128,256]{2,1,0:T(8,128)(2,1)S(1)}, bf16[4,128,256]{2,1,0:T(8,128)(2,1)}, u32[]{:S(2)}, u32[]{:S(2)}) collective-permute-start(bf16[4,128,256]{2,1,0:T(8,128)(2,1)S(1)} %collective-permute-done.2.refs_5_), channel_id=1, source_target_pairs={{0,8},{8,0},{16,24},{24,16},{32,40},{40,32},{48,56},{56,48},{64,72... | collective-permute-start | bytes 786440 | tf_op jit(solution)/shard_map/ppermute | solution.py:25
  30.3 1.0 copy-start
  31.3 33.3 %copy-start.1 = (bf16[512,256]{1,0:T(8,128)(2,1)S(1)}, bf16[512,256]{1,0:T(8,128)(2,1)}, u32[]{:S(2)}) copy-start(bf16[512,256]{1,0:T(8,128)(2,1)} %cotangent.1) | copy-start | bytes 786436
  31.3 33.3 %copy-start.2 = (bf16[256,256]{1,0:T(8,128)(2,1)S(1)}, bf16[256,256]{1,0:T(8,128)(2,1)}, u32[]{:S(2)}) copy-start(bf16[256,256]{1,0:T(8,128)(2,1)} %weight.1) | copy-start | bytes 393220
  31.3 33.3 %copy-start.3 = (f32[256]{0:T(256)S(1)}, f32[256]{0:T(256)}, u32[]{:S(2)}) copy-start(f32[256]{0:T(256)} %param.10) | copy-start | bytes 3076
  40.4 9.5 %collective-permute-start.17 = (bf16[4,128,256]{2,1,0:T(8,128)(2,1)S(1)}, bf16[4,128,256]{2,1,0:T(8,128)(2,1)S(1)}, u32[]{:S(2)}, u32[]{:S(2)}) collective-permute-start(bf16[4,128,256]{2,1,0:T(8,128)(2,1)S(1)} %get-tuple-element.37), channel_id=1, source_target_pairs={{0,1},{1,0},{2,3},{3,2},{4,5},{5,4},{6,7},{7,6},{8,9},{9,8},{10,11... | collective-permute-start | bytes 786440 | tf_op jit(solution)/shard_map/ppermute | solution.py:29
  40.7 9.2 %collective-permute-start.18 = (bf16[4,128,256]{2,1,0:T(8,128)(2,1)S(1)}, bf16[4,128,256]{2,1,0:T(8,128)(2,1)S(1)}, u32[]{:S(2)}, u32[]{:S(2)}) collective-permute-start(bf16[4,128,256]{2,1,0:T(8,128)(2,1)S(1)} %get-tuple-element.38), channel_id=1, source_target_pairs={{0,3},{1,2},{2,1},{3,0},{4,7},{5,6},{6,5},{7,4},{8,11},{9,10},{10,... | collective-permute-start | bytes 786440 | tf_op jit(solution)/shard_map/ppermute | solution.py:29
  41.3 13.2 %collective-permute-start.20 = (bf16[4,128,256]{2,1,0:T(8,128)(2,1)S(1)}, bf16[4,128,256]{2,1,0:T(8,128)(2,1)S(1)}, u32[]{:S(2)}, u32[]{:S(2)}) collective-permute-start(bf16[4,128,256]{2,1,0:T(8,128)(2,1)S(1)} %get-tuple-element.40), channel_id=1, source_target_pairs={{0,4},{1,5},{2,6},{3,7},{4,0},{5,1},{6,2},{7,3},{8,12},{9,13},{10,... | collective-permute-start | bytes 786440 | tf_op jit(solution)/shard_map/ppermute | solution.py:29
  47.4 12.4 %collective-permute-start.15 = (bf16[4,128,256]{2,1,0:T(8,128)(2,1)S(1)}, bf16[4,128,256]{2,1,0:T(8,128)(2,1)S(1)}, u32[]{:S(2)}, u32[]{:S(2)}) collective-permute-start(bf16[4,128,256]{2,1,0:T(8,128)(2,1)S(1)} %get-tuple-element.34), channel_id=1, source_target_pairs={{0,1},{1,0},{2,3},{3,2},{4,5},{5,4},{6,7},{7,6},{8,9},{9,8},{10,11... | collective-permute-start | bytes 786440 | tf_op jit(solution)/shard_map/ppermute | solution.py:29
  49.9 9.9 %collective-permute-start.16 = (bf16[4,128,256]{2,1,0:T(8,128)(2,1)S(1)}, bf16[4,128,256]{2,1,0:T(8,128)(2,1)S(1)}, u32[]{:S(2)}, u32[]{:S(2)}) collective-permute-start(bf16[4,128,256]{2,1,0:T(8,128)(2,1)S(1)} %get-tuple-element.35), channel_id=1, source_target_pairs={{0,3},{1,2},{2,1},{3,0},{4,7},{5,6},{6,5},{7,4},{8,11},{9,10},{10,... | collective-permute-start | bytes 786440 | tf_op jit(solution)/shard_map/ppermute | solution.py:29
  50.0 11.4 %collective-permute-start.19 = (bf16[4,128,256]{2,1,0:T(8,128)(2,1)S(1)}, bf16[4,128,256]{2,1,0:T(8,128)(2,1)S(1)}, u32[]{:S(2)}, u32[]{:S(2)}) collective-permute-start(bf16[4,128,256]{2,1,0:T(8,128)(2,1)S(1)} %add_convert_fusion.9), channel_id=1, source_target_pairs={{0,4},{1,5},{2,6},{3,7},{4,0},{5,1},{6,2},{7,3},{8,12},{9,13},{10,... | collective-permute-start | bytes 786440 | tf_op jit(solution)/shard_map/ppermute | solution.py:29
  54.6 10.0 %collective-permute-start.21 = (bf16[4,128,256]{2,1,0:T(8,128)(2,1)S(1)}, bf16[4,128,256]{2,1,0:T(8,128)(2,1)S(1)}, u32[]{:S(2)}, u32[]{:S(2)}) collective-permute-start(bf16[4,128,256]{2,1,0:T(8,128)(2,1)S(1)} %add_convert_fusion.8), channel_id=1, source_target_pairs={{0,2},{1,3},{2,0},{3,1},{4,6},{5,7},{6,4},{7,5},{8,10},{9,11},{10,... | collective-permute-start | bytes 786440 | tf_op jit(solution)/shard_map/ppermute | solution.py:29
  65.7 8.3 %collective-permute-start.25 = (bf16[256,256]{1,0:T(8,128)(2,1)S(1)}, bf16[256,256]{1,0:T(8,128)(2,1)S(1)}, u32[]{:S(2)}, u32[]{:S(2)}) collective-permute-start(bf16[256,256]{1,0:T(8,128)(2,1)S(1)} %convert_element_type.260), channel_id=1, source_target_pairs={{0,64},{8,72},{16,80},{24,88},{32,96},{40,104},{48,112},{56,120},{... | collective-permute-start | bytes 393224 | tf_op jit(solution)/shard_map/ppermute | solution.py:25
  66.1 7.9 %collective-permute-start.24 = (bf16[256,256]{1,0:T(8,128)(2,1)S(1)}, bf16[256,256]{1,0:T(8,128)(2,1)S(1)}, u32[]{:S(2)}, u32[]{:S(2)}) collective-permute-start(bf16[256,256]{1,0:T(8,128)(2,1)S(1)} %convert_element_type.260), channel_id=1, source_target_pairs={{0,32},{8,40},{16,48},{24,56},{32,0},{40,8},{48,16},{56,24},{64,96... | collective-permute-start | bytes 393224 | tf_op jit(solution)/shard_map/ppermute | solution.py:25
  68.0 6.2 %collective-permute-start.26 = (bf16[256,256]{1,0:T(8,128)(2,1)S(1)}, bf16[256,256]{1,0:T(8,128)(2,1)S(1)}, u32[]{:S(2)}, u32[]{:S(2)}) collective-permute-start(bf16[256,256]{1,0:T(8,128)(2,1)S(1)} %convert_element_type.260), channel_id=1, source_target_pairs={{0,96},{8,104},{16,112},{24,120},{32,64},{40,72},{48,80},{56,88},{... | collective-permute-start | bytes 393224 | tf_op jit(solution)/shard_map/ppermute | solution.py:25
  69.9 6.4 %collective-permute-start.23 = (bf16[4,128,256]{2,1,0:T(8,128)(2,1)S(1)}, bf16[4,128,256]{2,1,0:T(8,128)(2,1)S(1)}, u32[]{:S(2)}, u32[]{:S(2)}) collective-permute-start(bf16[4,128,256]{2,1,0:T(8,128)(2,1)S(1)} %get-tuple-element.44.refs_2_), channel_id=1, source_target_pairs={{0,4},{1,5},{2,6},{3,7},{4,0},{5,1},{6,2},{7,3},{8,12},{9,13},{10,... | collective-permute-start | bytes 786440 | tf_op jit(solution)/shard_map/ppermute | solution.py:29
  71.2 8.0 %collective-permute-start.22 = (bf16[4,128,256]{2,1,0:T(8,128)(2,1)S(1)}, bf16[4,128,256]{2,1,0:T(8,128)(2,1)S(1)}, u32[]{:S(2)}, u32[]{:S(2)}) collective-permute-start(bf16[4,128,256]{2,1,0:T(8,128)(2,1)S(1)} %get-tuple-element.44.refs_2_), channel_id=1, source_target_pairs={{0,2},{1,3},{2,0},{3,1},{4,6},{5,7},{6,4},{7,5},{8,10},{9,11},{10,... | collective-permute-start | bytes 786440 | tf_op jit(solution)/shard_map/ppermute | solution.py:29
  79.1 9.7 %collective-permute-start.33 = (bf16[256,256]{1,0:T(8,128)(2,1)S(1)}, bf16[256,256]{1,0:T(8,128)(2,1)S(1)}, u32[]{:S(2)}, u32[]{:S(2)}) collective-permute-start(bf16[256,256]{1,0:T(8,128)(2,1)S(1)} %add_add_fusion.2), channel_id=1, source_target_pairs={{0,4},{1,5},{2,6},{3,7},{4,0},{5,1},{6,2},{7,3},{8,12},{9,13},{10,... | collective-permute-start | bytes 393224 | tf_op jit(solution)/shard_map/ppermute | solution.py:226
  79.8 9.8 %collective-permute-start.32 = (bf16[256,256]{1,0:T(8,128)(2,1)S(1)}, bf16[256,256]{1,0:T(8,128)(2,1)S(1)}, u32[]{:S(2)}, u32[]{:S(2)}) collective-permute-start(bf16[256,256]{1,0:T(8,128)(2,1)S(1)} %add_add_fusion.2), channel_id=1, source_target_pairs={{0,16},{1,17},{2,18},{3,19},{4,20},{5,21},{6,22},{7,23},{8,24},{9,... | collective-permute-start | bytes 393224 | tf_op jit(solution)/shard_map/ppermute | solution.py:226
  82.2 8.0 %collective-permute-start.34 = (bf16[256,256]{1,0:T(8,128)(2,1)S(1)}, bf16[256,256]{1,0:T(8,128)(2,1)S(1)}, u32[]{:S(2)}, u32[]{:S(2)}) collective-permute-start(bf16[256,256]{1,0:T(8,128)(2,1)S(1)} %add_add_fusion.2), channel_id=1, source_target_pairs={{0,20},{1,21},{2,22},{3,23},{4,16},{5,17},{6,18},{7,19},{8,28},{9,... | collective-permute-start | bytes 393224 | tf_op jit(solution)/shard_map/ppermute | solution.py:226
  84.6 12.0 %collective-permute-start.31 = (bf16[4,128,256]{2,1,0:T(8,128)(2,1)S(1)}, bf16[4,128,256]{2,1,0:T(8,128)(2,1)S(1)}, u32[]{:S(2)}, u32[]{:S(2)}) collective-permute-start(bf16[4,128,256]{2,1,0:T(8,128)(2,1)S(1)} %get-tuple-element.44.refs_2_), channel_id=1, source_target_pairs={{0,3},{1,2},{2,1},{3,0},{4,7},{5,6},{6,5},{7,4},{8,11},{9,10},{10,... | collective-permute-start | bytes 786440 | tf_op jit(solution)/shard_map/ppermute | solution.py:29
  87.3 9.3 %collective-permute-start.30 = (bf16[4,128,256]{2,1,0:T(8,128)(2,1)S(1)}, bf16[4,128,256]{2,1,0:T(8,128)(2,1)S(1)}, u32[]{:S(2)}, u32[]{:S(2)}) collective-permute-start(bf16[4,128,256]{2,1,0:T(8,128)(2,1)S(1)} %get-tuple-element.44.refs_2_), channel_id=1, source_target_pairs={{0,1},{1,0},{2,3},{3,2},{4,5},{5,4},{6,7},{7,6},{8,9},{9,8},{10,11... | collective-permute-start | bytes 786440 | tf_op jit(solution)/shard_map/ppermute | solution.py:29
  88.8 7.8 %collective-permute-start.28 = (bf16[4,128,256]{2,1,0:T(8,128)(2,1)S(1)}, bf16[4,128,256]{2,1,0:T(8,128)(2,1)S(1)}, u32[]{:S(2)}, u32[]{:S(2)}) collective-permute-start(bf16[4,128,256]{2,1,0:T(8,128)(2,1)S(1)} %collective-permute-done.23.refs_6_), channel_id=1, source_target_pairs={{0,3},{1,2},{2,1},{3,0},{4,7},{5,6},{6,5},{7,4},{8,11},{9,10},{10,... | collective-permute-start | bytes 786440 | tf_op jit(solution)/shard_map/ppermute | solution.py:29
  89.6 8.4 %collective-permute-start.27 = (bf16[4,128,256]{2,1,0:T(8,128)(2,1)S(1)}, bf16[4,128,256]{2,1,0:T(8,128)(2,1)S(1)}, u32[]{:S(2)}, u32[]{:S(2)}) collective-permute-start(bf16[4,128,256]{2,1,0:T(8,128)(2,1)S(1)} %collective-permute-done.23.refs_6_), channel_id=1, source_target_pairs={{0,1},{1,0},{2,3},{3,2},{4,5},{5,4},{6,7},{7,6},{8,9},{9,8},{10,11... | collective-permute-start | bytes 786440 | tf_op jit(solution)/shard_map/ppermute | solution.py:29
  90.3 6.4 %collective-permute-start.29 = (bf16[4,128,256]{2,1,0:T(8,128)(2,1)S(1)}, bf16[4,128,256]{2,1,0:T(8,128)(2,1)S(1)}, u32[]{:S(2)}, u32[]{:S(2)}) collective-permute-start(bf16[4,128,256]{2,1,0:T(8,128)(2,1)S(1)} %collective-permute-done.22.refs_4_), channel_id=1, source_target_pairs={{0,4},{1,5},{2,6},{3,7},{4,0},{5,1},{6,2},{7,3},{8,12},{9,13},{10,... | collective-permute-start | bytes 786440 | tf_op jit(solution)/shard_map/ppermute | solution.py:29
  108.7 4.5 %collective-permute-start.35 = (bf16[8,4,128,256]{3,2,1,0:T(8,128)(2,1)S(1)}, bf16[8,4,128,256]{3,2,1,0:T(8,128)(2,1)S(1)}, u32[]{:S(2)}, u32[]{:S(2)}) collective-permute-start(bf16[8,4,128,256]{3,2,1,0:T(8,128)(2,1)S(1)} %get-tuple-element.54), channel_id=1, source_target_pairs={{0,8},{8,0},{16,24},{24,16},{32,40},{40,32},{48,56},{56,48},{64,72... | collective-permute-start | bytes 6291464 | tf_op jit(solution)/shard_map/ppermute | solution.py:25
  109.1 4.0 %collective-permute-start.36 = (bf16[256,256]{1,0:T(8,128)(2,1)S(1)}, bf16[256,256]{1,0:T(8,128)(2,1)S(1)}, u32[]{:S(2)}, u32[]{:S(2)}) collective-permute-start(bf16[256,256]{1,0:T(8,128)(2,1)S(1)} %add_add_fusion.1), channel_id=1, source_target_pairs={{0,8},{8,0},{16,24},{24,16},{32,40},{40,32},{48,56},{56,48},{64,72... | collective-permute-start | bytes 393224 | tf_op jit(solution)/shard_map/ppermute | solution.py:25
  113.2 10.1 %collective-permute-start.41 = (bf16[256,256]{1,0:T(8,128)(2,1)S(1)}, bf16[256,256]{1,0:T(8,128)(2,1)S(1)}, u32[]{:S(2)}, u32[]{:S(2)}) collective-permute-start(bf16[256,256]{1,0:T(8,128)(2,1)S(1)} %convert_add_fusion.3), channel_id=1, source_target_pairs={{0,2},{1,3},{2,0},{3,1},{4,6},{5,7},{6,4},{7,5},{8,10},{9,11},{10,... | collective-permute-start | bytes 393224 | tf_op jit(solution)/shard_map/ppermute | solution.py:29
  113.5 10.5 %collective-permute-start.40 = (bf16[256,256]{1,0:T(8,128)(2,1)S(1)}, bf16[256,256]{1,0:T(8,128)(2,1)S(1)}, u32[]{:S(2)}, u32[]{:S(2)}) collective-permute-start(bf16[256,256]{1,0:T(8,128)(2,1)S(1)} %convert_add_fusion.3), channel_id=1, source_target_pairs={{0,1},{1,0},{2,3},{3,2},{4,5},{5,4},{6,7},{7,6},{8,9},{9,8},{10,11... | collective-permute-start | bytes 393224 | tf_op jit(solution)/shard_map/ppermute | solution.py:29
  117.5 6.6 %collective-permute-start.42 = (bf16[256,256]{1,0:T(8,128)(2,1)S(1)}, bf16[256,256]{1,0:T(8,128)(2,1)S(1)}, u32[]{:S(2)}, u32[]{:S(2)}) collective-permute-start(bf16[256,256]{1,0:T(8,128)(2,1)S(1)} %convert_add_fusion.3), channel_id=1, source_target_pairs={{0,3},{1,2},{2,1},{3,0},{4,7},{5,6},{6,5},{7,4},{8,11},{9,10},{10,... | collective-permute-start | bytes 393224 | tf_op jit(solution)/shard_map/ppermute | solution.py:29
  118.3 9.4 %collective-permute-start.39 = (bf16[4,128,256]{2,1,0:T(8,128)(2,1)S(1)}, bf16[4,128,256]{2,1,0:T(8,128)(2,1)S(1)}, u32[]{:S(2)}, u32[]{:S(2)}) collective-permute-start(bf16[4,128,256]{2,1,0:T(8,128)(2,1)S(1)} %get-tuple-element.65), channel_id=1, source_target_pairs={{0,16},{8,24},{16,0},{24,8},{32,48},{40,56},{48,32},{56,40},{64,80... | collective-permute-start | bytes 786440 | tf_op jit(solution)/shard_map/ppermute | solution.py:25
  119.4 9.7 %collective-permute-start.38 = (bf16[4,128,256]{2,1,0:T(8,128)(2,1)S(1)}, bf16[4,128,256]{2,1,0:T(8,128)(2,1)S(1)}, u32[]{:S(2)}, u32[]{:S(2)}) collective-permute-start(bf16[4,128,256]{2,1,0:T(8,128)(2,1)S(1)} %get-tuple-element.66), channel_id=1, source_target_pairs={{0,96},{8,104},{16,112},{24,120},{32,64},{40,72},{48,80},{56,88},{... | collective-permute-start | bytes 786440 | tf_op jit(solution)/shard_map/ppermute | solution.py:25
  123.3 7.2 %collective-permute-start.37 = (bf16[4,128,256]{2,1,0:T(8,128)(2,1)S(1)}, bf16[4,128,256]{2,1,0:T(8,128)(2,1)S(1)}, u32[]{:S(2)}, u32[]{:S(2)}) collective-permute-start(bf16[4,128,256]{2,1,0:T(8,128)(2,1)S(1)} %get-tuple-element.67), channel_id=1, source_target_pairs={{0,32},{8,40},{16,48},{24,56},{32,0},{40,8},{48,16},{56,24},{64,96... | collective-permute-start | bytes 786440 | tf_op jit(solution)/shard_map/ppermute | solution.py:25
  130.8 8.1 %collective-permute-start.43 = (bf16[4,128,256]{2,1,0:T(8,128)(2,1)S(1)}, bf16[4,128,256]{2,1,0:T(8,128)(2,1)S(1)}, u32[]{:S(2)}, u32[]{:S(2)}) collective-permute-start(bf16[4,128,256]{2,1,0:T(8,128)(2,1)S(1)} %get-tuple-element.58), channel_id=1, source_target_pairs={{0,32},{8,40},{16,48},{24,56},{32,0},{40,8},{48,16},{56,24},{64,96... | collective-permute-start | bytes 786440 | tf_op jit(solution)/shard_map/ppermute | solution.py:25
  131.1 12.1 %collective-permute-start.44 = (bf16[4,128,256]{2,1,0:T(8,128)(2,1)S(1)}, bf16[4,128,256]{2,1,0:T(8,128)(2,1)S(1)}, u32[]{:S(2)}, u32[]{:S(2)}) collective-permute-start(bf16[4,128,256]{2,1,0:T(8,128)(2,1)S(1)} %get-tuple-element.59), channel_id=1, source_target_pairs={{0,96},{8,104},{16,112},{24,120},{32,64},{40,72},{48,80},{56,88},{... | collective-permute-start | bytes 786440 | tf_op jit(solution)/shard_map/ppermute | solution.py:25
  133.8 9.5 %collective-permute-start.45 = (bf16[4,128,256]{2,1,0:T(8,128)(2,1)S(1)}, bf16[4,128,256]{2,1,0:T(8,128)(2,1)S(1)}, u32[]{:S(2)}, u32[]{:S(2)}) collective-permute-start(bf16[4,128,256]{2,1,0:T(8,128)(2,1)S(1)} %get-tuple-element.60), channel_id=1, source_target_pairs={{0,16},{8,24},{16,0},{24,8},{32,48},{40,56},{48,32},{56,40},{64,80... | collective-permute-start | bytes 786440 | tf_op jit(solution)/shard_map/ppermute | solution.py:25
  135.6 9.3 %collective-permute-start.46 = (bf16[4,128,256]{2,1,0:T(8,128)(2,1)S(1)}, bf16[4,128,256]{2,1,0:T(8,128)(2,1)S(1)}, u32[]{:S(2)}, u32[]{:S(2)}) collective-permute-start(bf16[4,128,256]{2,1,0:T(8,128)(2,1)S(1)} %get-tuple-element.61), channel_id=1, source_target_pairs={{0,64},{8,72},{16,80},{24,88},{32,96},{40,104},{48,112},{56,120},{... | collective-permute-start | bytes 786440 | tf_op jit(solution)/shard_map/ppermute | solution.py:25
